TPU v7x, 32 devices: a whole 2x2x4 slice. The times are simulated.
32 devices in a mesh: region: 2 (over y), cell: 8 (over z, x), ray: 2 (over core).
Axes of the slice: x: 2, y: 2, z: 4, core: 2. Of those that a mesh axis runs over, the one named last changes fastest.
Arguments:
- blocks: bfloat16 [16, 2, 96, 128, 128], P(('region', 'cell'), 'ray'), parts along dimension 0, may hold values from -0.109375 to 0.109375
- row_ids: int32 [16, 2, 96], P(('region', 'cell'), 'ray'), parts along dimension 0, may hold values from 0 to 31
- col_ids: int32 [16, 2, 96], P(('region', 'cell'), 'ray'), parts along dimension 0, may hold values from 0 to 15
- counts: int32 [16, 2], P(('region', 'cell'), 'ray'), parts along dimension 0, may hold values from 48 to 96, as said below
- ray_weight: float32 [16384], P(('region', 'ray')), parts along dimension 0, may hold values from 0.25 to 4
- probes: float32 [16, 32, 1024], P(None, ('region', 'cell')), parts along dimension 1, may hold values from -6 to 6
- stiffness: float32 [32, 1024], P(('region', 'cell')), parts along dimension 0, may hold values from 0.05 to 0.5
Outputs:
- applied: float32 [16, 32, 1024], P(None, ('region', 'cell')), parts along dimension 1
- diag_estimate: float32 [32, 1024], P(('region', 'cell')), parts along dimension 0
There are 2 independent parts, one for each index of `region`. A program takes and returns all parts, laid end to end along the dimension named above; each array names one. Nothing has to cross between parts.
Inputs may be any that keep to these rules, and one draw needn't show every extreme that they name: `counts`: some device holds exactly 96 live slots in every draw.
All inputs are finite; a program needn't handle non-finite values.
Results may differ from a plain program's by a relative error of at most 0.0055.
Values may be sent and summed in bfloat16 or wider, within the bound.
No kernel may reach another device: no remote copies, remote signals or barrier semaphores. Data moves between devices by JAX's collectives and lax.ppermute only.
A program may use at most 64 MiB of HBM per device.

v0:
```python
import jax
import jax.numpy as jnp
from jax import lax
from jax.sharding import PartitionSpec as P

NY = 32
NZ = 32


def with_halo(value, sides, width):
    for axis, dim in sides:
        devices, length = (lax.axis_size(axis), value.shape[dim])
        up = [(i, (i + 1) % devices) for i in range(devices - 1)]
        down = [(j, i) for i, j in up]
        last = lax.slice_in_dim(value, length - width, length, axis=dim)
        initial = lax.slice_in_dim(value, 0, width, axis=dim)
        before = lax.ppermute(last, axis, up)
        after = lax.ppermute(initial, axis, down)
        value = jnp.concatenate([before, value, after], axis=dim)
    return value


def smoothing(padded_probe, padded_stiff):
    center = padded_probe[:, 1:-1, 1:-1, 1:-1]
    center_s = padded_stiff[1:-1, 1:-1, 1:-1]
    total = jnp.zeros_like(center)
    moves = [(0, 1), (0, -1), (1, 1), (1, -1), (2, 1), (2, -1)]
    for axis_pick, step in moves:
        starts = [1, 1, 1]
        starts[axis_pick] = 1 + step
        ends = [
            padded_stiff.shape[0] - 2 + starts[0],
            padded_stiff.shape[1] - 2 + starts[1],
            padded_stiff.shape[2] - 2 + starts[2],
        ]
        near_p = padded_probe[:, starts[0] : ends[0], starts[1] : ends[1], starts[2] : ends[2]]
        near_s = padded_stiff[starts[0] : ends[0], starts[1] : ends[1], starts[2] : ends[2]]
        total = total + 0.5 * (center_s + near_s)[None] * (center - near_p)
    return total


def local(blocks, row_ids, col_ids, counts, ray_weight, probes, stiffness):
    slots = blocks.shape[2]
    width = blocks.shape[3]
    tiles = blocks.reshape(slots, width, width)
    rows = row_ids.reshape(slots)
    cols = col_ids.reshape(slots)
    live = (jnp.arange(slots, dtype=jnp.int32) < counts.reshape(())).astype(jnp.float32)
    nprobe, slabs, plane = probes.shape
    ncols = slabs * plane // width
    nrows = ray_weight.shape[0] // width
    flat = probes.astype(jnp.bfloat16).reshape(nprobe, ncols, width)
    picked = jnp.take(flat, cols, axis=1)
    forward = (
        jnp.einsum("pnc,nrc->pnr", picked, tiles, preferred_element_type=jnp.float32)
        * live[None, :, None]
    )
    row_hot = (rows[:, None] == jnp.arange(nrows, dtype=jnp.int32)[None, :]).astype(jnp.float32)
    partial_value = jnp.einsum(
        "pnr,nk->pkr", forward, row_hot, precision=lax.Precision.HIGHEST
    ).reshape(nprobe, nrows * width)
    stacked = jnp.concatenate([probes, stiffness[None]], axis=0)
    padded = with_halo(stacked, (("cell", 1),), 1)
    grid_p = padded[:nprobe].reshape(nprobe, slabs + 2, NY, NZ)
    grid_s = padded[nprobe].reshape(slabs + 2, NY, NZ)
    padded_probe = jnp.pad(grid_p, ((0, 0), (0, 0), (1, 1), (1, 1)))
    padded_stiff = jnp.pad(grid_s, ((0, 0), (1, 1), (1, 1)))
    smooth_term = smoothing(padded_probe, padded_stiff).reshape(nprobe, slabs, plane)
    ray_sum = lax.psum(partial_value, "cell")
    weighted = (ray_sum * ray_weight[None, :]).astype(jnp.bfloat16)
    ray_rows = weighted.reshape(nprobe, nrows, width)
    picked_rows = jnp.take(ray_rows, rows, axis=1)
    backward = (
        jnp.einsum("pnr,nrc->pnc", picked_rows, tiles, preferred_element_type=jnp.float32)
        * live[None, :, None]
    )
    col_hot = (cols[:, None] == jnp.arange(ncols, dtype=jnp.int32)[None, :]).astype(jnp.float32)
    local_term = jnp.einsum(
        "pnc,nk->pkc", backward, col_hot, precision=lax.Precision.HIGHEST
    ).reshape(nprobe, slabs, plane)
    data_term = lax.psum(local_term.astype(jnp.bfloat16), "ray").astype(jnp.float32)
    applied = data_term + smooth_term
    diag_estimate = jnp.mean(probes * applied, axis=0)
    return (applied, diag_estimate)


def solution(mesh):
    return jax.shard_map(
        local,
        mesh=mesh,
        in_specs=(
            P(("region", "cell"), "ray", None, None, None),
            P(("region", "cell"), "ray", None),
            P(("region", "cell"), "ray", None),
            P(("region", "cell"), "ray"),
            P(("region", "ray")),
            P(None, ("region", "cell"), None),
            P(("region", "cell"), None),
        ),
        out_specs=(P(None, ("region", "cell"), None), P(("region", "cell"), None)),
        check_vma=False,
    )
```

profile of v0, /device:TPU:0, one launch (start us, length us, event | category | flops | bytes accessed | tf_op | source)
XLA Modules:
  0.0 129.1 jit_solution(9545435338922115142)
XLA Ops:
  7.2 0.0 copy-start
  7.2 0.0 copy-start.9
  7.2 0.0 all-reduce.5.cloned.1.call-start
  7.2 1.9 %pad_maximum_fusion.1 = (f32[17,1,1024]{2,1,0:T(1,128)S(1)}, f32[17,1,1024]{2,1,0:T(1,128)}) fusion(f32[1,2,1024]{2,1,0:T(2,128)} %bitcast.60, f32[16,2,1024]{2,1,0:T(2,128)} %param.12), kind=kLoop, calls=%fused_computation.58 | loop fusion | flops 34816 | bytes 278528 | tf_op jit(solution)/shard_map/concatenate | solution.py:62
  9.2 1.3 collective-permute-start
  10.5 5.5 %collective-permute-start.1 = (f32[17,1,1024]{2,1,0:T(1,128)S(1)}, f32[17,1,1024]{2,1,0:T(1,128)S(1)}, u32[]{:S(2)}, u32[]{:S(2)}) collective-permute-start(f32[17,1,1024]{2,1,0:T(1,128)S(1)} %get-tuple-element.6), channel_id=1, source_target_pairs={{0,2},{2,4},{4,6},{6,8},{8,10},{10,12},{12,14},{1,3},{3,5},{5,7},{... | collective-permute-start | bytes 208904 | tf_op jit(solution)/shard_map/ppermute | solution.py:17
  15.9 1.0 convert_element_type.31
  17.5 0.7 fusion.59
  18.2 0.7 compare_convert_fusion
  19.0 1.4 %gather_fusion = bf16[96,16,128]{2,1,0:T(8,128)(2,1)} fusion(bf16[16,16,128]{2,0,1:T(8,128)(2,1)S(1)} %copy.9, s32[1024]{0:T(1024)S(1)} %pad_clamp_fusion.1), kind=kCustom, calls=%fused_computation | custom fusion | bytes 786816 | tf_op jit(solution)/shard_map/jit(_take)/gather | solution.py:53
  20.4 0.0 copy-done
  20.4 2.8 %fusion.7 = f32[16,96,128]{2,0,1:T(8,128)S(1)} fusion(bf16[1,1,96,128,128]{4,3,2,1,0:T(8,128)(2,1)S(1)} %copy-done, bf16[96,16,128]{2,1,0:T(8,128)(2,1)} %gather_fusion, f32[96]{0:T(128)S(1)} %get-tuple-element.14, pred[96]{0:T(512)(128)(4,1)S(1)} %get-tuple-element.15), kind=kOutput, calls=%fused_computation.11 | convolution fusion | flops 50724864 | bytes 4325856 | tf_op jit(solution)/shard_map/pnc,nrc->pnr/dot_general | solution.py:55
  23.2 0.0 copy-done.9
  23.2 0.6 fusion.18
  23.8 0.0 copy-done.7
  23.8 0.9 copy.21
  24.7 0.0 all-reduce.5.cloned.1.call-update
  24.7 0.0 all-reduce.7.cloned.1.call-start
  24.7 0.0 copy-done.4
  24.8 0.7 slice.73
  25.4 0.6 compare_and_fusion.1
  26.0 0.6 pad_clamp_fusion
  26.6 0.0 collective-permute-done
  26.6 0.0 collective-permute-done.1
  26.6 0.6 copy-done.2
  27.3 0.6 copy-done.3
  27.9 0.0 copy-done.1
  27.9 0.6 pad_maximum_fusion.5
  28.5 1.1 pad_maximum_fusion
  29.6 1.3 %pad_maximum_fusion.2 = f32[1,4,1024]{2,1,0:T(4,128)} fusion(f32[17,1,1024]{2,1,0:T(1,128)} %copy-done.2, f32[17,1,1024]{2,1,0:T(1,128)} %copy-done.3, f32[1,2,1024]{2,1,0:T(2,128)} %bitcast.62, f32[16,2,1024]{2,1,0:T(2,128)S(1)} %copy-done.1), kind=kLoop, calls=%fused_computation.69 | loop fusion | flops 12288 | bytes 294912 | tf_op jit(solution)/shard_map/slice | solution.py:65
  31.0 1.4 %slice.76 = f32[2,32,32]{2,1,0:T(8,128)} reshape(f32[1,2,1024]{2,1,0:T(2,128)} %get-tuple-element.4) | data formatting | bytes 16384 | tf_op jit(solution)/shard_map/slice | solution.py:37
  32.4 1.4 %slice.82 = f32[2,32,32]{2,1,0:T(8,128)} reshape(f32[1,2,1024]{2,1,0:T(2,128)} %get-tuple-element.5) | data formatting | bytes 16384 | tf_op jit(solution)/shard_map/slice | solution.py:37
  33.7 1.4 %reshape_squeeze.3 = f32[4,32,32]{2,1,0:T(8,128)} reshape(f32[1,4,1024]{2,1,0:T(4,128)} %pad_maximum_fusion.2) | data formatting | bytes 32768 | tf_op jit(solution)/shard_map/reshape;squeeze | solution.py:65
  35.2 0.7 slice.99
  35.9 2.3 %reshape.135 = f32[16,4,32,32]{3,2,1,0:T(8,128)} reshape(f32[16,4,1024]{2,1,0:T(4,128)} %slice.99) | data formatting | bytes 524288 | tf_op jit(solution)/shard_map/reshape | solution.py:64
  38.2 1.6 %fusion.46 = (f32[2,32,32]{2,1,0:T(8,128)S(1)}, f32[2,32,32]{2,1,0:T(8,128)S(1)}, f32[2,32,32]{2,1,0:T(8,128)S(1)}, f32[2,32,32]{2,1,0:T(8,128)S(1)}, f32[2,32,32]{2,1,0:T(8,128)}, /*index=5*/f32[2,32,32]{2,1,0:T(8,128)}) fusion(f32[2,32,32]{2,1,0:T(8,128)} %slice.73, f32[4,32,32]{2,1,0:T(8,128)} %reshape_squeeze.3, f32[2,32,32]{2,1,0:T(8,128)} %slice.76, ...), kind=kLoop, calls=%fused_computation.60 | loop fusion | flops 24576 | bytes 90112 | tf_op jit(solution)/shard_map/mul | solution.py:38
  39.8 57.3 %all-reduce.5.cloned.1.call-done = f32[16,4096]{1,0:T(8,128)} async-done(((f32[16,4096]{1,0:T(8,128)}), f32[16,4096]{1,0:T(8,128)}) %all-reduce.5.cloned.1.call-update) | async-done | bytes 262160 | tf_op jit(solution)/shard_map/psum | solution.py:69
  97.1 1.0 copy_bitcast_fusion.1
  98.1 1.5 %gather_fusion.1 = bf16[96,16,128]{2,1,0:T(8,128)(2,1)} fusion(bf16[16,32,128]{2,0,1:T(8,128)(2,1)S(1)} %copy_bitcast_fusion.1, s32[1024]{0:T(1024)} %pad_clamp_fusion), kind=kCustom, calls=%fused_computation.1 | custom fusion | bytes 786816 | tf_op jit(solution)/shard_map/jit(_take)/gather | solution.py:72
  99.6 2.0 %fusion.13 = f32[16,96,128]{2,0,1:T(8,128)S(1)} fusion(bf16[1,1,96,128,128]{4,3,2,1,0:T(8,128)(2,1)S(1)} %copy-done, bf16[96,16,128]{2,1,0:T(8,128)(2,1)} %gather_fusion.1, f32[96]{0:T(128)} %copy-done.7, pred[96]{0:T(512)(128)(4,1)} %compare_and_fusion.1), kind=kOutput, calls=%fused_computation.13 | convolution fusion | flops 50724864 | bytes 4325856 | tf_op jit(solution)/shard_map/pnr,nrc->pnc/dot_general | solution.py:74
  101.6 0.6 fusion.16
  102.2 0.7 convert_element_type.36
  102.9 0.0 all-reduce.7.cloned.1.call-update
  102.9 3.8 %fusion.25 = f32[16,2,32,32]{3,2,1,0:T(8,128)} fusion(f32[16,4,32,32]{3,2,1,0:T(8,128)} %reshape.135, f32[2,32,32]{2,1,0:T(8,128)S(1)} %get-tuple-element.9, f32[2,32,32]{2,1,0:T(8,128)S(1)} %get-tuple-element.10, f32[2,32,32]{2,1,0:T(8,128)S(1)} %get-tuple-element.11, f32[2,32,32]{2,1,0:T(8,128)S(1)} %get-tuple-element.8, f32[2,32,32]{2,1,0:T(8,128)S(1)} %copy-done.6, ...), kind=kLoop, calls=%fused_computation.24 | loop fusion | flops 557056 | bytes 2801664 | tf_op jit(solution)/shard_map/add | solution.py:38
  106.7 1.3 %reshape.136 = f32[16,2,1024]{2,1,0:T(2,128)S(1)} reshape(f32[16,2,32,32]{3,2,1,0:T(8,128)} %fusion.25) | data formatting | bytes 262144 | tf_op jit(solution)/shard_map/reshape | solution.py:68
  108.0 12.0 %all-reduce.7.cloned.1.call-done = bf16[16,2,1024]{2,1,0:T(2,128)(2,1)} async-done(((bf16[16,2,1024]{2,1,0:T(2,128)(2,1)}), bf16[16,2,1024]{2,1,0:T(2,128)(2,1)}) %all-reduce.7.cloned.1.call-update) | async-done | bytes 65552 | tf_op jit(solution)/shard_map/psum | solution.py:81
  120.1 1.6 %multiply_reduce_fusion = (f32[2,1024]{1,0:T(2,128)S(1)}, f32[16,2,1024]{2,1,0:T(2,128)}) fusion(f32[16,2,1024]{2,1,0:T(2,128)S(1)} %copy-done.1, f32[16,2,1024]{2,1,0:T(2,128)S(1)} %reshape.136, bf16[16,2,1024]{2,1,0:T(2,128)(2,1)} %all-reduce.7.cloned.1.call-done), kind=kLoop, calls=%fused_computation.51 | loop fusion | flops 129024 | bytes 466944 | tf_op jit(solution)/shard_map/reduce_sum | solution.py:83
  121.7 0.6 broadcast_multiply_fusion
  (15 shorter events, 0.1 us)
Async XLA Ops:
  7.2 13.2 %copy-start = (bf16[1,1,96,128,128]{4,3,2,1,0:T(8,128)(2,1)S(1)}, bf16[1,1,96,128,128]{4,3,2,1,0:T(8,128)(2,1)}, u32[]{:S(2)}) copy-start(bf16[1,1,96,128,128]{4,3,2,1,0:T(8,128)(2,1)} %param.7) | copy-start | bytes 9437188
  7.2 16.0 %copy-start.9 = (s32[1,1,96]{2,1,0:T(1,128)S(1)}, s32[1,1,96]{2,1,0:T(1,128)}, u32[]{:S(2)}) copy-start(s32[1,1,96]{2,1,0:T(1,128)} %param.8) | copy-start | bytes 1156
  7.2 89.9 %all-reduce.5.cloned.1.call-start = ((), (), s32[]{:S(2)}) async-start(), calls=%async_computation | async-start | bytes 524288 | tf_op jit(solution)/shard_map/psum | solution.py:69
  9.2 17.5 %collective-permute-start = (f32[17,1,1024]{2,1,0:T(1,128)}, f32[17,1,1024]{2,1,0:T(1,128)S(1)}, u32[]{:S(2)}, u32[]{:S(2)}) collective-permute-start(f32[17,1,1024]{2,1,0:T(1,128)} %get-tuple-element.7), channel_id=1, source_target_pairs={{2,0},{4,2},{6,4},{8,6},{10,8},{12,10},{14,12},{3,1},{5,3},{7,5},{... | collective-permute-start | bytes 208904 | tf_op jit(solution)/shard_map/ppermute | solution.py:18
  10.5 16.2 %collective-permute-start.1 = (f32[17,1,1024]{2,1,0:T(1,128)S(1)}, f32[17,1,1024]{2,1,0:T(1,128)S(1)}, u32[]{:S(2)}, u32[]{:S(2)}) collective-permute-start(f32[17,1,1024]{2,1,0:T(1,128)S(1)} %get-tuple-element.6), channel_id=1, source_target_pairs={{0,2},{2,4},{4,6},{6,8},{8,10},{10,12},{12,14},{1,3},{3,5},{5,7},{... | collective-permute-start | bytes 208904 | tf_op jit(solution)/shard_map/ppermute | solution.py:17
  18.9 4.9 %copy-start.7 = (f32[96]{0:T(128)}, f32[96]{0:T(128)S(1)}, u32[]{:S(2)}) copy-start(f32[96]{0:T(128)S(1)} %get-tuple-element.14) | copy-start | bytes 1156
  20.4 4.4 %copy-start.4 = (f32[2,1024]{1,0:T(2,128)S(1)}, f32[2,1024]{1,0:T(2,128)}, u32[]{:S(2)}) copy-start(f32[2,1024]{1,0:T(2,128)} %param.13) | copy-start | bytes 24580
  20.4 7.5 %copy-start.1 = (f32[16,2,1024]{2,1,0:T(2,128)S(1)}, f32[16,2,1024]{2,1,0:T(2,128)}, u32[]{:S(2)}) copy-start(f32[16,2,1024]{2,1,0:T(2,128)} %param.12) | copy-start | bytes 393220
  24.7 95.4 %all-reduce.7.cloned.1.call-start = ((), (), s32[]{:S(2)}) async-start(), calls=%async_computation.1 | async-start | bytes 131072 | tf_op jit(solution)/shard_map/psum | solution.py:81
  26.6 0.6 copy-start.2
  27.3 0.6 copy-start.3
  38.2 63.4 %copy-start.8 = (s32[1,1,96]{2,1,0:T(1,128)S(1)}, s32[1,1,96]{2,1,0:T(1,128)}, u32[]{:S(2)}) copy-start(s32[1,1,96]{2,1,0:T(1,128)} %param.9) | copy-start | bytes 1156
  99.6 3.3 %copy-start.5 = (f32[2,32,32]{2,1,0:T(8,128)S(1)}, f32[2,32,32]{2,1,0:T(8,128)}, u32[]{:S(2)}) copy-start(f32[2,32,32]{2,1,0:T(8,128)} %get-tuple-element.12) | copy-start | bytes 24580
  99.6 3.3 %copy-start.6 = (f32[2,32,32]{2,1,0:T(8,128)S(1)}, f32[2,32,32]{2,1,0:T(8,128)}, u32[]{:S(2)}) copy-start(f32[2,32,32]{2,1,0:T(8,128)} %get-tuple-element.13) | copy-start | bytes 24580
Sparse Core Ops, SparseCore 0:
  24.8 72.2 all-reduce.4
  103.0 16.9 all-reduce.6
where the time goes:
time: 130 us; the launch traced here: 129 us
  waiting for transfers between devices  69.4 us (53%)
  other arithmetic  17 us (13%)
  local copies, waits for them, and re-layouts  15.1 us (12%)
  between operations  14.8 us (11%)
  starting transfers between devices  6.83 us (5%)
  matrix products  5.99 us (5%)
    psum x1, waiting for transfers between devices, local(): ray_sum = lax.psum(partial_value, 'cell')  57.3 us
    psum x1, waiting for transfers between devices, local(): lax.psum(local_term.astype(jnp.bfloat16), 'ray').astype(jnp.float32)  12 us
    ppermute x1, starting transfers between devices, with_halo(): before = lax.ppermute(last, axis, up)  5.47 us
    add x1, other arithmetic, smoothing(): total = total + 0.5 * (center_s + near_s)[None] * (center - near_p)  3.77 us
    dot_general x1, matrix products, local(): jnp.einsum('pnc,nrc->pnr', picked, tiles, preferred_element_type=jnp.floa...  2.8 us
    slice x2, local copies, waits for them, and re-layouts, smoothing(): padded_stiff[starts[0]:ends[0], starts[1]:ends[1], starts[2]:ends[2]]  2.79 us
  transfers between devices with their start and end apart: 4, of which 2 were waited for; matrix products, arithmetic and copies ran while one was open for 21% of the time, Pallas kernels for 0%

commit v1 on v0

v1 whole, which is shorter than its diff:
```python
import jax
import jax.numpy as jnp
from jax import lax
from jax.experimental import pallas as pl
from jax.experimental.pallas import tpu as pltpu
from jax.sharding import PartitionSpec as P

NY = 32
NZ = 32
CHUNK = 12
F32 = jnp.float32
BF16 = jnp.bfloat16
VMEM = pl.BlockSpec(memory_space=pltpu.VMEM)
SMEM = pl.BlockSpec(memory_space=pltpu.SMEM)
ANY = pl.BlockSpec(memory_space=pl.ANY)


def pieces(slots):
    return [(i, min(CHUNK, slots - i)) for i in range(0, slots, CHUNK)]


def block_copies(blocks, tiles, sems):
    slots = tiles.shape[0]
    return [
        pltpu.make_async_copy(
            blocks.at[0, 0, pl.ds(start, size)],
            tiles.at[pl.ds(start, size)],
            sems.at[i],
        )
        for i, (start, size) in enumerate(pieces(slots))
    ]


def forward_kernel(
    counts, rows, cols, blocks, probes, stiff, total, sent, low, high, flat, tiles, acc, flat16, sems
):
    slots, width = tiles.shape[0], tiles.shape[1]
    nprobe, slabs, plane = probes.shape
    each = plane // width
    nrows = total.shape[0]
    copies = block_copies(blocks, tiles, sems)
    for copy in copies:
        copy.start()
    for s in range(slabs):
        for j in range(each):
            value = probes[:, s, j * width : (j + 1) * width]
            flat[s * each + j] = value
            flat16[s * each + j] = value.astype(BF16)
    for out, s in ((low, 0), (high, slabs - 1)):
        out[0:each] = flat16[s * each : (s + 1) * each]
        out[each] = jnp.zeros((nprobe, width), BF16)
        for j in range(each):
            out[each, j : j + 1, :] = stiff[s : s + 1, j * width : (j + 1) * width].astype(BF16)
    acc[...] = jnp.zeros_like(acc)
    live = counts[0, 0]
    for copy, (start, size) in zip(copies, pieces(slots)):
        copy.wait()
        for n in range(start, start + size):
            row = jnp.where(n < live, rows[0, 0, n], nrows)
            acc[row] += lax.dot_general(
                flat16[cols[0, 0, n]],
                tiles[n],
                (((1,), (1,)), ((), ())),
                preferred_element_type=F32,
            )
    value = acc[0:nrows]
    total[...] = value
    sent[...] = value.astype(BF16)


def backward_kernel(counts, rows, cols, blocks, weighted, part, tiles, acc, sems):
    slots = tiles.shape[0]
    ncols = part.shape[0]
    copies = block_copies(blocks, tiles, sems)
    for copy in copies:
        copy.start()
    acc[...] = jnp.zeros_like(acc)
    live = counts[0, 0]
    for copy, (start, size) in zip(copies, pieces(slots)):
        copy.wait()
        for n in range(start, start + size):
            col = jnp.where(n < live, cols[0, 0, n], ncols)
            acc[col] += jnp.dot(weighted[rows[0, 0, n]], tiles[n], preferred_element_type=F32)
    part[...] = acc[0:ncols].astype(BF16)


def smooth_kernel(flat, stiff, below, above, smooth):
    ncols, nprobe, width = flat.shape
    slabs = stiff.shape[0]
    each = ncols // slabs
    lane = lax.broadcasted_iota(jnp.int32, (1, width), 1)
    at_z = lane % NZ

    def stiff_at(s, j):
        if j < 0 or j >= each:
            return jnp.zeros((1, width), F32)
        if s < 0:
            return below[each, j : j + 1, :].astype(F32)
        if s >= slabs:
            return above[each, j : j + 1, :].astype(F32)
        return stiff[s : s + 1, j * width : (j + 1) * width]

    def probe_at(s, j):
        if j < 0 or j >= each:
            return jnp.zeros((nprobe, width), F32)
        if s < 0:
            return below[j].astype(F32)
        if s >= slabs:
            return above[j].astype(F32)
        return flat[s * each + j]

    def neighbours(at, s, j):
        here, before, after = at(s, j), at(s, j - 1), at(s, j + 1)
        up = lambda v, by: pltpu.roll(v, width - by, 1)
        down = lambda v, by: pltpu.roll(v, by, 1)
        return [
            at(s + 1, j),
            at(s - 1, j),
            jnp.where(lane < width - NZ, up(here, NZ), up(after, NZ)),
            jnp.where(lane >= NZ, down(here, NZ), down(before, NZ)),
            jnp.where(at_z < NZ - 1, up(here, 1), 0.0),
            jnp.where(at_z > 0, down(here, 1), 0.0),
        ]

    for s in range(slabs):
        for j in range(each):
            here_s, here_p = stiff_at(s, j), probe_at(s, j)
            term = jnp.zeros((nprobe, width), F32)
            for near_s, near_p in zip(neighbours(stiff_at, s, j), neighbours(probe_at, s, j)):
                term = term + 0.5 * (here_s + near_s) * (here_p - near_p)
            smooth[s * each + j] = term


def combine_kernel(flat, smooth, mine, other, applied, diag):
    ncols, nprobe, width = flat.shape
    slabs = applied.shape[1]
    each = ncols // slabs
    for s in range(slabs):
        for j in range(each):
            c = s * each + j
            data = mine[c].astype(F32) + other[c].astype(F32)
            value = data + smooth[c]
            applied[:, s, j * width : (j + 1) * width] = value
            diag[s : s + 1, j * width : (j + 1) * width] = jnp.mean(
                flat[c] * value, axis=0, keepdims=True
            )


def power_of_two(n):
    return n & (n - 1) == 0


def local(blocks, row_ids, col_ids, counts, ray_weight, probes, stiffness):
    slots, width = blocks.shape[2], blocks.shape[3]
    nprobe, slabs, plane = probes.shape
    ncols = slabs * plane // width
    nrows = ray_weight.shape[0] // width
    each = plane // width
    ncopies = len(pieces(slots))
    ncell, nray = lax.axis_size("cell"), lax.axis_size("ray")
    shape = jax.ShapeDtypeStruct
    params = pltpu.CompilerParams(vmem_limit_bytes=16 * 1024 * 1024)
    flops = 2 * slots * nprobe * width * width

    total, sent, low, high, flat = pl.pallas_call(
        forward_kernel,
        out_shape=(
            shape((nrows, nprobe, width), F32),
            shape((nrows, nprobe, width), BF16),
            shape((each + 1, nprobe, width), BF16),
            shape((each + 1, nprobe, width), BF16),
            shape((ncols, nprobe, width), F32),
        ),
        in_specs=[SMEM, SMEM, SMEM, ANY, VMEM, VMEM],
        out_specs=(VMEM,) * 5,
        scratch_shapes=[
            pltpu.VMEM((slots, width, width), BF16),
            pltpu.VMEM((nrows + 1, nprobe, width), F32),
            pltpu.VMEM((ncols, nprobe, width), BF16),
            pltpu.SemaphoreType.DMA((ncopies,)),
        ],
        compiler_params=params,
        cost_estimate=pl.CostEstimate(flops=flops, bytes_accessed=2 * slots * width * width, transcendentals=0),
        name="forward",
    )(counts, row_ids, col_ids, blocks, probes, stiffness)

    up = [(i, i + 1) for i in range(ncell - 1)]
    below = lax.ppermute(high, "cell", up)
    above = lax.ppermute(low, "cell", [(j, i) for i, j in up])

    if power_of_two(ncell):
        step = 1
        while step < ncell:
            got = lax.ppermute(sent, "cell", [(i, i ^ step) for i in range(ncell)])
            total = total + got.astype(F32)
            sent = total.astype(BF16)
            step *= 2
    else:
        total = lax.psum(total, "cell")
    weighted = (total * ray_weight.reshape(nrows, 1, width)).astype(BF16)

    part = pl.pallas_call(
        backward_kernel,
        out_shape=shape((ncols, nprobe, width), BF16),
        in_specs=[SMEM, SMEM, SMEM, ANY, VMEM],
        out_specs=VMEM,
        scratch_shapes=[
            pltpu.VMEM((slots, width, width), BF16),
            pltpu.VMEM((ncols + 1, nprobe, width), F32),
            pltpu.SemaphoreType.DMA((ncopies,)),
        ],
        compiler_params=params,
        cost_estimate=pl.CostEstimate(flops=flops, bytes_accessed=2 * slots * width * width, transcendentals=0),
        name="backward",
    )(counts, row_ids, col_ids, blocks, weighted)

    if nray == 2:
        other = lax.ppermute(part, "ray", [(0, 1), (1, 0)])
    else:
        other = lax.psum(part.astype(F32), "ray").astype(F32) - part.astype(F32)

    smooth = pl.pallas_call(
        smooth_kernel,
        out_shape=shape((ncols, nprobe, width), F32),
        in_specs=[VMEM] * 4,
        out_specs=VMEM,
        compiler_params=params,
        name="smooth",
    )(flat, stiffness, below, above)

    return pl.pallas_call(
        combine_kernel,
        out_shape=(shape((nprobe, slabs, plane), F32), shape((slabs, plane), F32)),
        in_specs=[VMEM] * 4,
        out_specs=(VMEM, VMEM),
        compiler_params=params,
        name="combine",
    )(flat, smooth, part, other)


def solution(mesh):
    return jax.shard_map(
        local,
        mesh=mesh,
        in_specs=(
            P(("region", "cell"), "ray", None, None, None),
            P(("region", "cell"), "ray", None),
            P(("region", "cell"), "ray", None),
            P(("region", "cell"), "ray"),
            P(("region", "ray")),
            P(None, ("region", "cell"), None),
            P(("region", "cell"), None),
        ),
        out_specs=(P(None, ("region", "cell"), None), P(("region", "cell"), None)),
        check_vma=False,
    )
```

time: 130 us -> 45.1 us (0.35)
  waiting for transfers between devices: 69.4 us -> 15.7 us
  other arithmetic: 17 us -> 0.17 us
  between operations: 14.8 us -> 1.37 us
  local copies, waits for them, and re-layouts: 15.1 us -> 4.8 us
  Pallas kernels: 0 us -> 10.1 us
  matrix products: 5.99 us -> 0 us
  starting transfers between devices: 6.83 us -> 12.8 us
    psum x2 -> x0, waiting for transfers between devices: 69.3 us -> none  [the longest x1 57.3 us: local(): ray_sum = lax.psum(partial_value, 'cell')]
    ppermute x2 -> x6, waiting for transfers between devices: 0.01 us -> 15.7 us  [the longest x3 11.1 us: local(): got = lax.ppermute(sent, 'cell', [(i, i ^ step) for i in range(ncell)])]
    pallas_call x0 -> x4, Pallas kernels: none -> 10.1 us  [the longest x1 5.04 us: local(): pl.pallas_call(forward_kernel, out_shape=(shape((nrows, nprobe, width), F...]
    ppermute x2 -> x6, starting transfers between devices: 6.75 us -> 12.8 us  [the longest x3 7.75 us: local(): got = lax.ppermute(sent, 'cell', [(i, i ^ step) for i in range(ncell)])]
    dot_general x4 -> x0, matrix products: 5.99 us -> none  [the longest x1 2.8 us: local(): jnp.einsum('pnc,nrc->pnr', picked, tiles, preferred_element_type=jnp.floa...]
    slice x4 -> x0, local copies, waits for them, and re-layouts: 4.21 us -> none  [the longest x2 2.79 us: smoothing(): padded_stiff[starts[0]:ends[0], starts[1]:ends[1], starts[2]:ends[2]]]
    add x1 -> x0, other arithmetic: 3.77 us -> none  [smoothing(): total = total + 0.5 * (center_s + near_s)[None] * (center - near_p)]
    reshape x4 -> x0, local copies, waits for them, and re-layouts: 3.7 us -> none  [the longest x1 2.29 us: local(): grid_p = padded[:nprobe].reshape(nprobe, slabs + 2, NY, NZ)]
  transfers between devices with their start and end apart: 4 -> 6, of which waited for: 2 -> 5; matrix products, arithmetic and copies ran while one was open for 21% -> 0% of each run, Pallas kernels for 0% -> 1%
where the time goes in v1:
time: 45.1 us; the launch traced here: 44.9 us
  waiting for transfers between devices  15.7 us (35%)
  starting transfers between devices  12.8 us (28%)
  Pallas kernels  10.1 us (22%)
  local copies, waits for them, and re-layouts  4.8 us (11%)
  between operations  1.37 us (3%)
    ppermute x3, waiting for transfers between devices, local(): got = lax.ppermute(sent, 'cell', [(i, i ^ step) for i in range(ncell)])  11.1 us
    ppermute x3, starting transfers between devices, local(): got = lax.ppermute(sent, 'cell', [(i, i ^ step) for i in range(ncell)])  7.75 us
    pallas_call x1, Pallas kernels, local(): pl.pallas_call(forward_kernel, out_shape=(shape((nrows, nprobe, width), F...  5.04 us
    unnamed x14, local copies, waits for them, and re-layouts  4.8 us
    ppermute x1, waiting for transfers between devices, local(): above = lax.ppermute(low, 'cell', [(j, i) for i, j in up])  4.24 us
    pallas_call x1, Pallas kernels, local(): pl.pallas_call(backward_kernel, out_shape=shape((ncols, nprobe, width), B...  3.92 us
    ppermute x1, starting transfers between devices, local(): below = lax.ppermute(high, 'cell', up)  3.64 us
    ppermute x1, starting transfers between devices, local(): above = lax.ppermute(low, 'cell', [(j, i) for i, j in up])  1.29 us
  transfers between devices with their start and end apart: 6, of which 5 were waited for; matrix products, arithmetic and copies ran while one was open for 0% of the time, Pallas kernels for 1%

profile of v1, /device:TPU:0, one launch (start us, length us, event | category | flops | bytes accessed | tf_op | source)
XLA Modules:
  0.0 44.9 jit_solution(12237809270494211720)
XLA Ops:
  1.3 0.0 copy-start
  1.3 1.9 %copy-done = bf16[1,1,96,128,128]{4,3,2,1,0:T(8,128)(2,1)S(1)} copy-done((bf16[1,1,96,128,128]{4,3,2,1,0:T(8,128)(2,1)S(1)}, bf16[1,1,96,128,128]{4,3,2,1,0:T(8,128)(2,1)}, u32[]{:S(2)}) %copy-start) | copy-done | bytes 3145752
  3.2 0.0 copy-start.1
  3.2 0.9 %copy-done.1 = f32[16,2,1024]{2,1,0:T(2,128)S(1)} copy-done((f32[16,2,1024]{2,1,0:T(2,128)S(1)}, f32[16,2,1024]{2,1,0:T(2,128)}, u32[]{:S(2)}) %copy-start.1) | copy-done | bytes 131096
  4.1 0.0 copy-start.2
  4.1 0.7 %copy-done.2 = f32[2,1024]{1,0:T(2,128)S(1)} copy-done((f32[2,1024]{1,0:T(2,128)S(1)}, f32[2,1024]{1,0:T(2,128)}, u32[]{:S(2)}) %copy-start.2) | copy-done | bytes 8216
  4.8 0.0 copy-start.4
  4.8 0.7 %copy-done.4 = s32[1,1,96]{2,1,0:T(1,128)S(1)} copy-done((s32[1,1,96]{2,1,0:T(1,128)S(1)}, s32[1,1,96]{2,1,0:T(1,128)}, u32[]{:S(2)}) %copy-start.4) | copy-done | bytes 408
  5.4 0.0 copy-start.5
  5.4 0.7 %copy-done.5 = s32[1,1,96]{2,1,0:T(1,128)S(1)} copy-done((s32[1,1,96]{2,1,0:T(1,128)S(1)}, s32[1,1,96]{2,1,0:T(1,128)}, u32[]{:S(2)}) %copy-start.5) | copy-done | bytes 408
  6.1 0.0 copy-start.6
  6.1 5.0 %forward.1 = (f32[32,16,128]{2,1,0:T(8,128)S(1)}, bf16[32,16,128]{2,1,0:T(8,128)(2,1)S(1)}, bf16[9,16,128]{2,1,0:T(8,128)(2,1)S(1)}, bf16[9,16,128]{2,1,0:T(8,128)(2,1)S(1)}, f32[16,16,128]{2,1,0:T(8,128)S(1)}) custom-call(s32[1,1]{1,0:T(1,128)S(6)} %copy.9.counts, s32[1,1,96]{2,1,0:T(1,128)S(1)} %copy-done.4, s32[1,1,96]{2,1,0:T(1,128)S(1)} %copy-done.5, ...), custom_call_target="tpu_custom_call" | custom-call | flops 50331648 | bytes 3145728 | tf_op jit(solution)/shard_map/forward/pallas_call | solution.py:165
  11.1 0.0 copy-start.3
  11.1 3.0 %collective-permute-start.2 = (bf16[32,16,128]{2,1,0:T(8,128)(2,1)S(1)}, bf16[32,16,128]{2,1,0:T(8,128)(2,1)S(1)}, u32[]{:S(2)}, u32[]{:S(2)}) collective-permute-start(bf16[32,16,128]{2,1,0:T(8,128)(2,1)S(1)} %get-tuple-element.11), channel_id=1, source_target_pairs={{0,2},{2,0},{4,6},{6,4},{8,10},{10,8},{12,14},{14,12},{1,3},{3,1},... | collective-permute-start | bytes 393224 | tf_op jit(solution)/shard_map/ppermute | solution.py:194
  14.1 3.5 %collective-permute-done.2 = bf16[32,16,128]{2,1,0:T(8,128)(2,1)S(1)} collective-permute-done((bf16[32,16,128]{2,1,0:T(8,128)(2,1)S(1)}, bf16[32,16,128]{2,1,0:T(8,128)(2,1)S(1)}, u32[]{:S(2)}, u32[]{:S(2)}) %collective-permute-start.2) | collective-permute-done | bytes 131104 | tf_op jit(solution)/shard_map/ppermute | solution.py:194
  17.7 1.9 %collective-permute-start.3 = (bf16[32,16,128]{2,1,0:T(8,128)(2,1)S(1)}, bf16[32,16,128]{2,1,0:T(8,128)(2,1)S(1)}, u32[]{:S(2)}, u32[]{:S(2)}) collective-permute-start(bf16[32,16,128]{2,1,0:T(8,128)(2,1)S(1)} %fusion), channel_id=1, source_target_pairs={{0,4},{2,6},{4,0},{6,2},{8,12},{10,14},{12,8},{14,10},{1,5},{3,7},... | collective-permute-start | bytes 393224 | tf_op jit(solution)/shard_map/ppermute | solution.py:194
  19.6 3.1 %collective-permute-done.3 = bf16[32,16,128]{2,1,0:T(8,128)(2,1)S(1)} collective-permute-done((bf16[32,16,128]{2,1,0:T(8,128)(2,1)S(1)}, bf16[32,16,128]{2,1,0:T(8,128)(2,1)S(1)}, u32[]{:S(2)}, u32[]{:S(2)}) %collective-permute-start.3) | collective-permute-done | bytes 131104 | tf_op jit(solution)/shard_map/ppermute | solution.py:194
  22.7 0.1 fusion.1
  22.8 2.9 %collective-permute-start.4 = (bf16[32,16,128]{2,1,0:T(8,128)(2,1)S(1)}, bf16[32,16,128]{2,1,0:T(8,128)(2,1)S(1)}, u32[]{:S(2)}, u32[]{:S(2)}) collective-permute-start(bf16[32,16,128]{2,1,0:T(8,128)(2,1)S(1)} %fusion.1), channel_id=1, source_target_pairs={{0,8},{2,10},{4,12},{6,14},{8,0},{10,2},{12,4},{14,6},{1,9},{3,11}... | collective-permute-start | bytes 393224 | tf_op jit(solution)/shard_map/ppermute | solution.py:194
  25.7 4.5 %collective-permute-done.4 = bf16[32,16,128]{2,1,0:T(8,128)(2,1)S(1)} collective-permute-done((bf16[32,16,128]{2,1,0:T(8,128)(2,1)S(1)}, bf16[32,16,128]{2,1,0:T(8,128)(2,1)S(1)}, u32[]{:S(2)}, u32[]{:S(2)}) %collective-permute-start.4) | collective-permute-done | bytes 131104 | tf_op jit(solution)/shard_map/ppermute | solution.py:194
  30.1 0.0 copy-done.6
  30.1 0.1 multiply_convert_fusion.weighted
  30.2 3.9 %backward.1.mine = bf16[16,16,128]{2,1,0:T(8,128)(2,1)S(1)} custom-call(s32[1,1]{1,0:T(1,128)S(6)} %copy.9.counts, s32[1,1,96]{2,1,0:T(1,128)S(1)} %copy-done.4, s32[1,1,96]{2,1,0:T(1,128)S(1)} %copy-done.5, bf16[1,1,96,128,128]{4,3,2,1,0:T(8,128)(2,1)S(1)} %copy-done, bf16[32,16,128]{2,1,0:T(8,128)(2,1)S(1)} %multiply_convert_fusion.weighted), custom_call_target="tpu_custom_call" | custom-call | flops 50331648 | bytes 3145728 | tf_op jit(solution)/shard_map/backward/pallas_call | solution.py:202
  34.1 0.1 collective-permute-start.5
  34.2 3.6 %collective-permute-start = (bf16[9,16,128]{2,1,0:T(8,128)(2,1)S(1)}, bf16[9,16,128]{2,1,0:T(8,128)(2,1)S(1)}, u32[]{:S(2)}, u32[]{:S(2)}) collective-permute-start(bf16[9,16,128]{2,1,0:T(8,128)(2,1)S(1)} %get-tuple-element.8), channel_id=1, source_target_pairs={{0,2},{2,4},{4,6},{6,8},{8,10},{10,12},{12,14},{1,3},{3,5},{5,7},{... | collective-permute-start | bytes 110600 | tf_op jit(solution)/shard_map/ppermute | solution.py:188
  37.9 1.3 %collective-permute-start.1 = (bf16[9,16,128]{2,1,0:T(8,128)(2,1)S(1)}, bf16[9,16,128]{2,1,0:T(8,128)(2,1)S(1)}, u32[]{:S(2)}, u32[]{:S(2)}) collective-permute-start(bf16[9,16,128]{2,1,0:T(8,128)(2,1)S(1)} %get-tuple-element.9), channel_id=1, source_target_pairs={{2,0},{4,2},{6,4},{8,6},{10,8},{12,10},{14,12},{3,1},{5,3},{7,5},{... | collective-permute-start | bytes 110600 | tf_op jit(solution)/shard_map/ppermute | solution.py:189
  39.2 0.3 collective-permute-done.below
  39.5 4.2 %collective-permute-done.1.above = bf16[9,16,128]{2,1,0:T(8,128)(2,1)S(1)} collective-permute-done((bf16[9,16,128]{2,1,0:T(8,128)(2,1)S(1)}, bf16[9,16,128]{2,1,0:T(8,128)(2,1)S(1)}, u32[]{:S(2)}, u32[]{:S(2)}) %collective-permute-start.1) | collective-permute-done | bytes 36896 | tf_op jit(solution)/shard_map/ppermute | solution.py:189
  43.7 0.0 copy-done.3
  43.7 0.4 smooth.1
  44.1 0.0 collective-permute-done.5.other
  44.1 0.8 %combine.1 = (f32[16,2,1024]{2,1,0:T(2,128)}, f32[2,1024]{1,0:T(2,128)}) custom-call(f32[16,16,128]{2,1,0:T(8,128)S(1)} %get-tuple-element.7.flat, f32[16,16,128]{2,1,0:T(8,128)S(1)} %smooth.1, bf16[16,16,128]{2,1,0:T(8,128)(2,1)S(1)} %backward.1.mine, bf16[16,16,128]{2,1,0:T(8,128)(2,1)S(1)} %collective-permute-done.5.other), custom_call_target="tpu_custom_call" | custom-call | tf_op jit(solution)/shard_map/combine/pallas_call | solution.py:231
  (1 shorter events, 0.0 us)
Async XLA Ops:
  1.3 1.9 %copy-start = (bf16[1,1,96,128,128]{4,3,2,1,0:T(8,128)(2,1)S(1)}, bf16[1,1,96,128,128]{4,3,2,1,0:T(8,128)(2,1)}, u32[]{:S(2)}) copy-start(bf16[1,1,96,128,128]{4,3,2,1,0:T(8,128)(2,1)} %blocks.3) | copy-start | bytes 9437188
  3.2 0.9 %copy-start.1 = (f32[16,2,1024]{2,1,0:T(2,128)S(1)}, f32[16,2,1024]{2,1,0:T(2,128)}, u32[]{:S(2)}) copy-start(f32[16,2,1024]{2,1,0:T(2,128)} %probes.1) | copy-start | bytes 393220
  4.1 0.7 %copy-start.2 = (f32[2,1024]{1,0:T(2,128)S(1)}, f32[2,1024]{1,0:T(2,128)}, u32[]{:S(2)}) copy-start(f32[2,1024]{1,0:T(2,128)} %stiff.3) | copy-start | bytes 24580
  4.8 0.7 %copy-start.4 = (s32[1,1,96]{2,1,0:T(1,128)S(1)}, s32[1,1,96]{2,1,0:T(1,128)}, u32[]{:S(2)}) copy-start(s32[1,1,96]{2,1,0:T(1,128)} %rows.3) | copy-start | bytes 1156
  5.4 0.7 %copy-start.5 = (s32[1,1,96]{2,1,0:T(1,128)S(1)}, s32[1,1,96]{2,1,0:T(1,128)}, u32[]{:S(2)}) copy-start(s32[1,1,96]{2,1,0:T(1,128)} %cols.3) | copy-start | bytes 1156
  6.1 24.0 %copy-start.6 = (f32[4096]{0:T(1024)S(1)}, f32[4096]{0:T(1024)}, u32[]{:S(2)}) copy-start(f32[4096]{0:T(1024)} %param.11) | copy-start | bytes 49156
  11.1 32.6 %copy-start.3 = (f32[2,1024]{1,0:T(2,128)S(1)}, f32[2,1024]{1,0:T(2,128)}, u32[]{:S(2)}) copy-start(f32[2,1024]{1,0:T(2,128)} %stiff.3) | copy-start | bytes 24580
  11.1 6.5 %collective-permute-start.2 = (bf16[32,16,128]{2,1,0:T(8,128)(2,1)S(1)}, bf16[32,16,128]{2,1,0:T(8,128)(2,1)S(1)}, u32[]{:S(2)}, u32[]{:S(2)}) collective-permute-start(bf16[32,16,128]{2,1,0:T(8,128)(2,1)S(1)} %get-tuple-element.11), channel_id=1, source_target_pairs={{0,2},{2,0},{4,6},{6,4},{8,10},{10,8},{12,14},{14,12},{1,3},{3,1},... | collective-permute-start | bytes 393224 | tf_op jit(solution)/shard_map/ppermute | solution.py:194
  17.7 5.0 %collective-permute-start.3 = (bf16[32,16,128]{2,1,0:T(8,128)(2,1)S(1)}, bf16[32,16,128]{2,1,0:T(8,128)(2,1)S(1)}, u32[]{:S(2)}, u32[]{:S(2)}) collective-permute-start(bf16[32,16,128]{2,1,0:T(8,128)(2,1)S(1)} %fusion), channel_id=1, source_target_pairs={{0,4},{2,6},{4,0},{6,2},{8,12},{10,14},{12,8},{14,10},{1,5},{3,7},... | collective-permute-start | bytes 393224 | tf_op jit(solution)/shard_map/ppermute | solution.py:194
  22.8 7.3 %collective-permute-start.4 = (bf16[32,16,128]{2,1,0:T(8,128)(2,1)S(1)}, bf16[32,16,128]{2,1,0:T(8,128)(2,1)S(1)}, u32[]{:S(2)}, u32[]{:S(2)}) collective-permute-start(bf16[32,16,128]{2,1,0:T(8,128)(2,1)S(1)} %fusion.1), channel_id=1, source_target_pairs={{0,8},{2,10},{4,12},{6,14},{8,0},{10,2},{12,4},{14,6},{1,9},{3,11}... | collective-permute-start | bytes 393224 | tf_op jit(solution)/shard_map/ppermute | solution.py:194
  34.1 10.0 %collective-permute-start.5 = (bf16[16,16,128]{2,1,0:T(8,128)(2,1)S(1)}, bf16[16,16,128]{2,1,0:T(8,128)(2,1)S(1)}, u32[]{:S(2)}, u32[]{:S(2)}) collective-permute-start(bf16[16,16,128]{2,1,0:T(8,128)(2,1)S(1)} %backward.1.mine), channel_id=1, source_target_pairs={{0,1},{1,0},{2,3},{3,2},{4,5},{5,4},{6,7},{7,6},{8,9},{9,8},{10,11... | collective-permute-start | bytes 196616 | tf_op jit(solution)/shard_map/ppermute | solution.py:218
  34.2 5.3 %collective-permute-start = (bf16[9,16,128]{2,1,0:T(8,128)(2,1)S(1)}, bf16[9,16,128]{2,1,0:T(8,128)(2,1)S(1)}, u32[]{:S(2)}, u32[]{:S(2)}) collective-permute-start(bf16[9,16,128]{2,1,0:T(8,128)(2,1)S(1)} %get-tuple-element.8), channel_id=1, source_target_pairs={{0,2},{2,4},{4,6},{6,8},{8,10},{10,12},{12,14},{1,3},{3,5},{5,7},{... | collective-permute-start | bytes 110600 | tf_op jit(solution)/shard_map/ppermute | solution.py:188
  37.9 5.9 %collective-permute-start.1 = (bf16[9,16,128]{2,1,0:T(8,128)(2,1)S(1)}, bf16[9,16,128]{2,1,0:T(8,128)(2,1)S(1)}, u32[]{:S(2)}, u32[]{:S(2)}) collective-permute-start(bf16[9,16,128]{2,1,0:T(8,128)(2,1)S(1)} %get-tuple-element.9), channel_id=1, source_target_pairs={{2,0},{4,2},{6,4},{8,6},{10,8},{12,10},{14,12},{3,1},{5,3},{7,5},{... | collective-permute-start | bytes 110600 | tf_op jit(solution)/shard_map/ppermute | solution.py:189

commit v2 on v1

v2 whole, which is shorter than its diff:
```python
import jax
import jax.numpy as jnp
from jax import lax
from jax.experimental import pallas as pl
from jax.experimental.pallas import tpu as pltpu
from jax.sharding import PartitionSpec as P

NZ = 32
CHUNKS = 2
F32 = jnp.float32
BF16 = jnp.bfloat16
I32 = jnp.int32
VMEM = pl.BlockSpec(memory_space=pltpu.VMEM)
SMEM = pl.BlockSpec(memory_space=pltpu.SMEM)
HBM = pl.BlockSpec(memory_space=pltpu.HBM)


def groups(start, size):
    return [tuple(range(n, min(n + 2, start + size))) for n in range(start, start + size, 2)]


def forward_kernel(
    counts, rows_in, cols_in, blocks, probes_in, stiff_in,
    tiles, total, sent, odd, flat, stiff, rows, cols,
    probes, acc, flat16, sems, small,
):
    slots, width = tiles.shape[0], tiles.shape[1]
    nprobe, slabs, plane = probes.shape
    each = plane // width
    nrows = total.shape[0]
    run = -(-slots // CHUNKS)
    runs = [(i, min(run, slots - i)) for i in range(0, slots, run)]
    pairs = [(probes_in, probes), (cols_in, cols), (rows_in, rows), (stiff_in, stiff)]
    first = [pltpu.make_async_copy(a, b, small.at[i]) for i, (a, b) in enumerate(pairs)]
    copies = [
        pltpu.make_async_copy(blocks.at[0, 0, pl.ds(s, z)], tiles.at[pl.ds(s, z)], sems.at[i])
        for i, (s, z) in enumerate(runs)
    ]
    for copy in first + copies:
        copy.start()
    acc[...] = jnp.zeros_like(acc)
    for copy in first:
        copy.wait()
    for s in range(slabs):
        for j in range(each):
            value = probes[:, s, j * width : (j + 1) * width]
            flat[s * each + j] = value
            flat16[s * each + j] = value.astype(BF16)
    even = lax.rem(lax.axis_index("cell"), 2) == 0
    top = (slabs - 1) * each
    for j in range(each):
        low, high = flat16[j], flat16[top + j]
        sent[nrows + j] = jnp.where(even, high, low)
        odd[j] = jnp.where(even, low, high)
    sent[nrows + each] = jnp.zeros((nprobe, width), BF16)
    odd[each] = jnp.zeros((nprobe, width), BF16)
    for j in range(each):
        low = stiff[0:1, j * width : (j + 1) * width].astype(BF16)
        high = stiff[slabs - 1 : slabs, j * width : (j + 1) * width].astype(BF16)
        sent[nrows + each, j : j + 1, :] = jnp.where(even, high, low)
        odd[each, j : j + 1, :] = jnp.where(even, low, high)
    live = counts[0, 0]
    for copy, (start, size) in zip(copies, runs):
        copy.wait()
        outs = []
        for group in groups(start, size):
            left = jnp.concatenate([flat16[cols[0, 0, n]] for n in group], axis=0)
            right = jnp.concatenate([tiles[n] for n in group], axis=0)
            out = lax.dot_general(left, right, (((1,), (1,)), ((), ())), preferred_element_type=F32)
            outs += [
                (n, out[i * nprobe : (i + 1) * nprobe, i * width : (i + 1) * width])
                for i, n in enumerate(group)
            ]
        for n, out in outs:
            acc[jnp.where(n < live, rows[0, 0, n], nrows)] += out
    value = acc[0:nrows]
    total[...] = value
    sent[0:nrows] = value.astype(BF16)


def backward_kernel(counts, rows, cols, tiles, total, got, weight, part, weighted, acc):
    slots, width = tiles.shape[0], tiles.shape[1]
    nrows, nprobe = total.shape[0], total.shape[1]
    ncols = part.shape[0]
    for k in range(nrows):
        value = total[k] + got[k].astype(F32)
        weighted[k] = (value * weight[k : k + 1, :]).astype(BF16)
    acc[...] = jnp.zeros_like(acc)
    live = counts[0, 0]
    outs = []
    for group in groups(0, slots):
        left = jnp.concatenate([weighted[rows[0, 0, n]] for n in group], axis=0)
        right = jnp.concatenate([tiles[n] for n in group], axis=1)
        out = jnp.dot(left, right, preferred_element_type=F32)
        outs += [
            (n, out[i * nprobe : (i + 1) * nprobe, i * width : (i + 1) * width])
            for i, n in enumerate(group)
        ]
    for n, out in outs:
        acc[jnp.where(n < live, cols[0, 0, n], ncols)] += out
    part[...] = acc[0:ncols].astype(BF16)


def smooth_kernel(flat, stiff, got, odd, smooth, below, above):
    ncols, nprobe, width = flat.shape
    slabs = stiff.shape[0]
    each = ncols // slabs
    nrows = got.shape[0] - each - 1
    lane = lax.broadcasted_iota(I32, (1, width), 1)
    at_z = lane % NZ
    even = lax.rem(lax.axis_index("cell"), 2) == 0
    for j in range(each + 1):
        pair, other = got[nrows + j], odd[j]
        below[j] = jnp.where(even, other, pair).astype(F32)
        above[j] = jnp.where(even, pair, other).astype(F32)

    def stiff_at(s, j):
        if j < 0 or j >= each:
            return jnp.zeros((1, width), F32)
        if s < 0:
            return below[each, j : j + 1, :]
        if s >= slabs:
            return above[each, j : j + 1, :]
        return stiff[s : s + 1, j * width : (j + 1) * width]

    def probe_at(s, j):
        if j < 0 or j >= each:
            return jnp.zeros((nprobe, width), F32)
        if s < 0:
            return below[j]
        if s >= slabs:
            return above[j]
        return flat[s * each + j]

    def up(value, by):
        return pltpu.roll(value, width - by, 1)

    def down(value, by):
        return pltpu.roll(value, by, 1)

    def neighbours(at, s, j):
        here, before, after = at(s, j), at(s, j - 1), at(s, j + 1)
        return [
            at(s + 1, j),
            at(s - 1, j),
            jnp.where(lane < width - NZ, up(here, NZ), up(after, NZ)),
            jnp.where(lane >= NZ, down(here, NZ), down(before, NZ)),
            jnp.where(at_z < NZ - 1, up(here, 1), 0.0),
            jnp.where(at_z > 0, down(here, 1), 0.0),
        ]

    for s in range(slabs):
        for j in range(each):
            here_s, here_p = stiff_at(s, j), probe_at(s, j)
            term = jnp.zeros((nprobe, width), F32)
            for near_s, near_p in zip(neighbours(stiff_at, s, j), neighbours(probe_at, s, j)):
                term = term + 0.5 * (here_s + near_s) * (here_p - near_p)
            smooth[s * each + j] = term


def combine_kernel(flat, smooth, mine, other, applied, diag):
    ncols, nprobe, width = flat.shape
    slabs = applied.shape[1]
    each = ncols // slabs
    for s in range(slabs):
        for j in range(each):
            c = s * each + j
            value = mine[c].astype(F32) + other[c].astype(F32) + smooth[c]
            applied[:, s, j * width : (j + 1) * width] = value
            diag[s : s + 1, j * width : (j + 1) * width] = jnp.mean(
                flat[c] * value, axis=0, keepdims=True
            )


def local(blocks, row_ids, col_ids, counts, ray_weight, probes, stiffness):
    slots, width = blocks.shape[2], blocks.shape[3]
    nprobe, slabs, plane = probes.shape
    ncols = slabs * plane // width
    nrows = ray_weight.shape[0] // width
    each = plane // width
    ncell, nray = lax.axis_size("cell"), lax.axis_size("ray")
    assert ncell > 1 and ncell & (ncell - 1) == 0 and nray == 2
    params = pltpu.CompilerParams(vmem_limit_bytes=8 * 1024 * 1024)
    cost = pl.CostEstimate(
        flops=2 * slots * nprobe * width * width,
        bytes_accessed=2 * slots * width * width,
        transcendentals=0,
    )
    pinned = [
        pltpu.with_memory_space_constraint(x, pltpu.HBM)
        for x in (row_ids, col_ids, blocks, probes, stiffness)
    ]
    tiles, total, sent, odd, flat, stiff, rows, cols = pl.pallas_call(
        forward_kernel,
        out_shape=(
            pltpu.VMEM((slots, width, width), BF16),
            pltpu.VMEM((nrows, nprobe, width), F32),
            pltpu.VMEM((nrows + each + 1, nprobe, width), BF16),
            pltpu.VMEM((each + 1, nprobe, width), BF16),
            pltpu.VMEM((ncols, nprobe, width), F32),
            pltpu.VMEM((slabs, plane), F32),
            pltpu.SMEM(row_ids.shape, I32),
            pltpu.SMEM(col_ids.shape, I32),
        ),
        in_specs=[SMEM] + [HBM] * 5,
        out_specs=(VMEM,) * 6 + (SMEM,) * 2,
        scratch_shapes=[
            pltpu.VMEM((nprobe, slabs, plane), F32),
            pltpu.VMEM((nrows + 1, nprobe, width), F32),
            pltpu.VMEM((ncols, nprobe, width), BF16),
            pltpu.SemaphoreType.DMA((CHUNKS,)),
            pltpu.SemaphoreType.DMA((4,)),
        ],
        compiler_params=params,
        cost_estimate=cost,
        name="forward",
    )(counts, *pinned)

    above_odd = [(i, i + 1) for i in range(1, ncell - 1, 2)]
    across = lax.ppermute(odd, "cell", above_odd + [(j, i) for i, j in above_odd])

    step = 1
    while True:
        got = lax.ppermute(sent, "cell", [(i, i ^ step) for i in range(ncell)])
        if step == 1:
            halo = got
        step *= 2
        if step == ncell:
            break
        total = total + got[:nrows].astype(F32)
        sent = total.astype(BF16)
        if step == 4:
            total, sent, across = lax.optimization_barrier((total, sent, across))

    part = pl.pallas_call(
        backward_kernel,
        out_shape=pltpu.VMEM((ncols, nprobe, width), BF16),
        in_specs=[SMEM] * 3 + [VMEM] * 4,
        out_specs=VMEM,
        scratch_shapes=[
            pltpu.VMEM((nrows, nprobe, width), BF16),
            pltpu.VMEM((ncols + 1, nprobe, width), F32),
        ],
        compiler_params=params,
        cost_estimate=cost,
        name="backward",
    )(counts, rows, cols, tiles, total, got, ray_weight.reshape(nrows, width))

    other = lax.ppermute(part, "ray", [(0, 1), (1, 0)])

    smooth = pl.pallas_call(
        smooth_kernel,
        out_shape=pltpu.VMEM((ncols, nprobe, width), F32),
        in_specs=[VMEM] * 4,
        out_specs=VMEM,
        scratch_shapes=[pltpu.VMEM((each + 1, nprobe, width), F32)] * 2,
        compiler_params=params,
        name="smooth",
    )(flat, stiff, halo, across)

    return pl.pallas_call(
        combine_kernel,
        out_shape=(
            jax.ShapeDtypeStruct((nprobe, slabs, plane), F32),
            jax.ShapeDtypeStruct((slabs, plane), F32),
        ),
        in_specs=[VMEM] * 4,
        out_specs=(VMEM, VMEM),
        compiler_params=params,
        name="combine",
    )(flat, smooth, part, other)


def solution(mesh):
    return jax.shard_map(
        local,
        mesh=mesh,
        in_specs=(
            P(("region", "cell"), "ray", None, None, None),
            P(("region", "cell"), "ray", None),
            P(("region", "cell"), "ray", None),
            P(("region", "cell"), "ray"),
            P(("region", "ray")),
            P(None, ("region", "cell"), None),
            P(("region", "cell"), None),
        ),
        out_specs=(P(None, ("region", "cell"), None), P(("region", "cell"), None)),
        check_vma=False,
    )
```

time: 45.1 us -> 30.1 us (0.67)
  Pallas kernels: 10.1 us -> 4.7 us
  local copies, waits for them, and re-layouts: 4.8 us -> 0.01 us
  waiting for transfers between devices: 15.7 us -> 11.7 us
  starting transfers between devices: 12.8 us -> 12 us
    pallas_call x4, Pallas kernels: 10.1 us -> 4.7 us  [the longest x1 2.89 us: local(): pl.pallas_call(forward_kernel, out_shape=(pltpu.VMEM((slots, width, width...]
    unnamed x14 -> x2, local copies, waits for them, and re-layouts: 4.8 us -> 0.01 us
    ppermute x2 -> x1, waiting for transfers between devices: 4.55 us -> 0.01 us  [local(): lax.ppermute(odd, 'cell', above_odd + [(j, i) for i, j in above_odd])]
    ppermute x2 -> x1, starting transfers between devices: 4.93 us -> 0.65 us  [local(): lax.ppermute(odd, 'cell', above_odd + [(j, i) for i, j in above_odd])]
    ppermute x3, starting transfers between devices: 7.75 us -> 11.3 us  [local(): got = lax.ppermute(sent, 'cell', [(i, i ^ step) for i in range(ncell)])]
    ppermute x1, waiting for transfers between devices: 0.01 us -> 0.87 us  [local(): other = lax.ppermute(part, 'ray', [(0, 1), (1, 0)])]
  transfers between devices with their start and end apart: 6 -> 5, of which waited for: 5 -> 4; matrix products, arithmetic and copies ran while one was open for 0% -> 0% of each run, Pallas kernels for 1% -> 1%
where the time goes in v2:
time: 30.1 us; the launch traced here: 29.9 us
  starting transfers between devices  12 us (40%)
  waiting for transfers between devices  11.7 us (39%)
  Pallas kernels  4.7 us (16%)
  between operations  1.36 us (5%)
    ppermute x3, starting transfers between devices, local(): got = lax.ppermute(sent, 'cell', [(i, i ^ step) for i in range(ncell)])  11.3 us
    ppermute x3, waiting for transfers between devices, local(): got = lax.ppermute(sent, 'cell', [(i, i ^ step) for i in range(ncell)])  10.8 us
    pallas_call x1, Pallas kernels, local(): pl.pallas_call(forward_kernel, out_shape=(pltpu.VMEM((slots, width, width...  2.89 us
    ppermute x1, waiting for transfers between devices, local(): other = lax.ppermute(part, 'ray', [(0, 1), (1, 0)])  0.87 us
    pallas_call x1, Pallas kernels, local(): pl.pallas_call(combine_kernel, out_shape=(jax.ShapeDtypeStruct((nprobe, s...  0.76 us
    pallas_call x1, Pallas kernels, local(): pl.pallas_call(backward_kernel, out_shape=pltpu.VMEM((ncols, nprobe, widt...  0.69 us
    ppermute x1, starting transfers between devices, local(): lax.ppermute(odd, 'cell', above_odd + [(j, i) for i, j in above_odd])  0.65 us
  transfers between devices with their start and end apart: 5, of which 4 were waited for; matrix products, arithmetic and copies ran while one was open for 0% of the time, Pallas kernels for 1%

profile of v2, /device:TPU:0, one launch (start us, length us, event | category | flops | bytes accessed | tf_op | source)
XLA Modules:
  0.0 29.9 jit_solution(16587195670591247288)
XLA Ops:
  0.6 0.0 copy-start
  1.3 2.9 %forward.1 = (bf16[96,128,128]{2,1,0:T(8,128)(2,1)S(1)}, f32[32,16,128]{2,1,0:T(8,128)S(1)}, bf16[41,16,128]{2,1,0:T(8,128)(2,1)S(1)}, bf16[9,16,128]{2,1,0:T(8,...) custom-call(s32[1,1]{1,0:T(1,128)S(6)} %copy.9.counts, ...), custom_call_target="tpu_custom_call" | custom-call | flops 50331648 | bytes 3145728 | tf_op jit(solution)/shard_map/forward/pallas_call | solution.py:193
  4.2 3.0 %collective-permute-start = (bf16[41,16,128]{2,1,0:T(8,128)(2,1)S(1)}, bf16[41,16,128]{2,1,0:T(8,128)(2,1)S(1)}, u32[]{:S(2)}, u32[]{:S(2)}) collective-permute-start(bf16[41,16,128]{2,1,0:T(8,128)(2,1)S(1)} %get-tuple-element.15), channel_id=1, source_target_pairs={{0,2},{2,0},{4,6},{6,4},{8,10},{10,8},{12,14},{14,12},{1,3},{3,1},... | collective-permute-start | bytes 503816 | tf_op jit(solution)/shard_map/ppermute | solution.py:224
  7.2 4.3 %collective-permute-done.got = bf16[41,16,128]{2,1,0:T(8,128)(2,1)S(1)} collective-permute-done((bf16[41,16,128]{2,1,0:T(8,128)(2,1)S(1)}, bf16[41,16,128]{2,1,0:T(8,128)(2,1)S(1)}, u32[]{:S(2)}, u32[]{:S(2)}) %collective-permute-start) | collective-permute-done | bytes 167968 | tf_op jit(solution)/shard_map/ppermute | solution.py:224
  11.6 1.9 %collective-permute-start.1 = (bf16[32,16,128]{2,1,0:T(8,128)(2,1)S(1)}, bf16[32,16,128]{2,1,0:T(8,128)(2,1)S(1)}, u32[]{:S(2)}, u32[]{:S(2)}) collective-permute-start(bf16[32,16,128]{2,1,0:T(8,128)(2,1)S(1)} %fusion), channel_id=1, source_target_pairs={{0,4},{2,6},{4,0},{6,2},{8,12},{10,14},{12,8},{14,10},{1,5},{3,7},... | collective-permute-start | bytes 393224 | tf_op jit(solution)/shard_map/ppermute | solution.py:224
  13.5 0.7 %collective-permute-start.2 = (bf16[9,16,128]{2,1,0:T(8,128)(2,1)S(1)}, bf16[9,16,128]{2,1,0:T(8,128)(2,1)S(1)}, u32[]{:S(2)}, u32[]{:S(2)}) collective-permute-start(bf16[9,16,128]{2,1,0:T(8,128)(2,1)S(1)} %get-tuple-element.17), channel_id=1, source_target_pairs={{2,4},{6,8},{10,12},{4,2},{8,6},{12,10},{3,5},{7,9},{11,13},{5,3},... | collective-permute-start | bytes 110600 | tf_op jit(solution)/shard_map/ppermute | solution.py:220
  14.1 2.5 %collective-permute-done.1 = bf16[32,16,128]{2,1,0:T(8,128)(2,1)S(1)} collective-permute-done((bf16[32,16,128]{2,1,0:T(8,128)(2,1)S(1)}, bf16[32,16,128]{2,1,0:T(8,128)(2,1)S(1)}, u32[]{:S(2)}, u32[]{:S(2)}) %collective-permute-start.1) | collective-permute-done | bytes 131104 | tf_op jit(solution)/shard_map/ppermute | solution.py:224
  16.6 0.1 fusion.1
  16.6 0.0 collective-permute-done.2.odd
  16.7 6.4 %collective-permute-start.3 = (bf16[32,16,128]{2,1,0:T(8,128)(2,1)S(1)}, bf16[32,16,128]{2,1,0:T(8,128)(2,1)S(1)}, u32[]{:S(2)}, u32[]{:S(2)}) collective-permute-start(bf16[32,16,128]{2,1,0:T(8,128)(2,1)S(1)} %get-tuple-element.23), channel_id=1, source_target_pairs={{0,8},{2,10},{4,12},{6,14},{8,0},{10,2},{12,4},{14,6},{1,9},{3,11}... | collective-permute-start | bytes 393224 | tf_op jit(solution)/shard_map/ppermute | solution.py:224
  23.1 4.0 %collective-permute-done.3.got = bf16[32,16,128]{2,1,0:T(8,128)(2,1)S(1)} collective-permute-done((bf16[32,16,128]{2,1,0:T(8,128)(2,1)S(1)}, bf16[32,16,128]{2,1,0:T(8,128)(2,1)S(1)}, u32[]{:S(2)}, u32[]{:S(2)}) %collective-permute-start.3) | collective-permute-done | bytes 131104 | tf_op jit(solution)/shard_map/ppermute | solution.py:224
  27.1 0.0 copy-done
  27.1 0.7 %backward.1.mine = bf16[16,16,128]{2,1,0:T(8,128)(2,1)S(1)} custom-call(s32[1,1]{1,0:T(1,128)S(6)} %copy.9.counts, s32[1,1,96]{2,1,0:T(1,128)S(4)} %get-tuple-element.19.rows, s32[1,1,96]{2,1,0:T(1,128)S(4)} %get-tuple-element.20.cols, bf16[96,128,128]{2,1,0:T(8,128)(2,1)S(1)} %get-tuple-element.21.tiles, f32[32,16,128]{2,1,0:T(8,128)S(1)} %get-tuple-element.22.total, ...), custom_call_target="tpu_custom_call" | custom-call | flops 50331648 | bytes 3145728 | tf_op jit(solution)/shard_map/backward/pallas_call | solution.py:235
  27.8 0.1 collective-permute-start.4
  27.9 0.4 %smooth.1 = f32[16,16,128]{2,1,0:T(8,128)S(1)} custom-call(f32[16,16,128]{2,1,0:T(8,128)S(1)} %get-tuple-element.13.flat, f32[2,1024]{1,0:T(2,128)S(1)} %get-tuple-element.14.stiff, bf16[41,16,128]{2,1,0:T(8,128)(2,1)S(1)} %collective-permute-done.got, bf16[9,16,128]{2,1,0:T(8,128)(2,1)S(1)} %collective-permute-done.2.odd), custom_call_target="tpu_custom_call" | custom-call | tf_op jit(solution)/shard_map/smooth/pallas_call | solution.py:251
  28.2 0.9 %collective-permute-done.4.other = bf16[16,16,128]{2,1,0:T(8,128)(2,1)S(1)} collective-permute-done((bf16[16,16,128]{2,1,0:T(8,128)(2,1)S(1)}, bf16[16,16,128]{2,1,0:T(8,128)(2,1)S(1)}, u32[]{:S(2)}, u32[]{:S(2)}) %collective-permute-start.4) | collective-permute-done | bytes 65568 | tf_op jit(solution)/shard_map/ppermute | solution.py:249
  29.1 0.8 %combine.1 = (f32[16,2,1024]{2,1,0:T(2,128)}, f32[2,1024]{1,0:T(2,128)}) custom-call(f32[16,16,128]{2,1,0:T(8,128)S(1)} %get-tuple-element.13.flat, f32[16,16,128]{2,1,0:T(8,128)S(1)} %smooth.1, bf16[16,16,128]{2,1,0:T(8,128)(2,1)S(1)} %backward.1.mine, bf16[16,16,128]{2,1,0:T(8,128)(2,1)S(1)} %collective-permute-done.4.other), custom_call_target="tpu_custom_call" | custom-call | tf_op jit(solution)/shard_map/combine/pallas_call | solution.py:261
  (1 shorter events, 0.0 us)
Async XLA Ops:
  0.6 26.5 %copy-start = (f32[4096]{0:T(1024)S(1)}, f32[4096]{0:T(1024)}, u32[]{:S(2)}) copy-start(f32[4096]{0:T(1024)} %param.11) | copy-start | bytes 49156
  4.2 7.3 %collective-permute-start = (bf16[41,16,128]{2,1,0:T(8,128)(2,1)S(1)}, bf16[41,16,128]{2,1,0:T(8,128)(2,1)S(1)}, u32[]{:S(2)}, u32[]{:S(2)}) collective-permute-start(bf16[41,16,128]{2,1,0:T(8,128)(2,1)S(1)} %get-tuple-element.15), channel_id=1, source_target_pairs={{0,2},{2,0},{4,6},{6,4},{8,10},{10,8},{12,14},{14,12},{1,3},{3,1},... | collective-permute-start | bytes 503816 | tf_op jit(solution)/shard_map/ppermute | solution.py:224
  11.6 5.0 %collective-permute-start.1 = (bf16[32,16,128]{2,1,0:T(8,128)(2,1)S(1)}, bf16[32,16,128]{2,1,0:T(8,128)(2,1)S(1)}, u32[]{:S(2)}, u32[]{:S(2)}) collective-permute-start(bf16[32,16,128]{2,1,0:T(8,128)(2,1)S(1)} %fusion), channel_id=1, source_target_pairs={{0,4},{2,6},{4,0},{6,2},{8,12},{10,14},{12,8},{14,10},{1,5},{3,7},... | collective-permute-start | bytes 393224 | tf_op jit(solution)/shard_map/ppermute | solution.py:224
  13.5 3.2 %collective-permute-start.2 = (bf16[9,16,128]{2,1,0:T(8,128)(2,1)S(1)}, bf16[9,16,128]{2,1,0:T(8,128)(2,1)S(1)}, u32[]{:S(2)}, u32[]{:S(2)}) collective-permute-start(bf16[9,16,128]{2,1,0:T(8,128)(2,1)S(1)} %get-tuple-element.17), channel_id=1, source_target_pairs={{2,4},{6,8},{10,12},{4,2},{8,6},{12,10},{3,5},{7,9},{11,13},{5,3},... | collective-permute-start | bytes 110600 | tf_op jit(solution)/shard_map/ppermute | solution.py:220
  16.7 10.4 %collective-permute-start.3 = (bf16[32,16,128]{2,1,0:T(8,128)(2,1)S(1)}, bf16[32,16,128]{2,1,0:T(8,128)(2,1)S(1)}, u32[]{:S(2)}, u32[]{:S(2)}) collective-permute-start(bf16[32,16,128]{2,1,0:T(8,128)(2,1)S(1)} %get-tuple-element.23), channel_id=1, source_target_pairs={{0,8},{2,10},{4,12},{6,14},{8,0},{10,2},{12,4},{14,6},{1,9},{3,11}... | collective-permute-start | bytes 393224 | tf_op jit(solution)/shard_map/ppermute | solution.py:224
  27.8 1.3 %collective-permute-start.4 = (bf16[16,16,128]{2,1,0:T(8,128)(2,1)S(1)}, bf16[16,16,128]{2,1,0:T(8,128)(2,1)S(1)}, u32[]{:S(2)}, u32[]{:S(2)}) collective-permute-start(bf16[16,16,128]{2,1,0:T(8,128)(2,1)S(1)} %backward.1.mine), channel_id=1, source_target_pairs={{0,1},{1,0},{2,3},{3,2},{4,5},{5,4},{6,7},{7,6},{8,9},{9,8},{10,11... | collective-permute-start | bytes 196616 | tf_op jit(solution)/shard_map/ppermute | solution.py:249

commit v3 on v2

--- a/solution.py
+++ b/solution.py
@@ -19,9 +19,13 @@
     return [tuple(range(n, min(n + 2, start + size))) for n in range(start, start + size, 2)]
 
 
+def looks_up():
+    return lax.rem(lax.axis_index("cell") + lax.axis_index("ray"), 2) == 1
+
+
 def forward_kernel(
     counts, rows_in, cols_in, blocks, probes_in, stiff_in,
-    tiles, total, sent, odd, flat, stiff, rows, cols,
+    tiles, total, sent, edge, flat, stiff, rows, cols,
     probes, acc, flat16, sems, small,
 ):
     slots, width = tiles.shape[0], tiles.shape[1]
@@ -46,19 +50,14 @@
             value = probes[:, s, j * width : (j + 1) * width]
             flat[s * each + j] = value
             flat16[s * each + j] = value.astype(BF16)
-    even = lax.rem(lax.axis_index("cell"), 2) == 0
-    top = (slabs - 1) * each
+    upper, top = looks_up(), (slabs - 1) * each
     for j in range(each):
-        low, high = flat16[j], flat16[top + j]
-        sent[nrows + j] = jnp.where(even, high, low)
-        odd[j] = jnp.where(even, low, high)
-    sent[nrows + each] = jnp.zeros((nprobe, width), BF16)
-    odd[each] = jnp.zeros((nprobe, width), BF16)
+        edge[j] = jnp.where(upper, flat16[top + j], flat16[j])
+    edge[each] = jnp.zeros((nprobe, width), BF16)
     for j in range(each):
-        low = stiff[0:1, j * width : (j + 1) * width].astype(BF16)
-        high = stiff[slabs - 1 : slabs, j * width : (j + 1) * width].astype(BF16)
-        sent[nrows + each, j : j + 1, :] = jnp.where(even, high, low)
-        odd[each, j : j + 1, :] = jnp.where(even, low, high)
+        low = stiff[0:1, j * width : (j + 1) * width]
+        high = stiff[slabs - 1 : slabs, j * width : (j + 1) * width]
+        edge[each, j : j + 1, :] = jnp.where(upper, high, low).astype(BF16)
     live = counts[0, 0]
     for copy, (start, size) in zip(copies, runs):
         copy.wait()
@@ -75,10 +74,12 @@
             acc[jnp.where(n < live, rows[0, 0, n], nrows)] += out
     value = acc[0:nrows]
     total[...] = value
-    sent[0:nrows] = value.astype(BF16)
-
-
-def backward_kernel(counts, rows, cols, tiles, total, got, weight, part, weighted, acc):
+    sent[...] = value.astype(BF16)
+
+
+def backward_kernel(
+    counts, rows, cols, tiles, total, got, weight, flat, stiff, beyond, part, weighted, acc
+):
     slots, width = tiles.shape[0], tiles.shape[1]
     nrows, nprobe = total.shape[0], total.shape[1]
     ncols = part.shape[0]
@@ -98,38 +99,33 @@
         ]
     for n, out in outs:
         acc[jnp.where(n < live, cols[0, 0, n], ncols)] += out
+    slabs, plane = stiff.shape
+    each = plane // width
+    upper = looks_up()
+    base = jnp.where(upper, (slabs - 1) * each, 0)
+    for j in range(each):
+        span = slice(j * width, (j + 1) * width)
+        here = jnp.where(upper, stiff[slabs - 1 : slabs, span], stiff[0:1, span])
+        scale = 0.5 * (here + beyond[each, j : j + 1, :].astype(F32))
+        acc[base + j] += scale * (flat[base + j] - beyond[j].astype(F32))
     part[...] = acc[0:ncols].astype(BF16)
 
 
-def smooth_kernel(flat, stiff, got, odd, smooth, below, above):
+def smooth_kernel(flat, stiff, smooth):
     ncols, nprobe, width = flat.shape
     slabs = stiff.shape[0]
     each = ncols // slabs
-    nrows = got.shape[0] - each - 1
     lane = lax.broadcasted_iota(I32, (1, width), 1)
     at_z = lane % NZ
-    even = lax.rem(lax.axis_index("cell"), 2) == 0
-    for j in range(each + 1):
-        pair, other = got[nrows + j], odd[j]
-        below[j] = jnp.where(even, other, pair).astype(F32)
-        above[j] = jnp.where(even, pair, other).astype(F32)
 
     def stiff_at(s, j):
         if j < 0 or j >= each:
             return jnp.zeros((1, width), F32)
-        if s < 0:
-            return below[each, j : j + 1, :]
-        if s >= slabs:
-            return above[each, j : j + 1, :]
         return stiff[s : s + 1, j * width : (j + 1) * width]
 
     def probe_at(s, j):
         if j < 0 or j >= each:
             return jnp.zeros((nprobe, width), F32)
-        if s < 0:
-            return below[j]
-        if s >= slabs:
-            return above[j]
         return flat[s * each + j]
 
     def up(value, by):
@@ -140,9 +136,7 @@
 
     def neighbours(at, s, j):
         here, before, after = at(s, j), at(s, j - 1), at(s, j + 1)
-        return [
-            at(s + 1, j),
-            at(s - 1, j),
+        return [at(t, j) for t in (s - 1, s + 1) if 0 <= t < slabs] + [
             jnp.where(lane < width - NZ, up(here, NZ), up(after, NZ)),
             jnp.where(lane >= NZ, down(here, NZ), down(before, NZ)),
             jnp.where(at_z < NZ - 1, up(here, 1), 0.0),
@@ -190,12 +184,12 @@
         pltpu.with_memory_space_constraint(x, pltpu.HBM)
         for x in (row_ids, col_ids, blocks, probes, stiffness)
     ]
-    tiles, total, sent, odd, flat, stiff, rows, cols = pl.pallas_call(
+    tiles, total, sent, edge, flat, stiff, rows, cols = pl.pallas_call(
         forward_kernel,
         out_shape=(
             pltpu.VMEM((slots, width, width), BF16),
             pltpu.VMEM((nrows, nprobe, width), F32),
-            pltpu.VMEM((nrows + each + 1, nprobe, width), BF16),
+            pltpu.VMEM((nrows, nprobe, width), BF16),
             pltpu.VMEM((each + 1, nprobe, width), BF16),
             pltpu.VMEM((ncols, nprobe, width), F32),
             pltpu.VMEM((slabs, plane), F32),
@@ -216,26 +210,24 @@
         name="forward",
     )(counts, *pinned)
 
-    above_odd = [(i, i + 1) for i in range(1, ncell - 1, 2)]
-    across = lax.ppermute(odd, "cell", above_odd + [(j, i) for i, j in above_odd])
-
-    step = 1
-    while True:
-        got = lax.ppermute(sent, "cell", [(i, i ^ step) for i in range(ncell)])
-        if step == 1:
-            halo = got
-        step *= 2
-        if step == ncell:
-            break
-        total = total + got[:nrows].astype(F32)
-        sent = total.astype(BF16)
-        if step == 4:
-            total, sent, across = lax.optimization_barrier((total, sent, across))
+    first = [(c, r) for c in range(ncell - 1) for r in range(nray) if (c + r) % 2 == 1]
+    ends = [(c * nray + r, (c + 1) * nray + r) for c, r in first]
+    beyond = lax.ppermute(edge, ("cell", "ray"), ends + [(j, i) for i, j in ends])
+
+    steps = [1 << i for i in range(ncell.bit_length() - 1)]
+    turns = list(zip(steps, steps[-1:] + steps[:-1]))
+    for i, turn in enumerate(turns):
+        pairs = [(c * nray + r, (c ^ turn[r]) * nray + r) for c in range(ncell) for r in range(nray)]
+        got = lax.ppermute(sent, ("cell", "ray"), pairs)
+        if i < len(turns) - 1:
+            total = total + got.astype(F32)
+            sent = total.astype(BF16)
+    got, beyond = lax.optimization_barrier((got, beyond))
 
     part = pl.pallas_call(
         backward_kernel,
         out_shape=pltpu.VMEM((ncols, nprobe, width), BF16),
-        in_specs=[SMEM] * 3 + [VMEM] * 4,
+        in_specs=[SMEM] * 3 + [VMEM] * 7,
         out_specs=VMEM,
         scratch_shapes=[
             pltpu.VMEM((nrows, nprobe, width), BF16),
@@ -244,19 +236,18 @@
         compiler_params=params,
         cost_estimate=cost,
         name="backward",
-    )(counts, rows, cols, tiles, total, got, ray_weight.reshape(nrows, width))
+    )(counts, rows, cols, tiles, total, got, ray_weight.reshape(nrows, width), flat, stiff, beyond)
 
     other = lax.ppermute(part, "ray", [(0, 1), (1, 0)])
 
     smooth = pl.pallas_call(
         smooth_kernel,
         out_shape=pltpu.VMEM((ncols, nprobe, width), F32),
-        in_specs=[VMEM] * 4,
+        in_specs=[VMEM] * 2,
         out_specs=VMEM,
-        scratch_shapes=[pltpu.VMEM((each + 1, nprobe, width), F32)] * 2,
         compiler_params=params,
         name="smooth",
-    )(flat, stiff, halo, across)
+    )(flat, stiff)
 
     return pl.pallas_call(
         combine_kernel,

time: 30.1 us -> 27.1 us (0.900)
  the two profiles are of different devices: /device:TPU:0 before, /device:TPU:9 now
where the time goes in v3:
time: 27.1 us; the launch traced here: 26.9 us
  starting transfers between devices  12.5 us (46%)
  waiting for transfers between devices  8.27 us (31%)
  Pallas kernels  4.71 us (17%)
  between operations  1.34 us (5%)
    ppermute x3, waiting for transfers between devices, local(): got = lax.ppermute(sent, ('cell', 'ray'), pairs)  6.1 us
    ppermute x1, starting transfers between devices, local(): other = lax.ppermute(part, 'ray', [(0, 1), (1, 0)])  4.91 us
    ppermute x3, starting transfers between devices, local(): got = lax.ppermute(sent, ('cell', 'ray'), pairs)  4.16 us
    ppermute x1, starting transfers between devices, local(): lax.ppermute(edge, ('cell', 'ray'), ends + [(j, i) for i, j in ends])  3.44 us
    pallas_call x1, Pallas kernels, local(): pl.pallas_call(forward_kernel, out_shape=(pltpu.VMEM((slots, width, width...  2.87 us
    ppermute x1, waiting for transfers between devices, local(): lax.ppermute(edge, ('cell', 'ray'), ends + [(j, i) for i, j in ends])  1.63 us
    pallas_call x1, Pallas kernels, local(): pl.pallas_call(combine_kernel, out_shape=(jax.ShapeDtypeStruct((nprobe, s...  0.76 us
    pallas_call x1, Pallas kernels, local(): pl.pallas_call(backward_kernel, out_shape=pltpu.VMEM((ncols, nprobe, widt...  0.72 us
  transfers between devices with their start and end apart: 5, of which 4 were waited for; matrix products, arithmetic and copies ran while one was open for 0% of the time, Pallas kernels for 1%

profile of v3, /device:TPU:9, one launch (start us, length us, event | category | flops | bytes accessed | tf_op | source)
XLA Modules:
  0.0 26.9 jit_solution(8873365545420308911)
XLA Ops:
  0.6 0.0 copy-start
  1.3 2.9 %forward.1 = (bf16[96,128,128]{2,1,0:T(8,128)(2,1)S(1)}, f32[32,16,128]{2,1,0:T(8,128)S(1)}, bf16[32,16,128]{2,1,0:T(8,128)(2,1)S(1)}, bf16[9,16,128]{2,1,0:T(8,...) custom-call(s32[1,1]{1,0:T(1,128)S(6)} %copy.9.counts, ...), custom_call_target="tpu_custom_call" | custom-call | flops 50331648 | bytes 3145728 | tf_op jit(solution)/shard_map/forward/pallas_call | solution.py:187
  4.2 2.4 %collective-permute-start = (bf16[32,16,128]{2,1,0:T(8,128)(2,1)S(1)}, bf16[32,16,128]{2,1,0:T(8,128)(2,1)S(1)}, u32[]{:S(2)}, u32[]{:S(2)}) collective-permute-start(bf16[32,16,128]{2,1,0:T(8,128)(2,1)S(1)} %get-tuple-element.18), channel_id=1, source_target_pairs={{0,2},{1,9},{2,0},{3,11},{4,6},{5,13},{6,4},{7,15},{8,10},{9,1},{1... | collective-permute-start | bytes 393224 | tf_op jit(solution)/shard_map/ppermute | solution.py:221
  6.5 3.2 %collective-permute-done = bf16[32,16,128]{2,1,0:T(8,128)(2,1)S(1)} collective-permute-done((bf16[32,16,128]{2,1,0:T(8,128)(2,1)S(1)}, bf16[32,16,128]{2,1,0:T(8,128)(2,1)S(1)}, u32[]{:S(2)}, u32[]{:S(2)}) %collective-permute-start) | collective-permute-done | bytes 131104 | tf_op jit(solution)/shard_map/ppermute | solution.py:221
  9.8 1.3 %collective-permute-start.1 = (bf16[32,16,128]{2,1,0:T(8,128)(2,1)S(1)}, bf16[32,16,128]{2,1,0:T(8,128)(2,1)S(1)}, u32[]{:S(2)}, u32[]{:S(2)}) collective-permute-start(bf16[32,16,128]{2,1,0:T(8,128)(2,1)S(1)} %fusion), channel_id=1, source_target_pairs={{0,4},{1,3},{2,6},{3,1},{4,0},{5,7},{6,2},{7,5},{8,12},{9,11},{10,... | collective-permute-start | bytes 393224 | tf_op jit(solution)/shard_map/ppermute | solution.py:221
  11.1 2.9 %collective-permute-done.1 = bf16[32,16,128]{2,1,0:T(8,128)(2,1)S(1)} collective-permute-done((bf16[32,16,128]{2,1,0:T(8,128)(2,1)S(1)}, bf16[32,16,128]{2,1,0:T(8,128)(2,1)S(1)}, u32[]{:S(2)}, u32[]{:S(2)}) %collective-permute-start.1) | collective-permute-done | bytes 131104 | tf_op jit(solution)/shard_map/ppermute | solution.py:221
  14.0 0.1 fusion.1
  14.0 0.5 %collective-permute-start.2 = (bf16[32,16,128]{2,1,0:T(8,128)(2,1)S(1)}, bf16[32,16,128]{2,1,0:T(8,128)(2,1)S(1)}, u32[]{:S(2)}, u32[]{:S(2)}) collective-permute-start(bf16[32,16,128]{2,1,0:T(8,128)(2,1)S(1)} %get-tuple-element.22), channel_id=1, source_target_pairs={{0,8},{1,5},{2,10},{3,7},{4,12},{5,1},{6,14},{7,3},{8,0},{9,13},{1... | collective-permute-start | bytes 393224 | tf_op jit(solution)/shard_map/ppermute | solution.py:221
  14.5 3.4 %collective-permute-start.3 = (bf16[9,16,128]{2,1,0:T(8,128)(2,1)S(1)}, bf16[9,16,128]{2,1,0:T(8,128)(2,1)S(1)}, u32[]{:S(2)}, u32[]{:S(2)}) collective-permute-start(bf16[9,16,128]{2,1,0:T(8,128)(2,1)S(1)} %get-tuple-element.19), channel_id=1, source_target_pairs={{1,3},{2,4},{5,7},{6,8},{9,11},{10,12},{13,15},{3,1},{4,2},{7,5},{... | collective-permute-start | bytes 110600 | tf_op jit(solution)/shard_map/ppermute | solution.py:215
  18.0 1.6 %collective-permute-done.3.beyond = bf16[9,16,128]{2,1,0:T(8,128)(2,1)S(1)} collective-permute-done((bf16[9,16,128]{2,1,0:T(8,128)(2,1)S(1)}, bf16[9,16,128]{2,1,0:T(8,128)(2,1)S(1)}, u32[]{:S(2)}, u32[]{:S(2)}) %collective-permute-start.3) | collective-permute-done | bytes 36896 | tf_op jit(solution)/shard_map/ppermute | solution.py:215
  19.6 0.0 collective-permute-done.2.got
  19.6 0.0 copy-done
  19.6 0.7 %backward.1.mine = bf16[16,16,128]{2,1,0:T(8,128)(2,1)S(1)} custom-call(s32[1,1]{1,0:T(1,128)S(6)} %copy.9.counts, s32[1,1,96]{2,1,0:T(1,128)S(4)} %get-tuple-element.14.rows, s32[1,1,96]{2,1,0:T(1,128)S(4)} %get-tuple-element.15.cols, bf16[96,128,128]{2,1,0:T(8,128)(2,1)S(1)} %get-tuple-element.16.tiles, f32[32,16,128]{2,1,0:T(8,128)S(1)} %get-tuple-element.23.total, ...), custom_call_target="tpu_custom_call" | custom-call | flops 50331648 | bytes 3145728 | tf_op jit(solution)/shard_map/backward/pallas_call | solution.py:227
  20.3 4.9 %collective-permute-start.4 = (bf16[16,16,128]{2,1,0:T(8,128)(2,1)S(1)}, bf16[16,16,128]{2,1,0:T(8,128)(2,1)S(1)}, u32[]{:S(2)}, u32[]{:S(2)}) collective-permute-start(bf16[16,16,128]{2,1,0:T(8,128)(2,1)S(1)} %backward.1.mine), channel_id=1, source_target_pairs={{0,1},{1,0},{2,3},{3,2},{4,5},{5,4},{6,7},{7,6},{8,9},{9,8},{10,11... | collective-permute-start | bytes 196616 | tf_op jit(solution)/shard_map/ppermute | solution.py:241
  25.3 0.4 %smooth.1 = f32[16,16,128]{2,1,0:T(8,128)S(1)} custom-call(f32[16,16,128]{2,1,0:T(8,128)S(1)} %get-tuple-element.12.flat, f32[2,1024]{1,0:T(2,128)S(1)} %get-tuple-element.13.stiff), custom_call_target="tpu_custom_call" | custom-call | tf_op jit(solution)/shard_map/smooth/pallas_call | solution.py:243
  25.6 0.5 %collective-permute-done.4.other = bf16[16,16,128]{2,1,0:T(8,128)(2,1)S(1)} collective-permute-done((bf16[16,16,128]{2,1,0:T(8,128)(2,1)S(1)}, bf16[16,16,128]{2,1,0:T(8,128)(2,1)S(1)}, u32[]{:S(2)}, u32[]{:S(2)}) %collective-permute-start.4) | collective-permute-done | bytes 65568 | tf_op jit(solution)/shard_map/ppermute | solution.py:241
  26.2 0.8 %combine.1 = (f32[16,2,1024]{2,1,0:T(2,128)}, f32[2,1024]{1,0:T(2,128)}) custom-call(f32[16,16,128]{2,1,0:T(8,128)S(1)} %get-tuple-element.12.flat, f32[16,16,128]{2,1,0:T(8,128)S(1)} %smooth.1, bf16[16,16,128]{2,1,0:T(8,128)(2,1)S(1)} %backward.1.mine, bf16[16,16,128]{2,1,0:T(8,128)(2,1)S(1)} %collective-permute-done.4.other), custom_call_target="tpu_custom_call" | custom-call | tf_op jit(solution)/shard_map/combine/pallas_call | solution.py:252
  (1 shorter events, 0.0 us)
Async XLA Ops:
  0.6 19.0 %copy-start = (f32[4096]{0:T(1024)S(1)}, f32[4096]{0:T(1024)}, u32[]{:S(2)}) copy-start(f32[4096]{0:T(1024)} %param.11) | copy-start | bytes 49156
  4.2 5.6 %collective-permute-start = (bf16[32,16,128]{2,1,0:T(8,128)(2,1)S(1)}, bf16[32,16,128]{2,1,0:T(8,128)(2,1)S(1)}, u32[]{:S(2)}, u32[]{:S(2)}) collective-permute-start(bf16[32,16,128]{2,1,0:T(8,128)(2,1)S(1)} %get-tuple-element.18), channel_id=1, source_target_pairs={{0,2},{1,9},{2,0},{3,11},{4,6},{5,13},{6,4},{7,15},{8,10},{9,1},{1... | collective-permute-start | bytes 393224 | tf_op jit(solution)/shard_map/ppermute | solution.py:221
  9.8 4.2 %collective-permute-start.1 = (bf16[32,16,128]{2,1,0:T(8,128)(2,1)S(1)}, bf16[32,16,128]{2,1,0:T(8,128)(2,1)S(1)}, u32[]{:S(2)}, u32[]{:S(2)}) collective-permute-start(bf16[32,16,128]{2,1,0:T(8,128)(2,1)S(1)} %fusion), channel_id=1, source_target_pairs={{0,4},{1,3},{2,6},{3,1},{4,0},{5,7},{6,2},{7,5},{8,12},{9,11},{10,... | collective-permute-start | bytes 393224 | tf_op jit(solution)/shard_map/ppermute | solution.py:221
  14.0 5.6 %collective-permute-start.2 = (bf16[32,16,128]{2,1,0:T(8,128)(2,1)S(1)}, bf16[32,16,128]{2,1,0:T(8,128)(2,1)S(1)}, u32[]{:S(2)}, u32[]{:S(2)}) collective-permute-start(bf16[32,16,128]{2,1,0:T(8,128)(2,1)S(1)} %get-tuple-element.22), channel_id=1, source_target_pairs={{0,8},{1,5},{2,10},{3,7},{4,12},{5,1},{6,14},{7,3},{8,0},{9,13},{1... | collective-permute-start | bytes 393224 | tf_op jit(solution)/shard_map/ppermute | solution.py:221
  14.5 5.1 %collective-permute-start.3 = (bf16[9,16,128]{2,1,0:T(8,128)(2,1)S(1)}, bf16[9,16,128]{2,1,0:T(8,128)(2,1)S(1)}, u32[]{:S(2)}, u32[]{:S(2)}) collective-permute-start(bf16[9,16,128]{2,1,0:T(8,128)(2,1)S(1)} %get-tuple-element.19), channel_id=1, source_target_pairs={{1,3},{2,4},{5,7},{6,8},{9,11},{10,12},{13,15},{3,1},{4,2},{7,5},{... | collective-permute-start | bytes 110600 | tf_op jit(solution)/shard_map/ppermute | solution.py:215
  20.3 5.8 %collective-permute-start.4 = (bf16[16,16,128]{2,1,0:T(8,128)(2,1)S(1)}, bf16[16,16,128]{2,1,0:T(8,128)(2,1)S(1)}, u32[]{:S(2)}, u32[]{:S(2)}) collective-permute-start(bf16[16,16,128]{2,1,0:T(8,128)(2,1)S(1)} %backward.1.mine), channel_id=1, source_target_pairs={{0,1},{1,0},{2,3},{3,2},{4,5},{5,4},{6,7},{7,6},{8,9},{9,8},{10,11... | collective-permute-start | bytes 196616 | tf_op jit(solution)/shard_map/ppermute | solution.py:241

commit v4 on v3

v4 whole, which is shorter than its diff:
```python
import jax
import jax.numpy as jnp
from jax import lax
from jax.experimental import pallas as pl
from jax.experimental.pallas import tpu as pltpu
from jax.sharding import PartitionSpec as P

NZ = 32
F32 = jnp.float32
BF16 = jnp.bfloat16
I32 = jnp.int32
VMEM = pl.BlockSpec(memory_space=pltpu.VMEM)
SMEM = pl.BlockSpec(memory_space=pltpu.SMEM)
HBM = pl.BlockSpec(memory_space=pltpu.HBM)


def rows_of(ref, s, j, slabs, ncols):
    return pl.ds(j * slabs + s, ref.shape[0] // ncols, stride=ncols)


def groups(slots):
    return [tuple(range(n, min(n + 2, slots))) for n in range(0, slots, 2)]


def even_cell():
    return lax.rem(lax.axis_index("cell"), 2) == 0


def prepare_kernel(
    rows_in, cols_in, probes_in, stiff_in, flat, paired, odd, probes, stiff, rows, cols, sems
):
    ncols, slabs = flat.shape[0], stiff.shape[0] // (paired.shape[0] - 1)
    each = ncols // slabs
    pairs = [(probes_in, probes), (stiff_in, stiff), (rows_in, rows), (cols_in, cols)]
    copies = [pltpu.make_async_copy(a, b, sems.at[i]) for i, (a, b) in enumerate(pairs)]
    for copy in copies:
        copy.start()
    for copy in copies:
        copy.wait()
    for s in range(slabs):
        for j in range(each):
            flat[s * each + j] = probes[rows_of(probes, s, j, slabs, ncols), :].astype(BF16)
    even, top = even_cell(), (slabs - 1) * each
    for out, high in ((paired, even), (odd, jnp.logical_not(even))):
        for j in range(each):
            out[j] = jnp.where(high, flat[top + j], flat[j])
        low_end = stiff[pl.ds(0, each, stride=slabs), :]
        high_end = stiff[pl.ds(slabs - 1, each, stride=slabs), :]
        end = jnp.where(high, high_end, low_end)
        rest = jnp.zeros((out.shape[1] - each, out.shape[2]), F32)
        out[each] = jnp.concatenate([end, rest], axis=0).astype(BF16)


def forward_kernel(counts, rows, cols, tiles, flat, total, sent, acc):
    slots, width = tiles.shape[2], tiles.shape[3]
    nrows, nprobe = total.shape[0], total.shape[1]
    acc[...] = jnp.zeros_like(acc)
    live = counts[0, 0]
    outs = []
    for group in groups(slots):
        left = jnp.concatenate([flat[cols[0, 0, n]] for n in group], axis=0)
        right = jnp.concatenate([tiles[0, 0, n] for n in group], axis=0)
        out = lax.dot_general(left, right, (((1,), (1,)), ((), ())), preferred_element_type=F32)
        outs += [
            (n, out[i * nprobe : (i + 1) * nprobe, i * width : (i + 1) * width])
            for i, n in enumerate(group)
        ]
    for n, out in outs:
        acc[jnp.where(n < live, rows[0, 0, n], nrows)] += out
    value = acc[0:nrows]
    total[...] = value
    sent[...] = value.astype(BF16)


def backward_kernel(
    counts, rows, cols, tiles, total, got, weight, probes, stiff, paired, odd, part, weighted, acc
):
    slots, width = tiles.shape[2], tiles.shape[3]
    nrows, nprobe = total.shape[0], total.shape[1]
    ncols = part.shape[0]
    for k in range(nrows):
        value = total[k] + got[k].astype(F32)
        weighted[k] = (value * weight[k : k + 1, :]).astype(BF16)
    acc[...] = jnp.zeros_like(acc)
    live = counts[0, 0]
    outs = []
    for group in groups(slots):
        left = jnp.concatenate([weighted[rows[0, 0, n]] for n in group], axis=0)
        right = jnp.concatenate([tiles[0, 0, n] for n in group], axis=1)
        out = jnp.dot(left, right, preferred_element_type=F32)
        outs += [
            (n, out[i * nprobe : (i + 1) * nprobe, i * width : (i + 1) * width])
            for i, n in enumerate(group)
        ]
    for n, out in outs:
        acc[jnp.where(n < live, cols[0, 0, n], ncols)] += out
    each = paired.shape[0] - 1
    slabs = ncols // each
    mine = lax.axis_index("ray") == 1
    even, cell = even_cell(), lax.axis_index("cell")
    inner = jnp.logical_and(cell > 0, cell < lax.axis_size("cell") - 1)
    for s, near in (
        (0, jnp.where(even, odd[...], paired[...]).astype(F32)),
        (slabs - 1, jnp.where(even, paired[...], odd[...]).astype(F32)),
    ):
        there = jnp.logical_or(inner, even if s else jnp.logical_not(even))
        near = jnp.where(there, near, 0.0)
        for j in range(each):
            row = j * slabs + s
            scale = 0.5 * (stiff[row : row + 1, :] + near[each, j : j + 1, :])
            term = scale * (probes[rows_of(probes, s, j, slabs, ncols), :] - near[j])
            acc[s * each + j] += jnp.where(mine, term, 0.0)
    part[...] = acc[0:ncols].astype(BF16)


def smooth_kernel(probes, stiff, smooth, each):
    ncols, nprobe, width = smooth.shape
    slabs = ncols // each
    lane = lax.broadcasted_iota(I32, (1, width), 1)
    at_z = lane % NZ

    def stiff_at(s, j):
        if j < 0 or j >= each:
            return jnp.zeros((1, width), F32)
        return stiff[j * slabs + s : j * slabs + s + 1, :]

    def probe_at(s, j):
        if j < 0 or j >= each:
            return jnp.zeros((nprobe, width), F32)
        return probes[rows_of(probes, s, j, slabs, ncols), :]

    def up(value, by):
        return pltpu.roll(value, width - by, 1)

    def down(value, by):
        return pltpu.roll(value, by, 1)

    def neighbours(at, s, j):
        here, before, after = at(s, j), at(s, j - 1), at(s, j + 1)
        return [at(t, j) for t in (s - 1, s + 1) if 0 <= t < slabs] + [
            jnp.where(lane < width - NZ, up(here, NZ), up(after, NZ)),
            jnp.where(lane >= NZ, down(here, NZ), down(before, NZ)),
            jnp.where(at_z < NZ - 1, up(here, 1), 0.0),
            jnp.where(at_z > 0, down(here, 1), 0.0),
        ]

    for s in range(slabs):
        for j in range(each):
            here_s, here_p = stiff_at(s, j), probe_at(s, j)
            term = jnp.zeros((nprobe, width), F32)
            for near_s, near_p in zip(neighbours(stiff_at, s, j), neighbours(probe_at, s, j)):
                term = term + 0.5 * (here_s + near_s) * (here_p - near_p)
            smooth[s * each + j] = term


def combine_kernel(probes, smooth, mine, other, applied, diag, each):
    ncols = smooth.shape[0]
    slabs = ncols // each
    for s in range(slabs):
        for j in range(each):
            c, row = s * each + j, j * slabs + s
            value = mine[c].astype(F32) + other[c].astype(F32) + smooth[c]
            span = rows_of(probes, s, j, slabs, ncols)
            applied[span, :] = value
            diag[row : row + 1, :] = jnp.mean(probes[span, :] * value, axis=0, keepdims=True)


def to_rows(value, width):
    *lead, slabs, plane = value.shape
    value = value.reshape(*lead, slabs, plane // width, width)
    return jnp.swapaxes(value, -2, -3).reshape(-1, width)


def from_rows(value, shape):
    *lead, slabs, plane = shape
    width = value.shape[1]
    value = value.reshape(*lead, plane // width, slabs, width)
    return jnp.swapaxes(value, -2, -3).reshape(shape)


def local(blocks, row_ids, col_ids, counts, ray_weight, probes, stiffness):
    slots, width = blocks.shape[2], blocks.shape[3]
    nprobe, slabs, plane = probes.shape
    ncols = slabs * plane // width
    nrows = ray_weight.shape[0] // width
    each = plane // width
    ncell, nray = lax.axis_size("cell"), lax.axis_size("ray")
    assert ncell > 1 and ncell & (ncell - 1) == 0 and nray == 2
    params = pltpu.CompilerParams(vmem_limit_bytes=8 * 1024 * 1024)

    def cost(flops, moved):
        return pl.CostEstimate(flops=flops, bytes_accessed=moved, transcendentals=0)

    products = cost(2 * slots * nprobe * width * width, 2 * slots * width * width)
    edge = pltpu.VMEM((each + 1, nprobe, width), BF16)
    pinned = [
        pltpu.with_memory_space_constraint(x, pltpu.HBM)
        for x in (row_ids, col_ids, to_rows(probes, width), to_rows(stiffness, width))
    ]
    flat, paired, odd, grid, stiff, rows, cols = pl.pallas_call(
        prepare_kernel,
        out_shape=(
            pltpu.VMEM((ncols, nprobe, width), BF16),
            edge,
            edge,
            pltpu.VMEM((nprobe * ncols, width), F32),
            pltpu.VMEM((ncols, width), F32),
            pltpu.SMEM(row_ids.shape, I32),
            pltpu.SMEM(col_ids.shape, I32),
        ),
        in_specs=[HBM] * 4,
        out_specs=(VMEM,) * 5 + (SMEM,) * 2,
        scratch_shapes=[pltpu.SemaphoreType.DMA((4,))],
        compiler_params=params,
        cost_estimate=cost(12 * 10**8, 1000),
        name="prepare",
    )(*pinned)

    total, sent = pl.pallas_call(
        forward_kernel,
        out_shape=(
            pltpu.VMEM((nrows, nprobe, width), F32),
            pltpu.VMEM((nrows, nprobe, width), BF16),
        ),
        in_specs=[SMEM] * 3 + [VMEM] * 2,
        out_specs=(VMEM,) * 2,
        scratch_shapes=[pltpu.VMEM((nrows + 1, nprobe, width), F32)],
        compiler_params=params,
        cost_estimate=products,
        name="forward",
    )(counts, rows, cols, blocks, flat)

    def swap(value, first, cores):
        ends = [(c * nray + r, (c + 1) * nray + r) for c in range(first, ncell - 1, 2) for r in cores]
        return lax.ppermute(value, ("cell", "ray"), ends + [(j, i) for i, j in ends])

    paired, odd = swap(paired, 0, (0, 1)), swap(odd, 1, (1,))

    steps = [1 << i for i in range(ncell.bit_length() - 1)]
    turns = list(zip(steps, steps[-1:] + steps[:-1]))
    for i, turn in enumerate(turns):
        pairs = [(c * nray + r, (c ^ turn[r]) * nray + r) for c in range(ncell) for r in range(nray)]
        got = lax.ppermute(sent, ("cell", "ray"), pairs)
        if i == 0:
            got, odd = lax.optimization_barrier((got, odd))
        if i < len(turns) - 1:
            total = total + got.astype(F32)
            sent = total.astype(BF16)
    got, paired = lax.optimization_barrier((got, paired))

    part = pl.pallas_call(
        backward_kernel,
        out_shape=pltpu.VMEM((ncols, nprobe, width), BF16),
        in_specs=[SMEM] * 3 + [VMEM] * 8,
        out_specs=VMEM,
        scratch_shapes=[
            pltpu.VMEM((nrows, nprobe, width), BF16),
            pltpu.VMEM((ncols + 1, nprobe, width), F32),
        ],
        compiler_params=params,
        cost_estimate=products,
        name="backward",
    )(counts, rows, cols, blocks, total, got, ray_weight.reshape(nrows, width), grid, stiff, paired, odd)

    other = lax.ppermute(part, "ray", [(0, 1), (1, 0)])

    smooth = pl.pallas_call(
        lambda *refs: smooth_kernel(*refs, each=each),
        out_shape=pltpu.VMEM((ncols, nprobe, width), F32),
        in_specs=[VMEM] * 2,
        out_specs=VMEM,
        compiler_params=params,
        name="smooth",
    )(grid, stiff)

    applied, diag = pl.pallas_call(
        lambda *refs: combine_kernel(*refs, each=each),
        out_shape=(
            jax.ShapeDtypeStruct((nprobe * ncols, width), F32),
            jax.ShapeDtypeStruct((ncols, width), F32),
        ),
        in_specs=[VMEM] * 4,
        out_specs=(VMEM, VMEM),
        compiler_params=params,
        name="combine",
    )(grid, smooth, part, other)
    return from_rows(applied, probes.shape), from_rows(diag, stiffness.shape)


def solution(mesh):
    return jax.shard_map(
        local,
        mesh=mesh,
        in_specs=(
            P(("region", "cell"), "ray", None, None, None),
            P(("region", "cell"), "ray", None),
            P(("region", "cell"), "ray", None),
            P(("region", "cell"), "ray"),
            P(("region", "ray")),
            P(None, ("region", "cell"), None),
            P(("region", "cell"), None),
        ),
        out_specs=(P(None, ("region", "cell"), None), P(("region", "cell"), None)),
        check_vma=False,
    )
```

time: 27.1 us -> 25.1 us (0.926)
  the two profiles are of different devices: /device:TPU:9 before, /device:TPU:0 now
where the time goes in v4:
time: 25.1 us; the launch traced here: 24.9 us
  starting transfers between devices  10.7 us (43%)
  waiting for transfers between devices  8.4 us (33%)
  Pallas kernels  4.28 us (17%)
  between operations  1.51 us (6%)
    ppermute x3, starting transfers between devices, local(): got = lax.ppermute(sent, ('cell', 'ray'), pairs)  8.26 us
    ppermute x3, waiting for transfers between devices, local(): got = lax.ppermute(sent, ('cell', 'ray'), pairs)  5.23 us
    ppermute x2, waiting for transfers between devices, swap(): lax.ppermute(value, ('cell', 'ray'), ends + [(j, i) for i, j in ends])  2.45 us
    ppermute x2, starting transfers between devices, swap(): lax.ppermute(value, ('cell', 'ray'), ends + [(j, i) for i, j in ends])  2.16 us
    pallas_call x1, Pallas kernels, local(): pl.pallas_call(forward_kernel, out_shape=(pltpu.VMEM((nrows, nprobe, widt...  1.23 us
    pallas_call x1, Pallas kernels, local(): pl.pallas_call(prepare_kernel, out_shape=(pltpu.VMEM((ncols, nprobe, widt...  1.17 us
    pallas_call x1, Pallas kernels, local(): pl.pallas_call(backward_kernel, out_shape=pltpu.VMEM((ncols, nprobe, widt...  0.76 us
    pallas_call x1, Pallas kernels, local(): pl.pallas_call(lambda *refs: combine_kernel(*refs, each=each), out_shape=...  0.76 us
  transfers between devices with their start and end apart: 6, of which 4 were waited for; matrix products, arithmetic and copies ran while one was open for 0% of the time, Pallas kernels for 1%

profile of v4, /device:TPU:0, one launch (start us, length us, event | category | flops | bytes accessed | tf_op | source)
XLA Modules:
  0.0 24.9 jit_solution(17526719599745945419)
XLA Ops:
  0.6 0.0 copy-start
  1.4 1.2 %prepare.1 = (bf16[16,16,128]{2,1,0:T(8,128)(2,1)S(1)}, bf16[9,16,128]{2,1,0:T(8,128)(2,1)S(1)}, bf16[9,16,128]{2,1,0:T(8,128)(2,1)S(1)}, f32[256,128]{1,0:T(8,1...) custom-call(s32[1,1,96]{2,1,0:T(1,128)} %rows_in.1, s32[1,1,96]{2,1,0:T(1,128)} %cols_in.1, ...), custom_call_target="tpu_custom_call" | custom-call | flops 1200000000 | bytes 1000 | tf_op jit(solution)/shard_map/prepare/pallas_call | solution.py:200
  2.6 0.0 copy-start.1
  2.6 0.0 copy-done
  2.6 1.2 %forward.1 = (f32[32,16,128]{2,1,0:T(8,128)S(1)}, bf16[32,16,128]{2,1,0:T(8,128)(2,1)S(1)}) custom-call(s32[1,1]{1,0:T(1,128)S(6)} %copy.13.counts, s32[1,1,96]{2,1,0:T(1,128)S(4)} %get-tuple-element.19.rows, s32[1,1,96]{2,1,0:T(1,128)S(4)} %get-tuple-element.20.cols, bf16[1,1,96,128,128]{4,3,2,1,0:T(8,128)(2,1)S(1)} %copy-done, ...), custom_call_target="tpu_custom_call" | custom-call | flops 50331648 | bytes 3145728 | tf_op jit(solution)/shard_map/forward/pallas_call | solution.py:219
  3.9 3.0 %collective-permute-start = (bf16[32,16,128]{2,1,0:T(8,128)(2,1)S(1)}, bf16[32,16,128]{2,1,0:T(8,128)(2,1)S(1)}, u32[]{:S(2)}, u32[]{:S(2)}) collective-permute-start(bf16[32,16,128]{2,1,0:T(8,128)(2,1)S(1)} %get-tuple-element.23), channel_id=1, source_target_pairs={{0,2},{1,9},{2,0},{3,11},{4,6},{5,13},{6,4},{7,15},{8,10},{9,1},{1... | collective-permute-start | bytes 393224 | tf_op jit(solution)/shard_map/ppermute | solution.py:243
  6.9 0.7 %collective-permute-start.1 = (bf16[9,16,128]{2,1,0:T(8,128)(2,1)S(1)}, bf16[9,16,128]{2,1,0:T(8,128)(2,1)S(1)}, u32[]{:S(2)}, u32[]{:S(2)}) collective-permute-start(bf16[9,16,128]{2,1,0:T(8,128)(2,1)S(1)} %get-tuple-element.24), channel_id=1, source_target_pairs={{3,5},{7,9},{11,13},{5,3},{9,7},{13,11},{19,21},{23,25},{27,29},{2... | collective-permute-start | bytes 110600 | tf_op jit(solution)/shard_map/ppermute | solution.py:235
  7.5 0.0 collective-permute-done.1.odd
  7.5 2.3 %collective-permute-done = bf16[32,16,128]{2,1,0:T(8,128)(2,1)S(1)} collective-permute-done((bf16[32,16,128]{2,1,0:T(8,128)(2,1)S(1)}, bf16[32,16,128]{2,1,0:T(8,128)(2,1)S(1)}, u32[]{:S(2)}, u32[]{:S(2)}) %collective-permute-start) | collective-permute-done | bytes 131104 | tf_op jit(solution)/shard_map/ppermute | solution.py:243
  9.9 2.2 %collective-permute-start.2 = (bf16[32,16,128]{2,1,0:T(8,128)(2,1)S(1)}, bf16[32,16,128]{2,1,0:T(8,128)(2,1)S(1)}, u32[]{:S(2)}, u32[]{:S(2)}) collective-permute-start(bf16[32,16,128]{2,1,0:T(8,128)(2,1)S(1)} %fusion), channel_id=1, source_target_pairs={{0,4},{1,3},{2,6},{3,1},{4,0},{5,7},{6,2},{7,5},{8,12},{9,11},{10,... | collective-permute-start | bytes 393224 | tf_op jit(solution)/shard_map/ppermute | solution.py:243
  12.0 2.9 %collective-permute-done.2 = bf16[32,16,128]{2,1,0:T(8,128)(2,1)S(1)} collective-permute-done((bf16[32,16,128]{2,1,0:T(8,128)(2,1)S(1)}, bf16[32,16,128]{2,1,0:T(8,128)(2,1)S(1)}, u32[]{:S(2)}, u32[]{:S(2)}) %collective-permute-start.2) | collective-permute-done | bytes 131104 | tf_op jit(solution)/shard_map/ppermute | solution.py:243
  15.0 3.1 %collective-permute-start.3 = (bf16[32,16,128]{2,1,0:T(8,128)(2,1)S(1)}, bf16[32,16,128]{2,1,0:T(8,128)(2,1)S(1)}, u32[]{:S(2)}, u32[]{:S(2)}) collective-permute-start(bf16[32,16,128]{2,1,0:T(8,128)(2,1)S(1)} %get-tuple-element.32), channel_id=1, source_target_pairs={{0,8},{1,5},{2,10},{3,7},{4,12},{5,1},{6,14},{7,3},{8,0},{9,13},{1... | collective-permute-start | bytes 393224 | tf_op jit(solution)/shard_map/ppermute | solution.py:243
  18.1 1.5 %collective-permute-start.4 = (bf16[9,16,128]{2,1,0:T(8,128)(2,1)S(1)}, bf16[9,16,128]{2,1,0:T(8,128)(2,1)S(1)}, u32[]{:S(2)}, u32[]{:S(2)}) collective-permute-start(bf16[9,16,128]{2,1,0:T(8,128)(2,1)S(1)} %get-tuple-element.26), channel_id=1, source_target_pairs={{0,2},{1,3},{4,6},{5,7},{8,10},{9,11},{12,14},{13,15},{2,0},{3,1},... | collective-permute-start | bytes 110600 | tf_op jit(solution)/shard_map/ppermute | solution.py:235
  19.6 2.4 %collective-permute-done.4.paired = bf16[9,16,128]{2,1,0:T(8,128)(2,1)S(1)} collective-permute-done((bf16[9,16,128]{2,1,0:T(8,128)(2,1)S(1)}, bf16[9,16,128]{2,1,0:T(8,128)(2,1)S(1)}, u32[]{:S(2)}, u32[]{:S(2)}) %collective-permute-start.4) | collective-permute-done | bytes 36896 | tf_op jit(solution)/shard_map/ppermute | solution.py:235
  22.1 0.0 collective-permute-done.3.got
  22.1 0.0 copy-done.1
  22.1 0.8 %backward.1.refs_2_ = bf16[16,16,128]{2,1,0:T(8,128)(2,1)S(1)} custom-call(s32[1,1]{1,0:T(1,128)S(6)} %copy.13.counts, s32[1,1,96]{2,1,0:T(1,128)S(4)} %get-tuple-element.19.rows, s32[1,1,96]{2,1,0:T(1,128)S(4)} %get-tuple-element.20.cols, bf16[1,1,96,128,128]{4,3,2,1,0:T(8,128)(2,1)S(1)} %copy-done, f32[32,16,128]{2,1,0:T(8,128)S(1)} %get-tuple-element.33.total, ...), custom_call_target="tpu_custom_call" | custom-call | flops 50331648 | bytes 3145728 | tf_op jit(solution)/shard_map/backward/pallas_call | solution.py:251
  22.8 0.2 collective-permute-start.5
  23.1 0.4 %smooth.1.refs_1_ = f32[16,16,128]{2,1,0:T(8,128)S(1)} custom-call(f32[256,128]{1,0:T(8,128)S(1)} %get-tuple-element.17.refs_0_.probes, f32[16,128]{1,0:T(8,128)S(1)} %get-tuple-element.18.refs_1_.stiff), custom_call_target="tpu_custom_call" | custom-call | tf_op jit(solution)/shard_map/smooth/pallas_call | solution.py:267
  23.4 0.7 %collective-permute-done.5.refs_3_ = bf16[16,16,128]{2,1,0:T(8,128)(2,1)S(1)} collective-permute-done((bf16[16,16,128]{2,1,0:T(8,128)(2,1)S(1)}, bf16[16,16,128]{2,1,0:T(8,128)(2,1)S(1)}, u32[]{:S(2)}, u32[]{:S(2)}) %collective-permute-start.5) | collective-permute-done | bytes 65568 | tf_op jit(solution)/shard_map/ppermute | solution.py:265
  24.2 0.8 %combine.1 = (f32[256,128]{1,0:T(8,128)}, f32[16,128]{1,0:T(8,128)}) custom-call(f32[256,128]{1,0:T(8,128)S(1)} %get-tuple-element.17.refs_0_.probes, f32[16,16,128]{2,1,0:T(8,128)S(1)} %smooth.1.refs_1_, bf16[16,16,128]{2,1,0:T(8,128)(2,1)S(1)} %backward.1.refs_2_, bf16[16,16,128]{2,1,0:T(8,128)(2,1)S(1)} %collective-permute-done.5.refs_3_), custom_call_target="tpu_custom_call" | custom-call | tf_op jit(solution)/shard_map/combine/pallas_call | solution.py:276
  (2 shorter events, 0.1 us)
Async XLA Ops:
  0.6 2.0 %copy-start = (bf16[1,1,96,128,128]{4,3,2,1,0:T(8,128)(2,1)S(1)}, bf16[1,1,96,128,128]{4,3,2,1,0:T(8,128)(2,1)}, u32[]{:S(2)}) copy-start(bf16[1,1,96,128,128]{4,3,2,1,0:T(8,128)(2,1)} %tiles.3) | copy-start | bytes 9437188
  2.6 19.5 %copy-start.1 = (f32[4096]{0:T(1024)S(1)}, f32[4096]{0:T(1024)}, u32[]{:S(2)}) copy-start(f32[4096]{0:T(1024)} %param.11) | copy-start | bytes 49156
  3.9 5.9 %collective-permute-start = (bf16[32,16,128]{2,1,0:T(8,128)(2,1)S(1)}, bf16[32,16,128]{2,1,0:T(8,128)(2,1)S(1)}, u32[]{:S(2)}, u32[]{:S(2)}) collective-permute-start(bf16[32,16,128]{2,1,0:T(8,128)(2,1)S(1)} %get-tuple-element.23), channel_id=1, source_target_pairs={{0,2},{1,9},{2,0},{3,11},{4,6},{5,13},{6,4},{7,15},{8,10},{9,1},{1... | collective-permute-start | bytes 393224 | tf_op jit(solution)/shard_map/ppermute | solution.py:243
  6.9 0.7 %collective-permute-start.1 = (bf16[9,16,128]{2,1,0:T(8,128)(2,1)S(1)}, bf16[9,16,128]{2,1,0:T(8,128)(2,1)S(1)}, u32[]{:S(2)}, u32[]{:S(2)}) collective-permute-start(bf16[9,16,128]{2,1,0:T(8,128)(2,1)S(1)} %get-tuple-element.24), channel_id=1, source_target_pairs={{3,5},{7,9},{11,13},{5,3},{9,7},{13,11},{19,21},{23,25},{27,29},{2... | collective-permute-start | bytes 110600 | tf_op jit(solution)/shard_map/ppermute | solution.py:235
  9.9 5.1 %collective-permute-start.2 = (bf16[32,16,128]{2,1,0:T(8,128)(2,1)S(1)}, bf16[32,16,128]{2,1,0:T(8,128)(2,1)S(1)}, u32[]{:S(2)}, u32[]{:S(2)}) collective-permute-start(bf16[32,16,128]{2,1,0:T(8,128)(2,1)S(1)} %fusion), channel_id=1, source_target_pairs={{0,4},{1,3},{2,6},{3,1},{4,0},{5,7},{6,2},{7,5},{8,12},{9,11},{10,... | collective-permute-start | bytes 393224 | tf_op jit(solution)/shard_map/ppermute | solution.py:243
  15.0 7.0 %collective-permute-start.3 = (bf16[32,16,128]{2,1,0:T(8,128)(2,1)S(1)}, bf16[32,16,128]{2,1,0:T(8,128)(2,1)S(1)}, u32[]{:S(2)}, u32[]{:S(2)}) collective-permute-start(bf16[32,16,128]{2,1,0:T(8,128)(2,1)S(1)} %get-tuple-element.32), channel_id=1, source_target_pairs={{0,8},{1,5},{2,10},{3,7},{4,12},{5,1},{6,14},{7,3},{8,0},{9,13},{1... | collective-permute-start | bytes 393224 | tf_op jit(solution)/shard_map/ppermute | solution.py:243
  18.1 4.0 %collective-permute-start.4 = (bf16[9,16,128]{2,1,0:T(8,128)(2,1)S(1)}, bf16[9,16,128]{2,1,0:T(8,128)(2,1)S(1)}, u32[]{:S(2)}, u32[]{:S(2)}) collective-permute-start(bf16[9,16,128]{2,1,0:T(8,128)(2,1)S(1)} %get-tuple-element.26), channel_id=1, source_target_pairs={{0,2},{1,3},{4,6},{5,7},{8,10},{9,11},{12,14},{13,15},{2,0},{3,1},... | collective-permute-start | bytes 110600 | tf_op jit(solution)/shard_map/ppermute | solution.py:235
  22.8 1.3 %collective-permute-start.5 = (bf16[16,16,128]{2,1,0:T(8,128)(2,1)S(1)}, bf16[16,16,128]{2,1,0:T(8,128)(2,1)S(1)}, u32[]{:S(2)}, u32[]{:S(2)}) collective-permute-start(bf16[16,16,128]{2,1,0:T(8,128)(2,1)S(1)} %backward.1.refs_2_), channel_id=1, source_target_pairs={{0,1},{1,0},{2,3},{3,2},{4,5},{5,4},{6,7},{7,6},{8,9},{9,8},{10,11... | collective-permute-start | bytes 196616 | tf_op jit(solution)/shard_map/ppermute | solution.py:265

commit v5 on v4

--- a/solution.py
+++ b/solution.py
@@ -59,21 +59,17 @@
     outs = []
     for group in groups(slots):
         left = jnp.concatenate([flat[cols[0, 0, n]] for n in group], axis=0)
-        right = jnp.concatenate([tiles[0, 0, n] for n in group], axis=0)
-        out = lax.dot_general(left, right, (((1,), (1,)), ((), ())), preferred_element_type=F32)
-        outs += [
-            (n, out[i * nprobe : (i + 1) * nprobe, i * width : (i + 1) * width])
-            for i, n in enumerate(group)
-        ]
-    for n, out in outs:
-        acc[jnp.where(n < live, rows[0, 0, n], nrows)] += out
+        right = jnp.concatenate([tiles[0, 0, n].T for n in group], axis=1)
+        out = jnp.dot(left, right, preferred_element_type=F32)
+        for i, n in enumerate(group):
+            acc[jnp.where(n < live, rows[0, 0, n], nrows)] += out[i * nprobe : (i + 1) * nprobe, i * width : (i + 1) * width]
     value = acc[0:nrows]
     total[...] = value
     sent[...] = value.astype(BF16)
 
 
 def backward_kernel(
-    counts, rows, cols, tiles, total, got, weight, probes, stiff, paired, odd, part, weighted, acc
+    counts, rows, cols, tiles, total, got, weight, probes, stiff, odd, part, weighted, acc
 ):
     slots, width = tiles.shape[2], tiles.shape[3]
     nrows, nprobe = total.shape[0], total.shape[1]
@@ -94,26 +90,22 @@
         ]
     for n, out in outs:
         acc[jnp.where(n < live, cols[0, 0, n], ncols)] += out
-    each = paired.shape[0] - 1
+    each = odd.shape[0] - 1
     slabs = ncols // each
-    mine = lax.axis_index("ray") == 1
     even, cell = even_cell(), lax.axis_index("cell")
     inner = jnp.logical_and(cell > 0, cell < lax.axis_size("cell") - 1)
-    for s, near in (
-        (0, jnp.where(even, odd[...], paired[...]).astype(F32)),
-        (slabs - 1, jnp.where(even, paired[...], odd[...]).astype(F32)),
-    ):
-        there = jnp.logical_or(inner, even if s else jnp.logical_not(even))
-        near = jnp.where(there, near, 0.0)
+    mine = lax.axis_index("ray") == 1
+    for s, here in ((0, even), (slabs - 1, jnp.logical_not(even))):
         for j in range(each):
             row = j * slabs + s
-            scale = 0.5 * (stiff[row : row + 1, :] + near[each, j : j + 1, :])
-            term = scale * (probes[rows_of(probes, s, j, slabs, ncols), :] - near[j])
-            acc[s * each + j] += jnp.where(mine, term, 0.0)
+            scale = 0.5 * (stiff[row : row + 1, :] + jnp.where(inner, odd[each, j : j + 1, :].astype(F32), 0.0))
+            near = jnp.where(inner, odd[j].astype(F32), 0.0)
+            term = scale * (probes[rows_of(probes, s, j, slabs, ncols), :] - near)
+            acc[s * each + j] += jnp.where(jnp.logical_and(mine, here), term, 0.0)
     part[...] = acc[0:ncols].astype(BF16)
 
 
-def smooth_kernel(probes, stiff, smooth, each):
+def smooth_kernel(probes, stiff, paired, smooth, each):
     ncols, nprobe, width = smooth.shape
     slabs = ncols // each
     lane = lax.broadcasted_iota(I32, (1, width), 1)
@@ -151,6 +143,12 @@
             for near_s, near_p in zip(neighbours(stiff_at, s, j), neighbours(probe_at, s, j)):
                 term = term + 0.5 * (here_s + near_s) * (here_p - near_p)
             smooth[s * each + j] = term
+    even = even_cell()
+    for s, here in ((0, jnp.logical_not(even)), (slabs - 1, even)):
+        for j in range(each):
+            scale = 0.5 * (stiff_at(s, j) + paired[each, j : j + 1, :].astype(F32))
+            term = scale * (probe_at(s, j) - paired[j].astype(F32))
+            smooth[s * each + j] += jnp.where(here, term, 0.0)
 
 
 def combine_kernel(probes, smooth, mine, other, applied, diag, each):
@@ -241,17 +239,16 @@
     for i, turn in enumerate(turns):
         pairs = [(c * nray + r, (c ^ turn[r]) * nray + r) for c in range(ncell) for r in range(nray)]
         got = lax.ppermute(sent, ("cell", "ray"), pairs)
-        if i == 0:
-            got, odd = lax.optimization_barrier((got, odd))
         if i < len(turns) - 1:
             total = total + got.astype(F32)
             sent = total.astype(BF16)
-    got, paired = lax.optimization_barrier((got, paired))
+            if i == 0:
+                sent, odd = lax.optimization_barrier((sent, odd))
 
     part = pl.pallas_call(
         backward_kernel,
         out_shape=pltpu.VMEM((ncols, nprobe, width), BF16),
-        in_specs=[SMEM] * 3 + [VMEM] * 8,
+        in_specs=[SMEM] * 3 + [VMEM] * 7,
         out_specs=VMEM,
         scratch_shapes=[
             pltpu.VMEM((nrows, nprobe, width), BF16),
@@ -260,18 +257,19 @@
         compiler_params=params,
         cost_estimate=products,
         name="backward",
-    )(counts, rows, cols, blocks, total, got, ray_weight.reshape(nrows, width), grid, stiff, paired, odd)
-
+    )(counts, rows, cols, blocks, total, got, ray_weight.reshape(nrows, width), grid, stiff, odd)
+
+    part, paired = lax.optimization_barrier((part, paired))
     other = lax.ppermute(part, "ray", [(0, 1), (1, 0)])
 
     smooth = pl.pallas_call(
         lambda *refs: smooth_kernel(*refs, each=each),
         out_shape=pltpu.VMEM((ncols, nprobe, width), F32),
-        in_specs=[VMEM] * 2,
+        in_specs=[VMEM] * 3,
         out_specs=VMEM,
         compiler_params=params,
         name="smooth",
-    )(grid, stiff)
+    )(grid, stiff, paired)
 
     applied, diag = pl.pallas_call(
         lambda *refs: combine_kernel(*refs, each=each),

time: 25.1 us -> 24.7 us (0.984)
  waiting for transfers between devices: 8.4 us -> 7.72 us
  starting transfers between devices: 10.7 us -> 11.1 us
    ppermute x2, waiting for transfers between devices: 2.45 us -> 0.01 us  [swap(): lax.ppermute(value, ('cell', 'ray'), ends + [(j, i) for i, j in ends])]
    ppermute x3, waiting for transfers between devices: 5.23 us -> 7.18 us  [local(): got = lax.ppermute(sent, ('cell', 'ray'), pairs)]
    ppermute x1, starting transfers between devices: 0.23 us -> 0.71 us  [local(): other = lax.ppermute(part, 'ray', [(0, 1), (1, 0)])]
  transfers between devices with their start and end apart: 6 -> 6, of which waited for: 4 -> 4; matrix products, arithmetic and copies ran while one was open for 0% -> 0% of each run, Pallas kernels for 1% -> 5%
where the time goes in v5:
time: 24.7 us; the launch traced here: 24.5 us
  starting transfers between devices  11.1 us (45%)
  waiting for transfers between devices  7.72 us (31%)
  Pallas kernels  4.07 us (16%)
  between operations  1.52 us (6%)
    ppermute x3, starting transfers between devices, local(): got = lax.ppermute(sent, ('cell', 'ray'), pairs)  8.3 us
    ppermute x3, waiting for transfers between devices, local(): got = lax.ppermute(sent, ('cell', 'ray'), pairs)  7.18 us
    ppermute x2, starting transfers between devices, swap(): lax.ppermute(value, ('cell', 'ray'), ends + [(j, i) for i, j in ends])  2.12 us
    pallas_call x1, Pallas kernels, local(): pl.pallas_call(prepare_kernel, out_shape=(pltpu.VMEM((ncols, nprobe, widt...  1.17 us
    pallas_call x1, Pallas kernels, local(): pl.pallas_call(forward_kernel, out_shape=(pltpu.VMEM((nrows, nprobe, widt...  1.04 us
    pallas_call x1, Pallas kernels, local(): pl.pallas_call(lambda *refs: combine_kernel(*refs, each=each), out_shape=...  0.75 us
    pallas_call x1, Pallas kernels, local(): pl.pallas_call(backward_kernel, out_shape=pltpu.VMEM((ncols, nprobe, widt...  0.75 us
    ppermute x1, starting transfers between devices, local(): other = lax.ppermute(part, 'ray', [(0, 1), (1, 0)])  0.71 us
  transfers between devices with their start and end apart: 6, of which 4 were waited for; matrix products, arithmetic and copies ran while one was open for 0% of the time, Pallas kernels for 5%

profile of v5, /device:TPU:0, one launch (start us, length us, event | category | flops | bytes accessed | tf_op | source)
XLA Modules:
  0.0 24.5 jit_solution(12623295506157738203)
XLA Ops:
  0.6 0.0 copy-start
  1.4 1.2 %prepare.1 = (bf16[16,16,128]{2,1,0:T(8,128)(2,1)S(1)}, bf16[9,16,128]{2,1,0:T(8,128)(2,1)S(1)}, bf16[9,16,128]{2,1,0:T(8,128)(2,1)S(1)}, f32[256,128]{1,0:T(8,1...) custom-call(s32[1,1,96]{2,1,0:T(1,128)} %rows_in.1, s32[1,1,96]{2,1,0:T(1,128)} %cols_in.1, ...), custom_call_target="tpu_custom_call" | custom-call | flops 1200000000 | bytes 1000 | tf_op jit(solution)/shard_map/prepare/pallas_call | solution.py:198
  2.6 0.0 copy-start.1
  2.6 0.0 copy-done
  2.6 1.0 %forward.1 = (f32[32,16,128]{2,1,0:T(8,128)S(1)}, bf16[32,16,128]{2,1,0:T(8,128)(2,1)S(1)}) custom-call(s32[1,1]{1,0:T(1,128)S(6)} %copy.13.counts, s32[1,1,96]{2,1,0:T(1,128)S(4)} %get-tuple-element.19.rows, s32[1,1,96]{2,1,0:T(1,128)S(4)} %get-tuple-element.20.cols, bf16[1,1,96,128,128]{4,3,2,1,0:T(8,128)(2,1)S(1)} %copy-done, ...), custom_call_target="tpu_custom_call" | custom-call | flops 50331648 | bytes 3145728 | tf_op jit(solution)/shard_map/forward/pallas_call | solution.py:217
  3.7 3.0 %collective-permute-start = (bf16[32,16,128]{2,1,0:T(8,128)(2,1)S(1)}, bf16[32,16,128]{2,1,0:T(8,128)(2,1)S(1)}, u32[]{:S(2)}, u32[]{:S(2)}) collective-permute-start(bf16[32,16,128]{2,1,0:T(8,128)(2,1)S(1)} %get-tuple-element.23), channel_id=1, source_target_pairs={{0,2},{1,9},{2,0},{3,11},{4,6},{5,13},{6,4},{7,15},{8,10},{9,1},{1... | collective-permute-start | bytes 393224 | tf_op jit(solution)/shard_map/ppermute | solution.py:241
  6.7 0.7 %collective-permute-start.1 = (bf16[9,16,128]{2,1,0:T(8,128)(2,1)S(1)}, bf16[9,16,128]{2,1,0:T(8,128)(2,1)S(1)}, u32[]{:S(2)}, u32[]{:S(2)}) collective-permute-start(bf16[9,16,128]{2,1,0:T(8,128)(2,1)S(1)} %get-tuple-element.24), channel_id=1, source_target_pairs={{3,5},{7,9},{11,13},{5,3},{9,7},{13,11},{19,21},{23,25},{27,29},{2... | collective-permute-start | bytes 110600 | tf_op jit(solution)/shard_map/ppermute | solution.py:233
  7.4 2.3 %collective-permute-done = bf16[32,16,128]{2,1,0:T(8,128)(2,1)S(1)} collective-permute-done((bf16[32,16,128]{2,1,0:T(8,128)(2,1)S(1)}, bf16[32,16,128]{2,1,0:T(8,128)(2,1)S(1)}, u32[]{:S(2)}, u32[]{:S(2)}) %collective-permute-start) | collective-permute-done | bytes 131104 | tf_op jit(solution)/shard_map/ppermute | solution.py:241
  9.7 0.0 collective-permute-done.1.odd
  9.7 2.2 %collective-permute-start.2 = (bf16[32,16,128]{2,1,0:T(8,128)(2,1)S(1)}, bf16[32,16,128]{2,1,0:T(8,128)(2,1)S(1)}, u32[]{:S(2)}, u32[]{:S(2)}) collective-permute-start(bf16[32,16,128]{2,1,0:T(8,128)(2,1)S(1)} %fusion), channel_id=1, source_target_pairs={{0,4},{1,3},{2,6},{3,1},{4,0},{5,7},{6,2},{7,5},{8,12},{9,11},{10,... | collective-permute-start | bytes 393224 | tf_op jit(solution)/shard_map/ppermute | solution.py:241
  11.9 2.9 %collective-permute-done.2 = bf16[32,16,128]{2,1,0:T(8,128)(2,1)S(1)} collective-permute-done((bf16[32,16,128]{2,1,0:T(8,128)(2,1)S(1)}, bf16[32,16,128]{2,1,0:T(8,128)(2,1)S(1)}, u32[]{:S(2)}, u32[]{:S(2)}) %collective-permute-start.2) | collective-permute-done | bytes 131104 | tf_op jit(solution)/shard_map/ppermute | solution.py:241
  14.9 3.1 %collective-permute-start.3 = (bf16[32,16,128]{2,1,0:T(8,128)(2,1)S(1)}, bf16[32,16,128]{2,1,0:T(8,128)(2,1)S(1)}, u32[]{:S(2)}, u32[]{:S(2)}) collective-permute-start(bf16[32,16,128]{2,1,0:T(8,128)(2,1)S(1)} %get-tuple-element.32), channel_id=1, source_target_pairs={{0,8},{1,5},{2,10},{3,7},{4,12},{5,1},{6,14},{7,3},{8,0},{9,13},{1... | collective-permute-start | bytes 393224 | tf_op jit(solution)/shard_map/ppermute | solution.py:241
  18.0 1.5 %collective-permute-start.4 = (bf16[9,16,128]{2,1,0:T(8,128)(2,1)S(1)}, bf16[9,16,128]{2,1,0:T(8,128)(2,1)S(1)}, u32[]{:S(2)}, u32[]{:S(2)}) collective-permute-start(bf16[9,16,128]{2,1,0:T(8,128)(2,1)S(1)} %get-tuple-element.27), channel_id=1, source_target_pairs={{0,2},{1,3},{4,6},{5,7},{8,10},{9,11},{12,14},{13,15},{2,0},{3,1},... | collective-permute-start | bytes 110600 | tf_op jit(solution)/shard_map/ppermute | solution.py:233
  19.4 1.9 %collective-permute-done.3.got = bf16[32,16,128]{2,1,0:T(8,128)(2,1)S(1)} collective-permute-done((bf16[32,16,128]{2,1,0:T(8,128)(2,1)S(1)}, bf16[32,16,128]{2,1,0:T(8,128)(2,1)S(1)}, u32[]{:S(2)}, u32[]{:S(2)}) %collective-permute-start.3) | collective-permute-done | bytes 131104 | tf_op jit(solution)/shard_map/ppermute | solution.py:241
  21.4 0.0 copy-done.1
  21.4 0.7 %backward.1.refs_2_ = bf16[16,16,128]{2,1,0:T(8,128)(2,1)S(1)} custom-call(s32[1,1]{1,0:T(1,128)S(6)} %copy.13.counts, s32[1,1,96]{2,1,0:T(1,128)S(4)} %get-tuple-element.19.rows, s32[1,1,96]{2,1,0:T(1,128)S(4)} %get-tuple-element.20.cols, bf16[1,1,96,128,128]{4,3,2,1,0:T(8,128)(2,1)S(1)} %copy-done, f32[32,16,128]{2,1,0:T(8,128)S(1)} %get-tuple-element.33.total, ...), custom_call_target="tpu_custom_call" | custom-call | flops 50331648 | bytes 3145728 | tf_op jit(solution)/shard_map/backward/pallas_call | solution.py:248
  22.1 0.0 collective-permute-done.4.refs_2_
  22.2 0.7 %collective-permute-start.5 = (bf16[16,16,128]{2,1,0:T(8,128)(2,1)S(1)}, bf16[16,16,128]{2,1,0:T(8,128)(2,1)S(1)}, u32[]{:S(2)}, u32[]{:S(2)}) collective-permute-start(bf16[16,16,128]{2,1,0:T(8,128)(2,1)S(1)} %backward.1.refs_2_), channel_id=1, source_target_pairs={{0,1},{1,0},{2,3},{3,2},{4,5},{5,4},{6,7},{7,6},{8,9},{9,8},{10,11... | collective-permute-start | bytes 196616 | tf_op jit(solution)/shard_map/ppermute | solution.py:263
  22.9 0.4 %smooth.1.refs_1_ = f32[16,16,128]{2,1,0:T(8,128)S(1)} custom-call(f32[256,128]{1,0:T(8,128)S(1)} %get-tuple-element.17.probes.refs_0_, f32[16,128]{1,0:T(8,128)S(1)} %get-tuple-element.18.stiff.refs_1_, bf16[9,16,128]{2,1,0:T(8,128)(2,1)S(1)} %collective-permute-done.4.refs_2_), custom_call_target="tpu_custom_call" | custom-call | tf_op jit(solution)/shard_map/smooth/pallas_call | solution.py:265
  23.2 0.5 %collective-permute-done.5.refs_3_ = bf16[16,16,128]{2,1,0:T(8,128)(2,1)S(1)} collective-permute-done((bf16[16,16,128]{2,1,0:T(8,128)(2,1)S(1)}, bf16[16,16,128]{2,1,0:T(8,128)(2,1)S(1)}, u32[]{:S(2)}, u32[]{:S(2)}) %collective-permute-start.5) | collective-permute-done | bytes 65568 | tf_op jit(solution)/shard_map/ppermute | solution.py:263
  23.8 0.7 %combine.1 = (f32[256,128]{1,0:T(8,128)}, f32[16,128]{1,0:T(8,128)}) custom-call(f32[256,128]{1,0:T(8,128)S(1)} %get-tuple-element.17.probes.refs_0_, f32[16,16,128]{2,1,0:T(8,128)S(1)} %smooth.1.refs_1_, bf16[16,16,128]{2,1,0:T(8,128)(2,1)S(1)} %backward.1.refs_2_, bf16[16,16,128]{2,1,0:T(8,128)(2,1)S(1)} %collective-permute-done.5.refs_3_), custom_call_target="tpu_custom_call" | custom-call | tf_op jit(solution)/shard_map/combine/pallas_call | solution.py:274
  (2 shorter events, 0.1 us)
Async XLA Ops:
  0.6 2.0 %copy-start = (bf16[1,1,96,128,128]{4,3,2,1,0:T(8,128)(2,1)S(1)}, bf16[1,1,96,128,128]{4,3,2,1,0:T(8,128)(2,1)}, u32[]{:S(2)}) copy-start(bf16[1,1,96,128,128]{4,3,2,1,0:T(8,128)(2,1)} %tiles.3) | copy-start | bytes 9437188
  2.6 18.8 %copy-start.1 = (f32[4096]{0:T(1024)S(1)}, f32[4096]{0:T(1024)}, u32[]{:S(2)}) copy-start(f32[4096]{0:T(1024)} %param.11) | copy-start | bytes 49156
  3.7 6.0 %collective-permute-start = (bf16[32,16,128]{2,1,0:T(8,128)(2,1)S(1)}, bf16[32,16,128]{2,1,0:T(8,128)(2,1)S(1)}, u32[]{:S(2)}, u32[]{:S(2)}) collective-permute-start(bf16[32,16,128]{2,1,0:T(8,128)(2,1)S(1)} %get-tuple-element.23), channel_id=1, source_target_pairs={{0,2},{1,9},{2,0},{3,11},{4,6},{5,13},{6,4},{7,15},{8,10},{9,1},{1... | collective-permute-start | bytes 393224 | tf_op jit(solution)/shard_map/ppermute | solution.py:241
  6.7 3.0 %collective-permute-start.1 = (bf16[9,16,128]{2,1,0:T(8,128)(2,1)S(1)}, bf16[9,16,128]{2,1,0:T(8,128)(2,1)S(1)}, u32[]{:S(2)}, u32[]{:S(2)}) collective-permute-start(bf16[9,16,128]{2,1,0:T(8,128)(2,1)S(1)} %get-tuple-element.24), channel_id=1, source_target_pairs={{3,5},{7,9},{11,13},{5,3},{9,7},{13,11},{19,21},{23,25},{27,29},{2... | collective-permute-start | bytes 110600 | tf_op jit(solution)/shard_map/ppermute | solution.py:233
  9.7 5.1 %collective-permute-start.2 = (bf16[32,16,128]{2,1,0:T(8,128)(2,1)S(1)}, bf16[32,16,128]{2,1,0:T(8,128)(2,1)S(1)}, u32[]{:S(2)}, u32[]{:S(2)}) collective-permute-start(bf16[32,16,128]{2,1,0:T(8,128)(2,1)S(1)} %fusion), channel_id=1, source_target_pairs={{0,4},{1,3},{2,6},{3,1},{4,0},{5,7},{6,2},{7,5},{8,12},{9,11},{10,... | collective-permute-start | bytes 393224 | tf_op jit(solution)/shard_map/ppermute | solution.py:241
  14.9 6.5 %collective-permute-start.3 = (bf16[32,16,128]{2,1,0:T(8,128)(2,1)S(1)}, bf16[32,16,128]{2,1,0:T(8,128)(2,1)S(1)}, u32[]{:S(2)}, u32[]{:S(2)}) collective-permute-start(bf16[32,16,128]{2,1,0:T(8,128)(2,1)S(1)} %get-tuple-element.32), channel_id=1, source_target_pairs={{0,8},{1,5},{2,10},{3,7},{4,12},{5,1},{6,14},{7,3},{8,0},{9,13},{1... | collective-permute-start | bytes 393224 | tf_op jit(solution)/shard_map/ppermute | solution.py:241
  18.0 4.2 %collective-permute-start.4 = (bf16[9,16,128]{2,1,0:T(8,128)(2,1)S(1)}, bf16[9,16,128]{2,1,0:T(8,128)(2,1)S(1)}, u32[]{:S(2)}, u32[]{:S(2)}) collective-permute-start(bf16[9,16,128]{2,1,0:T(8,128)(2,1)S(1)} %get-tuple-element.27), channel_id=1, source_target_pairs={{0,2},{1,3},{4,6},{5,7},{8,10},{9,11},{12,14},{13,15},{2,0},{3,1},... | collective-permute-start | bytes 110600 | tf_op jit(solution)/shard_map/ppermute | solution.py:233
  22.2 1.6 %collective-permute-start.5 = (bf16[16,16,128]{2,1,0:T(8,128)(2,1)S(1)}, bf16[16,16,128]{2,1,0:T(8,128)(2,1)S(1)}, u32[]{:S(2)}, u32[]{:S(2)}) collective-permute-start(bf16[16,16,128]{2,1,0:T(8,128)(2,1)S(1)} %backward.1.refs_2_), channel_id=1, source_target_pairs={{0,1},{1,0},{2,3},{3,2},{4,5},{5,4},{6,7},{7,6},{8,9},{9,8},{10,11... | collective-permute-start | bytes 196616 | tf_op jit(solution)/shard_map/ppermute | solution.py:263

commit v6 on v5

--- a/solution.py
+++ b/solution.py
@@ -59,11 +59,16 @@
     outs = []
     for group in groups(slots):
         left = jnp.concatenate([flat[cols[0, 0, n]] for n in group], axis=0)
-        right = jnp.concatenate([tiles[0, 0, n].T for n in group], axis=1)
-        out = jnp.dot(left, right, preferred_element_type=F32)
+        if group[0] // 2 % 3 == 0:
+            right = jnp.concatenate([tiles[0, 0, n] for n in group], axis=0)
+            out = lax.dot_general(left, right, (((1,), (1,)), ((), ())), preferred_element_type=F32)
+        else:
+            right = jnp.concatenate([tiles[0, 0, n].T for n in group], axis=1)
+            out = jnp.dot(left, right, preferred_element_type=F32)
         for i, n in enumerate(group):
-            acc[jnp.where(n < live, rows[0, 0, n], nrows)] += out[i * nprobe : (i + 1) * nprobe, i * width : (i + 1) * width]
-    value = acc[0:nrows]
+            piece = out[i * nprobe : (i + 1) * nprobe, i * width : (i + 1) * width]
+            acc[i, jnp.where(n < live, rows[0, 0, n], nrows)] += piece
+    value = acc[0, 0:nrows] + acc[1, 0:nrows]
     total[...] = value
     sent[...] = value.astype(BF16)
 
@@ -89,7 +94,7 @@
             for i, n in enumerate(group)
         ]
     for n, out in outs:
-        acc[jnp.where(n < live, cols[0, 0, n], ncols)] += out
+        acc[n % 2, jnp.where(n < live, cols[0, 0, n], ncols)] += out
     each = odd.shape[0] - 1
     slabs = ncols // each
     even, cell = even_cell(), lax.axis_index("cell")
@@ -101,8 +106,8 @@
             scale = 0.5 * (stiff[row : row + 1, :] + jnp.where(inner, odd[each, j : j + 1, :].astype(F32), 0.0))
             near = jnp.where(inner, odd[j].astype(F32), 0.0)
             term = scale * (probes[rows_of(probes, s, j, slabs, ncols), :] - near)
-            acc[s * each + j] += jnp.where(jnp.logical_and(mine, here), term, 0.0)
-    part[...] = acc[0:ncols].astype(BF16)
+            acc[0, s * each + j] += jnp.where(jnp.logical_and(mine, here), term, 0.0)
+    part[...] = (acc[0, 0:ncols] + acc[1, 0:ncols]).astype(BF16)
 
 
 def smooth_kernel(probes, stiff, paired, smooth, each):
@@ -222,7 +227,7 @@
         ),
         in_specs=[SMEM] * 3 + [VMEM] * 2,
         out_specs=(VMEM,) * 2,
-        scratch_shapes=[pltpu.VMEM((nrows + 1, nprobe, width), F32)],
+        scratch_shapes=[pltpu.VMEM((2, nrows + 1, nprobe, width), F32)],
         compiler_params=params,
         cost_estimate=products,
         name="forward",
@@ -252,7 +257,7 @@
         out_specs=VMEM,
         scratch_shapes=[
             pltpu.VMEM((nrows, nprobe, width), BF16),
-            pltpu.VMEM((ncols + 1, nprobe, width), F32),
+            pltpu.VMEM((2, ncols + 1, nprobe, width), F32),
         ],
         compiler_params=params,
         cost_estimate=products,

time: 24.7 us -> 24.4 us (0.988)
  Pallas kernels: 4.07 us -> 3.77 us
    pallas_call x1, Pallas kernels: 1.04 us -> 0.77 us  [local(): pl.pallas_call(forward_kernel, out_shape=(pltpu.VMEM((nrows, nprobe, widt...]
  transfers between devices with their start and end apart: 6 -> 6, of which waited for: 4 -> 4; matrix products, arithmetic and copies ran while one was open for 0% -> 0% of each run, Pallas kernels for 5% -> 4%
where the time goes in v6:
time: 24.4 us; the launch traced here: 24.2 us
  starting transfers between devices  11.1 us (45%)
  waiting for transfers between devices  7.7 us (32%)
  Pallas kernels  3.77 us (15%)
  between operations  1.52 us (6%)
    ppermute x3, starting transfers between devices, local(): got = lax.ppermute(sent, ('cell', 'ray'), pairs)  8.27 us
    ppermute x3, waiting for transfers between devices, local(): got = lax.ppermute(sent, ('cell', 'ray'), pairs)  7.16 us
    ppermute x2, starting transfers between devices, swap(): lax.ppermute(value, ('cell', 'ray'), ends + [(j, i) for i, j in ends])  2.14 us
    pallas_call x1, Pallas kernels, local(): pl.pallas_call(prepare_kernel, out_shape=(pltpu.VMEM((ncols, nprobe, widt...  1.17 us
    pallas_call x1, Pallas kernels, local(): pl.pallas_call(forward_kernel, out_shape=(pltpu.VMEM((nrows, nprobe, widt...  0.77 us
    pallas_call x1, Pallas kernels, local(): pl.pallas_call(lambda *refs: combine_kernel(*refs, each=each), out_shape=...  0.75 us
    ppermute x1, starting transfers between devices, local(): other = lax.ppermute(part, 'ray', [(0, 1), (1, 0)])  0.72 us
    pallas_call x1, Pallas kernels, local(): pl.pallas_call(backward_kernel, out_shape=pltpu.VMEM((ncols, nprobe, widt...  0.72 us
  transfers between devices with their start and end apart: 6, of which 4 were waited for; matrix products, arithmetic and copies ran while one was open for 0% of the time, Pallas kernels for 4%

profile of v6, /device:TPU:0, one launch (start us, length us, event | category | flops | bytes accessed | tf_op | source)
XLA Modules:
  0.0 24.2 jit_solution(13295987435214494244)
XLA Ops:
  0.6 0.0 copy-start
  1.4 1.2 %prepare.1 = (bf16[16,16,128]{2,1,0:T(8,128)(2,1)S(1)}, bf16[9,16,128]{2,1,0:T(8,128)(2,1)S(1)}, bf16[9,16,128]{2,1,0:T(8,128)(2,1)S(1)}, f32[256,128]{1,0:T(8,1...) custom-call(s32[1,1,96]{2,1,0:T(1,128)} %rows_in.1, s32[1,1,96]{2,1,0:T(1,128)} %cols_in.1, ...), custom_call_target="tpu_custom_call" | custom-call | flops 1200000000 | bytes 1000 | tf_op jit(solution)/shard_map/prepare/pallas_call | solution.py:203
  2.6 0.0 copy-start.1
  2.6 0.0 copy-done
  2.6 0.8 %forward.1 = (f32[32,16,128]{2,1,0:T(8,128)S(1)}, bf16[32,16,128]{2,1,0:T(8,128)(2,1)S(1)}) custom-call(s32[1,1]{1,0:T(1,128)S(6)} %copy.13.counts, s32[1,1,96]{2,1,0:T(1,128)S(4)} %get-tuple-element.19.rows, s32[1,1,96]{2,1,0:T(1,128)S(4)} %get-tuple-element.20.cols, bf16[1,1,96,128,128]{4,3,2,1,0:T(8,128)(2,1)S(1)} %copy-done, ...), custom_call_target="tpu_custom_call" | custom-call | flops 50331648 | bytes 3145728 | tf_op jit(solution)/shard_map/forward/pallas_call | solution.py:222
  3.4 3.0 %collective-permute-start = (bf16[32,16,128]{2,1,0:T(8,128)(2,1)S(1)}, bf16[32,16,128]{2,1,0:T(8,128)(2,1)S(1)}, u32[]{:S(2)}, u32[]{:S(2)}) collective-permute-start(bf16[32,16,128]{2,1,0:T(8,128)(2,1)S(1)} %get-tuple-element.23), channel_id=1, source_target_pairs={{0,2},{1,9},{2,0},{3,11},{4,6},{5,13},{6,4},{7,15},{8,10},{9,1},{1... | collective-permute-start | bytes 393224 | tf_op jit(solution)/shard_map/ppermute | solution.py:246
  6.4 0.7 %collective-permute-start.1 = (bf16[9,16,128]{2,1,0:T(8,128)(2,1)S(1)}, bf16[9,16,128]{2,1,0:T(8,128)(2,1)S(1)}, u32[]{:S(2)}, u32[]{:S(2)}) collective-permute-start(bf16[9,16,128]{2,1,0:T(8,128)(2,1)S(1)} %get-tuple-element.24), channel_id=1, source_target_pairs={{3,5},{7,9},{11,13},{5,3},{9,7},{13,11},{19,21},{23,25},{27,29},{2... | collective-permute-start | bytes 110600 | tf_op jit(solution)/shard_map/ppermute | solution.py:238
  7.1 2.3 %collective-permute-done = bf16[32,16,128]{2,1,0:T(8,128)(2,1)S(1)} collective-permute-done((bf16[32,16,128]{2,1,0:T(8,128)(2,1)S(1)}, bf16[32,16,128]{2,1,0:T(8,128)(2,1)S(1)}, u32[]{:S(2)}, u32[]{:S(2)}) %collective-permute-start) | collective-permute-done | bytes 131104 | tf_op jit(solution)/shard_map/ppermute | solution.py:246
  9.4 0.0 collective-permute-done.1.odd
  9.4 2.2 %collective-permute-start.2 = (bf16[32,16,128]{2,1,0:T(8,128)(2,1)S(1)}, bf16[32,16,128]{2,1,0:T(8,128)(2,1)S(1)}, u32[]{:S(2)}, u32[]{:S(2)}) collective-permute-start(bf16[32,16,128]{2,1,0:T(8,128)(2,1)S(1)} %fusion), channel_id=1, source_target_pairs={{0,4},{1,3},{2,6},{3,1},{4,0},{5,7},{6,2},{7,5},{8,12},{9,11},{10,... | collective-permute-start | bytes 393224 | tf_op jit(solution)/shard_map/ppermute | solution.py:246
  11.6 2.9 %collective-permute-done.2 = bf16[32,16,128]{2,1,0:T(8,128)(2,1)S(1)} collective-permute-done((bf16[32,16,128]{2,1,0:T(8,128)(2,1)S(1)}, bf16[32,16,128]{2,1,0:T(8,128)(2,1)S(1)}, u32[]{:S(2)}, u32[]{:S(2)}) %collective-permute-start.2) | collective-permute-done | bytes 131104 | tf_op jit(solution)/shard_map/ppermute | solution.py:246
  14.6 3.1 %collective-permute-start.3 = (bf16[32,16,128]{2,1,0:T(8,128)(2,1)S(1)}, bf16[32,16,128]{2,1,0:T(8,128)(2,1)S(1)}, u32[]{:S(2)}, u32[]{:S(2)}) collective-permute-start(bf16[32,16,128]{2,1,0:T(8,128)(2,1)S(1)} %get-tuple-element.32), channel_id=1, source_target_pairs={{0,8},{1,5},{2,10},{3,7},{4,12},{5,1},{6,14},{7,3},{8,0},{9,13},{1... | collective-permute-start | bytes 393224 | tf_op jit(solution)/shard_map/ppermute | solution.py:246
  17.7 1.5 %collective-permute-start.4 = (bf16[9,16,128]{2,1,0:T(8,128)(2,1)S(1)}, bf16[9,16,128]{2,1,0:T(8,128)(2,1)S(1)}, u32[]{:S(2)}, u32[]{:S(2)}) collective-permute-start(bf16[9,16,128]{2,1,0:T(8,128)(2,1)S(1)} %get-tuple-element.27), channel_id=1, source_target_pairs={{0,2},{1,3},{4,6},{5,7},{8,10},{9,11},{12,14},{13,15},{2,0},{3,1},... | collective-permute-start | bytes 110600 | tf_op jit(solution)/shard_map/ppermute | solution.py:238
  19.2 1.9 %collective-permute-done.3.got = bf16[32,16,128]{2,1,0:T(8,128)(2,1)S(1)} collective-permute-done((bf16[32,16,128]{2,1,0:T(8,128)(2,1)S(1)}, bf16[32,16,128]{2,1,0:T(8,128)(2,1)S(1)}, u32[]{:S(2)}, u32[]{:S(2)}) %collective-permute-start.3) | collective-permute-done | bytes 131104 | tf_op jit(solution)/shard_map/ppermute | solution.py:246
  21.1 0.0 copy-done.1
  21.1 0.7 %backward.1.refs_2_ = bf16[16,16,128]{2,1,0:T(8,128)(2,1)S(1)} custom-call(s32[1,1]{1,0:T(1,128)S(6)} %copy.13.counts, s32[1,1,96]{2,1,0:T(1,128)S(4)} %get-tuple-element.19.rows, s32[1,1,96]{2,1,0:T(1,128)S(4)} %get-tuple-element.20.cols, bf16[1,1,96,128,128]{4,3,2,1,0:T(8,128)(2,1)S(1)} %copy-done, f32[32,16,128]{2,1,0:T(8,128)S(1)} %get-tuple-element.33.total, ...), custom_call_target="tpu_custom_call" | custom-call | flops 50331648 | bytes 3145728 | tf_op jit(solution)/shard_map/backward/pallas_call | solution.py:253
  21.8 0.0 collective-permute-done.4.refs_2_
  21.8 0.7 %collective-permute-start.5 = (bf16[16,16,128]{2,1,0:T(8,128)(2,1)S(1)}, bf16[16,16,128]{2,1,0:T(8,128)(2,1)S(1)}, u32[]{:S(2)}, u32[]{:S(2)}) collective-permute-start(bf16[16,16,128]{2,1,0:T(8,128)(2,1)S(1)} %backward.1.refs_2_), channel_id=1, source_target_pairs={{0,1},{1,0},{2,3},{3,2},{4,5},{5,4},{6,7},{7,6},{8,9},{9,8},{10,11... | collective-permute-start | bytes 196616 | tf_op jit(solution)/shard_map/ppermute | solution.py:268
  22.6 0.4 %smooth.1.refs_1_ = f32[16,16,128]{2,1,0:T(8,128)S(1)} custom-call(f32[256,128]{1,0:T(8,128)S(1)} %get-tuple-element.17.probes.refs_0_, f32[16,128]{1,0:T(8,128)S(1)} %get-tuple-element.18.stiff.refs_1_, bf16[9,16,128]{2,1,0:T(8,128)(2,1)S(1)} %collective-permute-done.4.refs_2_), custom_call_target="tpu_custom_call" | custom-call | tf_op jit(solution)/shard_map/smooth/pallas_call | solution.py:270
  22.9 0.5 %collective-permute-done.5.refs_3_ = bf16[16,16,128]{2,1,0:T(8,128)(2,1)S(1)} collective-permute-done((bf16[16,16,128]{2,1,0:T(8,128)(2,1)S(1)}, bf16[16,16,128]{2,1,0:T(8,128)(2,1)S(1)}, u32[]{:S(2)}, u32[]{:S(2)}) %collective-permute-start.5) | collective-permute-done | bytes 65568 | tf_op jit(solution)/shard_map/ppermute | solution.py:268
  23.5 0.7 %combine.1 = (f32[256,128]{1,0:T(8,128)}, f32[16,128]{1,0:T(8,128)}) custom-call(f32[256,128]{1,0:T(8,128)S(1)} %get-tuple-element.17.probes.refs_0_, f32[16,16,128]{2,1,0:T(8,128)S(1)} %smooth.1.refs_1_, bf16[16,16,128]{2,1,0:T(8,128)(2,1)S(1)} %backward.1.refs_2_, bf16[16,16,128]{2,1,0:T(8,128)(2,1)S(1)} %collective-permute-done.5.refs_3_), custom_call_target="tpu_custom_call" | custom-call | tf_op jit(solution)/shard_map/combine/pallas_call | solution.py:279
  (2 shorter events, 0.1 us)
Async XLA Ops:
  0.6 2.0 %copy-start = (bf16[1,1,96,128,128]{4,3,2,1,0:T(8,128)(2,1)S(1)}, bf16[1,1,96,128,128]{4,3,2,1,0:T(8,128)(2,1)}, u32[]{:S(2)}) copy-start(bf16[1,1,96,128,128]{4,3,2,1,0:T(8,128)(2,1)} %tiles.3) | copy-start | bytes 9437188
  2.6 18.5 %copy-start.1 = (f32[4096]{0:T(1024)S(1)}, f32[4096]{0:T(1024)}, u32[]{:S(2)}) copy-start(f32[4096]{0:T(1024)} %param.11) | copy-start | bytes 49156
  3.4 5.9 %collective-permute-start = (bf16[32,16,128]{2,1,0:T(8,128)(2,1)S(1)}, bf16[32,16,128]{2,1,0:T(8,128)(2,1)S(1)}, u32[]{:S(2)}, u32[]{:S(2)}) collective-permute-start(bf16[32,16,128]{2,1,0:T(8,128)(2,1)S(1)} %get-tuple-element.23), channel_id=1, source_target_pairs={{0,2},{1,9},{2,0},{3,11},{4,6},{5,13},{6,4},{7,15},{8,10},{9,1},{1... | collective-permute-start | bytes 393224 | tf_op jit(solution)/shard_map/ppermute | solution.py:246
  6.4 3.0 %collective-permute-start.1 = (bf16[9,16,128]{2,1,0:T(8,128)(2,1)S(1)}, bf16[9,16,128]{2,1,0:T(8,128)(2,1)S(1)}, u32[]{:S(2)}, u32[]{:S(2)}) collective-permute-start(bf16[9,16,128]{2,1,0:T(8,128)(2,1)S(1)} %get-tuple-element.24), channel_id=1, source_target_pairs={{3,5},{7,9},{11,13},{5,3},{9,7},{13,11},{19,21},{23,25},{27,29},{2... | collective-permute-start | bytes 110600 | tf_op jit(solution)/shard_map/ppermute | solution.py:238
  9.4 5.1 %collective-permute-start.2 = (bf16[32,16,128]{2,1,0:T(8,128)(2,1)S(1)}, bf16[32,16,128]{2,1,0:T(8,128)(2,1)S(1)}, u32[]{:S(2)}, u32[]{:S(2)}) collective-permute-start(bf16[32,16,128]{2,1,0:T(8,128)(2,1)S(1)} %fusion), channel_id=1, source_target_pairs={{0,4},{1,3},{2,6},{3,1},{4,0},{5,7},{6,2},{7,5},{8,12},{9,11},{10,... | collective-permute-start | bytes 393224 | tf_op jit(solution)/shard_map/ppermute | solution.py:246
  14.6 6.5 %collective-permute-start.3 = (bf16[32,16,128]{2,1,0:T(8,128)(2,1)S(1)}, bf16[32,16,128]{2,1,0:T(8,128)(2,1)S(1)}, u32[]{:S(2)}, u32[]{:S(2)}) collective-permute-start(bf16[32,16,128]{2,1,0:T(8,128)(2,1)S(1)} %get-tuple-element.32), channel_id=1, source_target_pairs={{0,8},{1,5},{2,10},{3,7},{4,12},{5,1},{6,14},{7,3},{8,0},{9,13},{1... | collective-permute-start | bytes 393224 | tf_op jit(solution)/shard_map/ppermute | solution.py:246
  17.7 4.1 %collective-permute-start.4 = (bf16[9,16,128]{2,1,0:T(8,128)(2,1)S(1)}, bf16[9,16,128]{2,1,0:T(8,128)(2,1)S(1)}, u32[]{:S(2)}, u32[]{:S(2)}) collective-permute-start(bf16[9,16,128]{2,1,0:T(8,128)(2,1)S(1)} %get-tuple-element.27), channel_id=1, source_target_pairs={{0,2},{1,3},{4,6},{5,7},{8,10},{9,11},{12,14},{13,15},{2,0},{3,1},... | collective-permute-start | bytes 110600 | tf_op jit(solution)/shard_map/ppermute | solution.py:238
  21.8 1.6 %collective-permute-start.5 = (bf16[16,16,128]{2,1,0:T(8,128)(2,1)S(1)}, bf16[16,16,128]{2,1,0:T(8,128)(2,1)S(1)}, u32[]{:S(2)}, u32[]{:S(2)}) collective-permute-start(bf16[16,16,128]{2,1,0:T(8,128)(2,1)S(1)} %backward.1.refs_2_), channel_id=1, source_target_pairs={{0,1},{1,0},{2,3},{3,2},{4,5},{5,4},{6,7},{7,6},{8,9},{9,8},{10,11... | collective-permute-start | bytes 196616 | tf_op jit(solution)/shard_map/ppermute | solution.py:268

commit v7 on v6

--- a/solution.py
+++ b/solution.py
@@ -22,14 +22,14 @@
     return [tuple(range(n, min(n + 2, slots))) for n in range(0, slots, 2)]
 
 
-def even_cell():
-    return lax.rem(lax.axis_index("cell"), 2) == 0
+def looks_up():
+    return lax.rem(lax.axis_index("cell") + lax.axis_index("ray"), 2) == 0
 
 
 def prepare_kernel(
-    rows_in, cols_in, probes_in, stiff_in, flat, paired, odd, probes, stiff, rows, cols, sems
+    rows_in, cols_in, probes_in, stiff_in, flat, edge, probes, stiff, rows, cols, sems
 ):
-    ncols, slabs = flat.shape[0], stiff.shape[0] // (paired.shape[0] - 1)
+    ncols, slabs = flat.shape[0], stiff.shape[0] // (edge.shape[0] - 1)
     each = ncols // slabs
     pairs = [(probes_in, probes), (stiff_in, stiff), (rows_in, rows), (cols_in, cols)]
     copies = [pltpu.make_async_copy(a, b, sems.at[i]) for i, (a, b) in enumerate(pairs)]
@@ -40,15 +40,14 @@
     for s in range(slabs):
         for j in range(each):
             flat[s * each + j] = probes[rows_of(probes, s, j, slabs, ncols), :].astype(BF16)
-    even, top = even_cell(), (slabs - 1) * each
-    for out, high in ((paired, even), (odd, jnp.logical_not(even))):
-        for j in range(each):
-            out[j] = jnp.where(high, flat[top + j], flat[j])
-        low_end = stiff[pl.ds(0, each, stride=slabs), :]
-        high_end = stiff[pl.ds(slabs - 1, each, stride=slabs), :]
-        end = jnp.where(high, high_end, low_end)
-        rest = jnp.zeros((out.shape[1] - each, out.shape[2]), F32)
-        out[each] = jnp.concatenate([end, rest], axis=0).astype(BF16)
+    high, top = looks_up(), (slabs - 1) * each
+    for j in range(each):
+        edge[j] = jnp.where(high, flat[top + j], flat[j])
+    low_end = stiff[pl.ds(0, each, stride=slabs), :]
+    high_end = stiff[pl.ds(slabs - 1, each, stride=slabs), :]
+    end = jnp.where(high, high_end, low_end)
+    rest = jnp.zeros((edge.shape[1] - each, edge.shape[2]), F32)
+    edge[each] = jnp.concatenate([end, rest], axis=0).astype(BF16)
 
 
 def forward_kernel(counts, rows, cols, tiles, flat, total, sent, acc):
@@ -74,7 +73,7 @@
 
 
 def backward_kernel(
-    counts, rows, cols, tiles, total, got, weight, probes, stiff, odd, part, weighted, acc
+    counts, rows, cols, tiles, total, got, weight, term, part, weighted, acc
 ):
     slots, width = tiles.shape[2], tiles.shape[3]
     nrows, nprobe = total.shape[0], total.shape[1]
@@ -95,22 +94,13 @@
         ]
     for n, out in outs:
         acc[n % 2, jnp.where(n < live, cols[0, 0, n], ncols)] += out
-    each = odd.shape[0] - 1
-    slabs = ncols // each
-    even, cell = even_cell(), lax.axis_index("cell")
-    inner = jnp.logical_and(cell > 0, cell < lax.axis_size("cell") - 1)
-    mine = lax.axis_index("ray") == 1
-    for s, here in ((0, even), (slabs - 1, jnp.logical_not(even))):
-        for j in range(each):
-            row = j * slabs + s
-            scale = 0.5 * (stiff[row : row + 1, :] + jnp.where(inner, odd[each, j : j + 1, :].astype(F32), 0.0))
-            near = jnp.where(inner, odd[j].astype(F32), 0.0)
-            term = scale * (probes[rows_of(probes, s, j, slabs, ncols), :] - near)
-            acc[0, s * each + j] += jnp.where(jnp.logical_and(mine, here), term, 0.0)
+    half = term.shape[0] // 2
+    acc[0, 0:half] += term[0:half]
+    acc[0, ncols - half : ncols] += term[half:]
     part[...] = (acc[0, 0:ncols] + acc[1, 0:ncols]).astype(BF16)
 
 
-def smooth_kernel(probes, stiff, paired, smooth, each):
+def smooth_kernel(probes, stiff, beyond, smooth, term, each):
     ncols, nprobe, width = smooth.shape
     slabs = ncols // each
     lane = lax.broadcasted_iota(I32, (1, width), 1)
@@ -144,16 +134,19 @@
     for s in range(slabs):
         for j in range(each):
             here_s, here_p = stiff_at(s, j), probe_at(s, j)
-            term = jnp.zeros((nprobe, width), F32)
+            value = jnp.zeros((nprobe, width), F32)
             for near_s, near_p in zip(neighbours(stiff_at, s, j), neighbours(probe_at, s, j)):
-                term = term + 0.5 * (here_s + near_s) * (here_p - near_p)
-            smooth[s * each + j] = term
-    even = even_cell()
-    for s, here in ((0, jnp.logical_not(even)), (slabs - 1, even)):
+                value = value + 0.5 * (here_s + near_s) * (here_p - near_p)
+            smooth[s * each + j] = value
+    high, cell = looks_up(), lax.axis_index("cell")
+    inner = jnp.logical_and(cell > 0, cell < lax.axis_size("cell") - 1)
+    there = jnp.logical_or(inner, lax.axis_index("ray") == 0)
+    for i, (s, here) in enumerate(((0, jnp.logical_not(high)), (slabs - 1, high))):
         for j in range(each):
-            scale = 0.5 * (stiff_at(s, j) + paired[each, j : j + 1, :].astype(F32))
-            term = scale * (probe_at(s, j) - paired[j].astype(F32))
-            smooth[s * each + j] += jnp.where(here, term, 0.0)
+            near_s = jnp.where(there, beyond[each, j : j + 1, :].astype(F32), 0.0)
+            near_p = jnp.where(there, beyond[j].astype(F32), 0.0)
+            value = 0.5 * (stiff_at(s, j) + near_s) * (probe_at(s, j) - near_p)
+            term[i * each + j] = jnp.where(here, value, 0.0)
 
 
 def combine_kernel(probes, smooth, mine, other, applied, diag, each):
@@ -195,24 +188,22 @@
         return pl.CostEstimate(flops=flops, bytes_accessed=moved, transcendentals=0)
 
     products = cost(2 * slots * nprobe * width * width, 2 * slots * width * width)
-    edge = pltpu.VMEM((each + 1, nprobe, width), BF16)
     pinned = [
         pltpu.with_memory_space_constraint(x, pltpu.HBM)
         for x in (row_ids, col_ids, to_rows(probes, width), to_rows(stiffness, width))
     ]
-    flat, paired, odd, grid, stiff, rows, cols = pl.pallas_call(
+    flat, edge, grid, stiff, rows, cols = pl.pallas_call(
         prepare_kernel,
         out_shape=(
             pltpu.VMEM((ncols, nprobe, width), BF16),
-            edge,
-            edge,
+            pltpu.VMEM((each + 1, nprobe, width), BF16),
             pltpu.VMEM((nprobe * ncols, width), F32),
             pltpu.VMEM((ncols, width), F32),
             pltpu.SMEM(row_ids.shape, I32),
             pltpu.SMEM(col_ids.shape, I32),
         ),
         in_specs=[HBM] * 4,
-        out_specs=(VMEM,) * 5 + (SMEM,) * 2,
+        out_specs=(VMEM,) * 4 + (SMEM,) * 2,
         scratch_shapes=[pltpu.SemaphoreType.DMA((4,))],
         compiler_params=params,
         cost_estimate=cost(12 * 10**8, 1000),
@@ -233,27 +224,38 @@
         name="forward",
     )(counts, rows, cols, blocks, flat)
 
-    def swap(value, first, cores):
-        ends = [(c * nray + r, (c + 1) * nray + r) for c in range(first, ncell - 1, 2) for r in cores]
-        return lax.ppermute(value, ("cell", "ray"), ends + [(j, i) for i, j in ends])
-
-    paired, odd = swap(paired, 0, (0, 1)), swap(odd, 1, (1,))
+    ends = {c * nray: (c ^ 1) * nray for c in range(ncell)}
+    ends |= {c * nray + 1: ((c + 1 if c % 2 else c - 1) % ncell) * nray + 1 for c in range(ncell)}
+    beyond = lax.ppermute(edge, ("cell", "ray"), list(ends.items()))
+
+    smooth, term = pl.pallas_call(
+        lambda *refs: smooth_kernel(*refs, each=each),
+        out_shape=(
+            pltpu.VMEM((ncols, nprobe, width), F32),
+            pltpu.VMEM((2 * each, nprobe, width), F32),
+        ),
+        in_specs=[VMEM] * 3,
+        out_specs=(VMEM, VMEM),
+        compiler_params=params,
+        cost_estimate=cost(5 * 10**9, 1000),
+        name="smooth",
+    )(grid, stiff, beyond)
 
     steps = [1 << i for i in range(ncell.bit_length() - 1)]
     turns = list(zip(steps, steps[-1:] + steps[:-1]))
     for i, turn in enumerate(turns):
         pairs = [(c * nray + r, (c ^ turn[r]) * nray + r) for c in range(ncell) for r in range(nray)]
         got = lax.ppermute(sent, ("cell", "ray"), pairs)
+        if i == 1:
+            got, smooth, term = lax.optimization_barrier((got, smooth, term))
         if i < len(turns) - 1:
             total = total + got.astype(F32)
             sent = total.astype(BF16)
-            if i == 0:
-                sent, odd = lax.optimization_barrier((sent, odd))
 
     part = pl.pallas_call(
         backward_kernel,
         out_shape=pltpu.VMEM((ncols, nprobe, width), BF16),
-        in_specs=[SMEM] * 3 + [VMEM] * 7,
+        in_specs=[SMEM] * 3 + [VMEM] * 5,
         out_specs=VMEM,
         scratch_shapes=[
             pltpu.VMEM((nrows, nprobe, width), BF16),
@@ -262,19 +264,9 @@
         compiler_params=params,
         cost_estimate=products,
         name="backward",
-    )(counts, rows, cols, blocks, total, got, ray_weight.reshape(nrows, width), grid, stiff, odd)
-
-    part, paired = lax.optimization_barrier((part, paired))
+    )(counts, rows, cols, blocks, total, got, ray_weight.reshape(nrows, width), term)
+
     other = lax.ppermute(part, "ray", [(0, 1), (1, 0)])
-
-    smooth = pl.pallas_call(
-        lambda *refs: smooth_kernel(*refs, each=each),
-        out_shape=pltpu.VMEM((ncols, nprobe, width), F32),
-        in_specs=[VMEM] * 3,
-        out_specs=VMEM,
-        compiler_params=params,
-        name="smooth",
-    )(grid, stiff, paired)
 
     applied, diag = pl.pallas_call(
         lambda *refs: combine_kernel(*refs, each=each),

time: 24.4 us -> 24.1 us (0.988)
  the two profiles are of different devices: /device:TPU:0 before, /device:TPU:27 now
where the time goes in v7:
time: 24.1 us; the launch traced here: 24 us
  waiting for transfers between devices  11.6 us (48%)
  starting transfers between devices  7.08 us (29%)
  Pallas kernels  3.73 us (15%)
  between operations  1.5 us (6%)
    ppermute x3, waiting for transfers between devices, local(): got = lax.ppermute(sent, ('cell', 'ray'), pairs)  10.7 us
    ppermute x1, starting transfers between devices, local(): other = lax.ppermute(part, 'ray', [(0, 1), (1, 0)])  4.01 us
    ppermute x1, starting transfers between devices, local(): beyond = lax.ppermute(edge, ('cell', 'ray'), list(ends.items()))  2.17 us
    pallas_call x1, Pallas kernels, local(): pl.pallas_call(prepare_kernel, out_shape=(pltpu.VMEM((ncols, nprobe, widt...  1.17 us
    ppermute x3, starting transfers between devices, local(): got = lax.ppermute(sent, ('cell', 'ray'), pairs)  0.91 us
    ppermute x1, waiting for transfers between devices, local(): other = lax.ppermute(part, 'ray', [(0, 1), (1, 0)])  0.9 us
    pallas_call x1, Pallas kernels, local(): pl.pallas_call(forward_kernel, out_shape=(pltpu.VMEM((nrows, nprobe, widt...  0.77 us
    pallas_call x1, Pallas kernels, local(): pl.pallas_call(lambda *refs: combine_kernel(*refs, each=each), out_shape=...  0.75 us
  transfers between devices with their start and end apart: 5, of which 4 were waited for; matrix products, arithmetic and copies ran while one was open for 0% of the time, Pallas kernels for 2%

profile of v7, /device:TPU:27, one launch (start us, length us, event | category | flops | bytes accessed | tf_op | source)
XLA Modules:
  0.0 24.0 jit_solution(14708382417329132460)
XLA Ops:
  0.6 0.0 copy-start
  1.4 1.2 %prepare.1 = (bf16[16,16,128]{2,1,0:T(8,128)(2,1)S(1)}, bf16[9,16,128]{2,1,0:T(8,128)(2,1)S(1)}, f32[256,128]{1,0:T(8,128)S(1)}, f32[16,128]{1,0:T(8,128)S(1)}, ...) custom-call(s32[1,1,96]{2,1,0:T(1,128)} %rows_in.1, s32[1,1,96]{2,1,0:T(1,128)} %cols_in.1, f32[256,128]{1,0:T(8,128)} %bitcast.22, ...), custom_call_target="tpu_custom_call" | custom-call | flops 1200000000 | bytes 1000 | tf_op jit(solution)/shard_map/prepare/pallas_call | solution.py:195
  2.6 0.0 copy-done
  2.6 0.8 %forward.1 = (f32[32,16,128]{2,1,0:T(8,128)S(1)}, bf16[32,16,128]{2,1,0:T(8,128)(2,1)S(1)}) custom-call(s32[1,1]{1,0:T(1,128)S(6)} %copy.13.counts, s32[1,1,96]{2,1,0:T(1,128)S(4)} %get-tuple-element.18.rows, s32[1,1,96]{2,1,0:T(1,128)S(4)} %get-tuple-element.19.cols, bf16[1,1,96,128,128]{4,3,2,1,0:T(8,128)(2,1)S(1)} %copy-done, ...), custom_call_target="tpu_custom_call" | custom-call | flops 50331648 | bytes 3145728 | tf_op jit(solution)/shard_map/forward/pallas_call | solution.py:213
  3.4 0.1 collective-permute-start
  3.5 2.2 %collective-permute-start.2 = (bf16[9,16,128]{2,1,0:T(8,128)(2,1)S(1)}, bf16[9,16,128]{2,1,0:T(8,128)(2,1)S(1)}, u32[]{:S(2)}, u32[]{:S(2)}) collective-permute-start(bf16[9,16,128]{2,1,0:T(8,128)(2,1)S(1)} %get-tuple-element.24), channel_id=1, source_target_pairs={{0,2},{2,0},{4,6},{6,4},{8,10},{10,8},{12,14},{14,12},{1,15},{3,5}... | collective-permute-start | bytes 110600 | tf_op jit(solution)/shard_map/ppermute | solution.py:229
  5.7 3.8 %collective-permute-done = bf16[32,16,128]{2,1,0:T(8,128)(2,1)S(1)} collective-permute-done((bf16[32,16,128]{2,1,0:T(8,128)(2,1)S(1)}, bf16[32,16,128]{2,1,0:T(8,128)(2,1)S(1)}, u32[]{:S(2)}, u32[]{:S(2)}) %collective-permute-start) | collective-permute-done | bytes 131104 | tf_op jit(solution)/shard_map/ppermute | solution.py:248
  9.5 0.7 %collective-permute-start.1 = (bf16[32,16,128]{2,1,0:T(8,128)(2,1)S(1)}, bf16[32,16,128]{2,1,0:T(8,128)(2,1)S(1)}, u32[]{:S(2)}, u32[]{:S(2)}) collective-permute-start(bf16[32,16,128]{2,1,0:T(8,128)(2,1)S(1)} %fusion), channel_id=1, source_target_pairs={{0,4},{1,3},{2,6},{3,1},{4,0},{5,7},{6,2},{7,5},{8,12},{9,11},{10,... | collective-permute-start | bytes 393224 | tf_op jit(solution)/shard_map/ppermute | solution.py:248
  10.2 0.0 collective-permute-done.2.refs_2_
  10.2 0.0 copy-start.1
  10.2 0.4 %smooth.1 = (f32[16,16,128]{2,1,0:T(8,128)S(1)}, f32[16,16,128]{2,1,0:T(8,128)S(1)}) custom-call(f32[256,128]{1,0:T(8,128)S(1)} %get-tuple-element.17.refs_0_, f32[16,128]{1,0:T(8,128)S(1)} %get-tuple-element.23.refs_1_, bf16[9,16,128]{2,1,0:T(8,128)(2,1)S(1)} %collective-permute-done.2.refs_2_), custom_call_target="tpu_custom_call" | custom-call | flops 5000000000 | bytes 1000 | tf_op jit(solution)/shard_map/smooth/pallas_call | solution.py:231
  10.6 3.1 %collective-permute-done.1 = bf16[32,16,128]{2,1,0:T(8,128)(2,1)S(1)} collective-permute-done((bf16[32,16,128]{2,1,0:T(8,128)(2,1)S(1)}, bf16[32,16,128]{2,1,0:T(8,128)(2,1)S(1)}, u32[]{:S(2)}, u32[]{:S(2)}) %collective-permute-start.1) | collective-permute-done | bytes 131104 | tf_op jit(solution)/shard_map/ppermute | solution.py:248
  13.7 0.1 collective-permute-start.3
  13.8 3.8 %collective-permute-done.3.got = bf16[32,16,128]{2,1,0:T(8,128)(2,1)S(1)} collective-permute-done((bf16[32,16,128]{2,1,0:T(8,128)(2,1)S(1)}, bf16[32,16,128]{2,1,0:T(8,128)(2,1)S(1)}, u32[]{:S(2)}, u32[]{:S(2)}) %collective-permute-start.3) | collective-permute-done | bytes 131104 | tf_op jit(solution)/shard_map/ppermute | solution.py:248
  17.6 0.0 copy-done.1
  17.6 0.7 %backward.1.refs_2_ = bf16[16,16,128]{2,1,0:T(8,128)(2,1)S(1)} custom-call(s32[1,1]{1,0:T(1,128)S(6)} %copy.13.counts, s32[1,1,96]{2,1,0:T(1,128)S(4)} %get-tuple-element.18.rows, s32[1,1,96]{2,1,0:T(1,128)S(4)} %get-tuple-element.19.cols, bf16[1,1,96,128,128]{4,3,2,1,0:T(8,128)(2,1)S(1)} %copy-done, f32[32,16,128]{2,1,0:T(8,128)S(1)} %get-tuple-element.33.total, ...), custom_call_target="tpu_custom_call" | custom-call | flops 50331648 | bytes 3145728 | tf_op jit(solution)/shard_map/backward/pallas_call | solution.py:255
  18.3 4.0 %collective-permute-start.4 = (bf16[16,16,128]{2,1,0:T(8,128)(2,1)S(1)}, bf16[16,16,128]{2,1,0:T(8,128)(2,1)S(1)}, u32[]{:S(2)}, u32[]{:S(2)}) collective-permute-start(bf16[16,16,128]{2,1,0:T(8,128)(2,1)S(1)} %backward.1.refs_2_), channel_id=1, source_target_pairs={{0,1},{1,0},{2,3},{3,2},{4,5},{5,4},{6,7},{7,6},{8,9},{9,8},{10,11... | collective-permute-start | bytes 196616 | tf_op jit(solution)/shard_map/ppermute | solution.py:269
  22.3 0.9 %collective-permute-done.4.refs_3_ = bf16[16,16,128]{2,1,0:T(8,128)(2,1)S(1)} collective-permute-done((bf16[16,16,128]{2,1,0:T(8,128)(2,1)S(1)}, bf16[16,16,128]{2,1,0:T(8,128)(2,1)S(1)}, u32[]{:S(2)}, u32[]{:S(2)}) %collective-permute-start.4) | collective-permute-done | bytes 65568 | tf_op jit(solution)/shard_map/ppermute | solution.py:269
  23.2 0.7 %combine.1 = (f32[256,128]{1,0:T(8,128)}, f32[16,128]{1,0:T(8,128)}) custom-call(f32[256,128]{1,0:T(8,128)S(1)} %get-tuple-element.17.refs_0_, f32[16,16,128]{2,1,0:T(8,128)S(1)} %get-tuple-element.27.refs_1_, bf16[16,16,128]{2,1,0:T(8,128)(2,1)S(1)} %backward.1.refs_2_, bf16[16,16,128]{2,1,0:T(8,128)(2,1)S(1)} %collective-permute-done.4.refs_3_), custom_call_target="tpu_custom_call" | custom-call | tf_op jit(solution)/shard_map/combine/pallas_call | solution.py:271
  (2 shorter events, 0.1 us)
Async XLA Ops:
  0.6 2.0 %copy-start = (bf16[1,1,96,128,128]{4,3,2,1,0:T(8,128)(2,1)S(1)}, bf16[1,1,96,128,128]{4,3,2,1,0:T(8,128)(2,1)}, u32[]{:S(2)}) copy-start(bf16[1,1,96,128,128]{4,3,2,1,0:T(8,128)(2,1)} %tiles.3) | copy-start | bytes 9437188
  3.4 6.1 %collective-permute-start = (bf16[32,16,128]{2,1,0:T(8,128)(2,1)S(1)}, bf16[32,16,128]{2,1,0:T(8,128)(2,1)S(1)}, u32[]{:S(2)}, u32[]{:S(2)}) collective-permute-start(bf16[32,16,128]{2,1,0:T(8,128)(2,1)S(1)} %get-tuple-element.22), channel_id=1, source_target_pairs={{0,2},{1,9},{2,0},{3,11},{4,6},{5,13},{6,4},{7,15},{8,10},{9,1},{1... | collective-permute-start | bytes 393224 | tf_op jit(solution)/shard_map/ppermute | solution.py:248
  3.5 6.7 %collective-permute-start.2 = (bf16[9,16,128]{2,1,0:T(8,128)(2,1)S(1)}, bf16[9,16,128]{2,1,0:T(8,128)(2,1)S(1)}, u32[]{:S(2)}, u32[]{:S(2)}) collective-permute-start(bf16[9,16,128]{2,1,0:T(8,128)(2,1)S(1)} %get-tuple-element.24), channel_id=1, source_target_pairs={{0,2},{2,0},{4,6},{6,4},{8,10},{10,8},{12,14},{14,12},{1,15},{3,5}... | collective-permute-start | bytes 110600 | tf_op jit(solution)/shard_map/ppermute | solution.py:229
  9.5 4.2 %collective-permute-start.1 = (bf16[32,16,128]{2,1,0:T(8,128)(2,1)S(1)}, bf16[32,16,128]{2,1,0:T(8,128)(2,1)S(1)}, u32[]{:S(2)}, u32[]{:S(2)}) collective-permute-start(bf16[32,16,128]{2,1,0:T(8,128)(2,1)S(1)} %fusion), channel_id=1, source_target_pairs={{0,4},{1,3},{2,6},{3,1},{4,0},{5,7},{6,2},{7,5},{8,12},{9,11},{10,... | collective-permute-start | bytes 393224 | tf_op jit(solution)/shard_map/ppermute | solution.py:248
  10.2 7.4 %copy-start.1 = (f32[4096]{0:T(1024)S(1)}, f32[4096]{0:T(1024)}, u32[]{:S(2)}) copy-start(f32[4096]{0:T(1024)} %param.11) | copy-start | bytes 49156
  13.7 3.9 %collective-permute-start.3 = (bf16[32,16,128]{2,1,0:T(8,128)(2,1)S(1)}, bf16[32,16,128]{2,1,0:T(8,128)(2,1)S(1)}, u32[]{:S(2)}, u32[]{:S(2)}) collective-permute-start(bf16[32,16,128]{2,1,0:T(8,128)(2,1)S(1)} %get-tuple-element.32), channel_id=1, source_target_pairs={{0,8},{1,5},{2,10},{3,7},{4,12},{5,1},{6,14},{7,3},{8,0},{9,13},{1... | collective-permute-start | bytes 393224 | tf_op jit(solution)/shard_map/ppermute | solution.py:248
  18.3 4.9 %collective-permute-start.4 = (bf16[16,16,128]{2,1,0:T(8,128)(2,1)S(1)}, bf16[16,16,128]{2,1,0:T(8,128)(2,1)S(1)}, u32[]{:S(2)}, u32[]{:S(2)}) collective-permute-start(bf16[16,16,128]{2,1,0:T(8,128)(2,1)S(1)} %backward.1.refs_2_), channel_id=1, source_target_pairs={{0,1},{1,0},{2,3},{3,2},{4,5},{5,4},{6,7},{7,6},{8,9},{9,8},{10,11... | collective-permute-start | bytes 196616 | tf_op jit(solution)/shard_map/ppermute | solution.py:269

commit v8 on v7

--- a/solution.py
+++ b/solution.py
@@ -73,7 +73,7 @@
 
 
 def backward_kernel(
-    counts, rows, cols, tiles, total, got, weight, term, part, weighted, acc
+    rows, target, tiles, total, got, weight, term, part, weighted, acc
 ):
     slots, width = tiles.shape[2], tiles.shape[3]
     nrows, nprobe = total.shape[0], total.shape[1]
@@ -82,7 +82,6 @@
         value = total[k] + got[k].astype(F32)
         weighted[k] = (value * weight[k : k + 1, :]).astype(BF16)
     acc[...] = jnp.zeros_like(acc)
-    live = counts[0, 0]
     outs = []
     for group in groups(slots):
         left = jnp.concatenate([weighted[rows[0, 0, n]] for n in group], axis=0)
@@ -93,16 +92,18 @@
             for i, n in enumerate(group)
         ]
     for n, out in outs:
-        acc[n % 2, jnp.where(n < live, cols[0, 0, n], ncols)] += out
+        acc[n % 2, target[0, 0, n]] += out
     half = term.shape[0] // 2
     acc[0, 0:half] += term[0:half]
     acc[0, ncols - half : ncols] += term[half:]
     part[...] = (acc[0, 0:ncols] + acc[1, 0:ncols]).astype(BF16)
 
 
-def smooth_kernel(probes, stiff, beyond, smooth, term, each):
+def smooth_kernel(counts, cols, probes, stiff, beyond, smooth, term, target, each):
     ncols, nprobe, width = smooth.shape
     slabs = ncols // each
+    for n in range(cols.shape[2]):
+        target[0, 0, n] = jnp.where(n < counts[0, 0], cols[0, 0, n], ncols)
     lane = lax.broadcasted_iota(I32, (1, width), 1)
     at_z = lane % NZ
 
@@ -228,18 +229,19 @@
     ends |= {c * nray + 1: ((c + 1 if c % 2 else c - 1) % ncell) * nray + 1 for c in range(ncell)}
     beyond = lax.ppermute(edge, ("cell", "ray"), list(ends.items()))
 
-    smooth, term = pl.pallas_call(
+    smooth, term, target = pl.pallas_call(
         lambda *refs: smooth_kernel(*refs, each=each),
         out_shape=(
             pltpu.VMEM((ncols, nprobe, width), F32),
             pltpu.VMEM((2 * each, nprobe, width), F32),
-        ),
-        in_specs=[VMEM] * 3,
-        out_specs=(VMEM, VMEM),
+            pltpu.SMEM(col_ids.shape, I32),
+        ),
+        in_specs=[SMEM] * 2 + [VMEM] * 3,
+        out_specs=(VMEM, VMEM, SMEM),
         compiler_params=params,
         cost_estimate=cost(5 * 10**9, 1000),
         name="smooth",
-    )(grid, stiff, beyond)
+    )(counts, cols, grid, stiff, beyond)
 
     steps = [1 << i for i in range(ncell.bit_length() - 1)]
     turns = list(zip(steps, steps[-1:] + steps[:-1]))
@@ -255,7 +257,7 @@
     part = pl.pallas_call(
         backward_kernel,
         out_shape=pltpu.VMEM((ncols, nprobe, width), BF16),
-        in_specs=[SMEM] * 3 + [VMEM] * 5,
+        in_specs=[SMEM] * 2 + [VMEM] * 5,
         out_specs=VMEM,
         scratch_shapes=[
             pltpu.VMEM((nrows, nprobe, width), BF16),
@@ -264,7 +266,7 @@
         compiler_params=params,
         cost_estimate=products,
         name="backward",
-    )(counts, rows, cols, blocks, total, got, ray_weight.reshape(nrows, width), term)
+    )(rows, target, blocks, total, got, ray_weight.reshape(nrows, width), term)
 
     other = lax.ppermute(part, "ray", [(0, 1), (1, 0)])
 

time: 24.1 us -> 24.1 us (level)
  no operation moved by 1% of the time
where the time goes in v8:
time: 24.1 us; the launch traced here: 24 us
  waiting for transfers between devices  11.5 us (48%)
  starting transfers between devices  7.08 us (29%)
  Pallas kernels  3.85 us (16%)
  between operations  1.49 us (6%)
    ppermute x3, waiting for transfers between devices, local(): got = lax.ppermute(sent, ('cell', 'ray'), pairs)  10.6 us
    ppermute x1, starting transfers between devices, local(): other = lax.ppermute(part, 'ray', [(0, 1), (1, 0)])  4.01 us
    ppermute x1, starting transfers between devices, local(): beyond = lax.ppermute(edge, ('cell', 'ray'), list(ends.items()))  2.17 us
    pallas_call x1, Pallas kernels, local(): pl.pallas_call(prepare_kernel, out_shape=(pltpu.VMEM((ncols, nprobe, widt...  1.17 us
    ppermute x3, starting transfers between devices, local(): got = lax.ppermute(sent, ('cell', 'ray'), pairs)  0.91 us
    ppermute x1, waiting for transfers between devices, local(): other = lax.ppermute(part, 'ray', [(0, 1), (1, 0)])  0.9 us
    pallas_call x1, Pallas kernels, local(): pl.pallas_call(forward_kernel, out_shape=(pltpu.VMEM((nrows, nprobe, widt...  0.77 us
    pallas_call x1, Pallas kernels, local(): pl.pallas_call(lambda *refs: combine_kernel(*refs, each=each), out_shape=...  0.75 us
  transfers between devices with their start and end apart: 5, of which 4 were waited for; matrix products, arithmetic and copies ran while one was open for 0% of the time, Pallas kernels for 2%

profile of v8, /device:TPU:27, one launch (start us, length us, event | category | flops | bytes accessed | tf_op | source)
XLA Modules:
  0.0 24.0 jit_solution(719942995735399519)
XLA Ops:
  0.6 0.0 copy-start
  1.4 1.2 %prepare.1 = (bf16[16,16,128]{2,1,0:T(8,128)(2,1)S(1)}, bf16[9,16,128]{2,1,0:T(8,128)(2,1)S(1)}, f32[256,128]{1,0:T(8,128)S(1)}, f32[16,128]{1,0:T(8,128)S(1)}, ...) custom-call(s32[1,1,96]{2,1,0:T(1,128)} %rows_in.1, s32[1,1,96]{2,1,0:T(1,128)} %cols_in.1, f32[256,128]{1,0:T(8,128)} %bitcast.22, ...), custom_call_target="tpu_custom_call" | custom-call | flops 1200000000 | bytes 1000 | tf_op jit(solution)/shard_map/prepare/pallas_call | solution.py:196
  2.6 0.0 copy-done
  2.6 0.8 %forward.1 = (f32[32,16,128]{2,1,0:T(8,128)S(1)}, bf16[32,16,128]{2,1,0:T(8,128)(2,1)S(1)}) custom-call(s32[1,1]{1,0:T(1,128)S(6)} %copy.13.counts.refs_0_, s32[1,1,96]{2,1,0:T(1,128)S(4)} %get-tuple-element.19.rows, s32[1,1,96]{2,1,0:T(1,128)S(4)} %get-tuple-element.20.cols.refs_1_, bf16[1,1,96,128,128]{4,3,2,1,0:T(8,128)(2,1)S(1)} %copy-done, ...), custom_call_target="tpu_custom_call" | custom-call | flops 50331648 | bytes 3145728 | tf_op jit(solution)/shard_map/forward/pallas_call | solution.py:214
  3.4 0.1 collective-permute-start
  3.5 2.2 %collective-permute-start.2 = (bf16[9,16,128]{2,1,0:T(8,128)(2,1)S(1)}, bf16[9,16,128]{2,1,0:T(8,128)(2,1)S(1)}, u32[]{:S(2)}, u32[]{:S(2)}) collective-permute-start(bf16[9,16,128]{2,1,0:T(8,128)(2,1)S(1)} %get-tuple-element.25), channel_id=1, source_target_pairs={{0,2},{2,0},{4,6},{6,4},{8,10},{10,8},{12,14},{14,12},{1,15},{3,5}... | collective-permute-start | bytes 110600 | tf_op jit(solution)/shard_map/ppermute | solution.py:230
  5.7 3.8 %collective-permute-done = bf16[32,16,128]{2,1,0:T(8,128)(2,1)S(1)} collective-permute-done((bf16[32,16,128]{2,1,0:T(8,128)(2,1)S(1)}, bf16[32,16,128]{2,1,0:T(8,128)(2,1)S(1)}, u32[]{:S(2)}, u32[]{:S(2)}) %collective-permute-start) | collective-permute-done | bytes 131104 | tf_op jit(solution)/shard_map/ppermute | solution.py:250
  9.5 0.7 %collective-permute-start.1 = (bf16[32,16,128]{2,1,0:T(8,128)(2,1)S(1)}, bf16[32,16,128]{2,1,0:T(8,128)(2,1)S(1)}, u32[]{:S(2)}, u32[]{:S(2)}) collective-permute-start(bf16[32,16,128]{2,1,0:T(8,128)(2,1)S(1)} %fusion), channel_id=1, source_target_pairs={{0,4},{1,3},{2,6},{3,1},{4,0},{5,7},{6,2},{7,5},{8,12},{9,11},{10,... | collective-permute-start | bytes 393224 | tf_op jit(solution)/shard_map/ppermute | solution.py:250
  10.2 0.0 collective-permute-done.2.refs_4_
  10.2 0.0 copy-start.1
  10.2 0.5 %smooth.1 = (f32[16,16,128]{2,1,0:T(8,128)S(1)}, f32[16,16,128]{2,1,0:T(8,128)S(1)}, s32[1,1,96]{2,1,0:T(1,128)S(4)}) custom-call(s32[1,1]{1,0:T(1,128)S(6)} %copy.13.counts.refs_0_, s32[1,1,96]{2,1,0:T(1,128)S(4)} %get-tuple-element.20.cols.refs_1_, f32[256,128]{1,0:T(8,128)S(1)} %get-tuple-element.18.refs_2_.refs_0_, ...), custom_call_target="tpu_custom_call" | custom-call | flops 5000000000 | bytes 1000 | tf_op jit(solution)/shard_map/smooth/pallas_call | solution.py:232
  10.7 3.0 %collective-permute-done.1 = bf16[32,16,128]{2,1,0:T(8,128)(2,1)S(1)} collective-permute-done((bf16[32,16,128]{2,1,0:T(8,128)(2,1)S(1)}, bf16[32,16,128]{2,1,0:T(8,128)(2,1)S(1)}, u32[]{:S(2)}, u32[]{:S(2)}) %collective-permute-start.1) | collective-permute-done | bytes 131104 | tf_op jit(solution)/shard_map/ppermute | solution.py:250
  13.7 0.1 collective-permute-start.3
  13.8 3.8 %collective-permute-done.3.got = bf16[32,16,128]{2,1,0:T(8,128)(2,1)S(1)} collective-permute-done((bf16[32,16,128]{2,1,0:T(8,128)(2,1)S(1)}, bf16[32,16,128]{2,1,0:T(8,128)(2,1)S(1)}, u32[]{:S(2)}, u32[]{:S(2)}) %collective-permute-start.3) | collective-permute-done | bytes 131104 | tf_op jit(solution)/shard_map/ppermute | solution.py:250
  17.6 0.0 copy-done.1
  17.6 0.7 %backward.1.refs_2_ = bf16[16,16,128]{2,1,0:T(8,128)(2,1)S(1)} custom-call(s32[1,1,96]{2,1,0:T(1,128)S(4)} %get-tuple-element.19.rows, s32[1,1,96]{2,1,0:T(1,128)S(4)} %get-tuple-element.29.target, bf16[1,1,96,128,128]{4,3,2,1,0:T(8,128)(2,1)S(1)} %copy-done, f32[32,16,128]{2,1,0:T(8,128)S(1)} %get-tuple-element.35.total, ...), custom_call_target="tpu_custom_call" | custom-call | flops 50331648 | bytes 3145728 | tf_op jit(solution)/shard_map/backward/pallas_call | solution.py:257
  18.3 4.0 %collective-permute-start.4 = (bf16[16,16,128]{2,1,0:T(8,128)(2,1)S(1)}, bf16[16,16,128]{2,1,0:T(8,128)(2,1)S(1)}, u32[]{:S(2)}, u32[]{:S(2)}) collective-permute-start(bf16[16,16,128]{2,1,0:T(8,128)(2,1)S(1)} %backward.1.refs_2_), channel_id=1, source_target_pairs={{0,1},{1,0},{2,3},{3,2},{4,5},{5,4},{6,7},{7,6},{8,9},{9,8},{10,11... | collective-permute-start | bytes 196616 | tf_op jit(solution)/shard_map/ppermute | solution.py:271
  22.3 0.9 %collective-permute-done.4.refs_3_ = bf16[16,16,128]{2,1,0:T(8,128)(2,1)S(1)} collective-permute-done((bf16[16,16,128]{2,1,0:T(8,128)(2,1)S(1)}, bf16[16,16,128]{2,1,0:T(8,128)(2,1)S(1)}, u32[]{:S(2)}, u32[]{:S(2)}) %collective-permute-start.4) | collective-permute-done | bytes 65568 | tf_op jit(solution)/shard_map/ppermute | solution.py:271
  23.2 0.7 %combine.1 = (f32[256,128]{1,0:T(8,128)}, f32[16,128]{1,0:T(8,128)}) custom-call(f32[256,128]{1,0:T(8,128)S(1)} %get-tuple-element.18.refs_2_.refs_0_, f32[16,16,128]{2,1,0:T(8,128)S(1)} %get-tuple-element.28.refs_1_, bf16[16,16,128]{2,1,0:T(8,128)(2,1)S(1)} %backward.1.refs_2_, bf16[16,16,128]{2,1,0:T(8,128)(2,1)S(1)} %collective-permute-done.4.refs_3_), custom_call_target="tpu_custom_call" | custom-call | tf_op jit(solution)/shard_map/combine/pallas_call | solution.py:273
  (2 shorter events, 0.1 us)
Async XLA Ops:
  0.6 2.0 %copy-start = (bf16[1,1,96,128,128]{4,3,2,1,0:T(8,128)(2,1)S(1)}, bf16[1,1,96,128,128]{4,3,2,1,0:T(8,128)(2,1)}, u32[]{:S(2)}) copy-start(bf16[1,1,96,128,128]{4,3,2,1,0:T(8,128)(2,1)} %tiles.3) | copy-start | bytes 9437188
  3.4 6.1 %collective-permute-start = (bf16[32,16,128]{2,1,0:T(8,128)(2,1)S(1)}, bf16[32,16,128]{2,1,0:T(8,128)(2,1)S(1)}, u32[]{:S(2)}, u32[]{:S(2)}) collective-permute-start(bf16[32,16,128]{2,1,0:T(8,128)(2,1)S(1)} %get-tuple-element.23), channel_id=1, source_target_pairs={{0,2},{1,9},{2,0},{3,11},{4,6},{5,13},{6,4},{7,15},{8,10},{9,1},{1... | collective-permute-start | bytes 393224 | tf_op jit(solution)/shard_map/ppermute | solution.py:250
  3.5 6.7 %collective-permute-start.2 = (bf16[9,16,128]{2,1,0:T(8,128)(2,1)S(1)}, bf16[9,16,128]{2,1,0:T(8,128)(2,1)S(1)}, u32[]{:S(2)}, u32[]{:S(2)}) collective-permute-start(bf16[9,16,128]{2,1,0:T(8,128)(2,1)S(1)} %get-tuple-element.25), channel_id=1, source_target_pairs={{0,2},{2,0},{4,6},{6,4},{8,10},{10,8},{12,14},{14,12},{1,15},{3,5}... | collective-permute-start | bytes 110600 | tf_op jit(solution)/shard_map/ppermute | solution.py:230
  9.5 4.2 %collective-permute-start.1 = (bf16[32,16,128]{2,1,0:T(8,128)(2,1)S(1)}, bf16[32,16,128]{2,1,0:T(8,128)(2,1)S(1)}, u32[]{:S(2)}, u32[]{:S(2)}) collective-permute-start(bf16[32,16,128]{2,1,0:T(8,128)(2,1)S(1)} %fusion), channel_id=1, source_target_pairs={{0,4},{1,3},{2,6},{3,1},{4,0},{5,7},{6,2},{7,5},{8,12},{9,11},{10,... | collective-permute-start | bytes 393224 | tf_op jit(solution)/shard_map/ppermute | solution.py:250
  10.2 7.4 %copy-start.1 = (f32[4096]{0:T(1024)S(1)}, f32[4096]{0:T(1024)}, u32[]{:S(2)}) copy-start(f32[4096]{0:T(1024)} %param.11) | copy-start | bytes 49156
  13.7 3.9 %collective-permute-start.3 = (bf16[32,16,128]{2,1,0:T(8,128)(2,1)S(1)}, bf16[32,16,128]{2,1,0:T(8,128)(2,1)S(1)}, u32[]{:S(2)}, u32[]{:S(2)}) collective-permute-start(bf16[32,16,128]{2,1,0:T(8,128)(2,1)S(1)} %get-tuple-element.34), channel_id=1, source_target_pairs={{0,8},{1,5},{2,10},{3,7},{4,12},{5,1},{6,14},{7,3},{8,0},{9,13},{1... | collective-permute-start | bytes 393224 | tf_op jit(solution)/shard_map/ppermute | solution.py:250
  18.3 4.9 %collective-permute-start.4 = (bf16[16,16,128]{2,1,0:T(8,128)(2,1)S(1)}, bf16[16,16,128]{2,1,0:T(8,128)(2,1)S(1)}, u32[]{:S(2)}, u32[]{:S(2)}) collective-permute-start(bf16[16,16,128]{2,1,0:T(8,128)(2,1)S(1)} %backward.1.refs_2_), channel_id=1, source_target_pairs={{0,1},{1,0},{2,3},{3,2},{4,5},{5,4},{6,7},{7,6},{8,9},{9,8},{10,11... | collective-permute-start | bytes 196616 | tf_op jit(solution)/shard_map/ppermute | solution.py:271

commit v9 on v8

--- a/solution.py
+++ b/solution.py
@@ -78,9 +78,8 @@
     slots, width = tiles.shape[2], tiles.shape[3]
     nrows, nprobe = total.shape[0], total.shape[1]
     ncols = part.shape[0]
-    for k in range(nrows):
-        value = total[k] + got[k].astype(F32)
-        weighted[k] = (value * weight[k : k + 1, :]).astype(BF16)
+    value = total[...] + got[...].astype(F32)
+    weighted[...] = (value * weight[...][:, None, :]).astype(BF16)
     acc[...] = jnp.zeros_like(acc)
     outs = []
     for group in groups(slots):

time: 24.1 us -> 24.2 us (level)
  no operation moved by 1% of the time
where the time goes in v9:
time: 24.2 us; the launch traced here: 24 us
  waiting for transfers between devices  11.5 us (48%)
  starting transfers between devices  7.07 us (29%)
  Pallas kernels  3.88 us (16%)
  between operations  1.49 us (6%)
    ppermute x3, waiting for transfers between devices, local(): got = lax.ppermute(sent, ('cell', 'ray'), pairs)  10.6 us
    ppermute x1, starting transfers between devices, local(): other = lax.ppermute(part, 'ray', [(0, 1), (1, 0)])  4.01 us
    ppermute x1, starting transfers between devices, local(): beyond = lax.ppermute(edge, ('cell', 'ray'), list(ends.items()))  2.16 us
    pallas_call x1, Pallas kernels, local(): pl.pallas_call(prepare_kernel, out_shape=(pltpu.VMEM((ncols, nprobe, widt...  1.17 us
    ppermute x3, starting transfers between devices, local(): got = lax.ppermute(sent, ('cell', 'ray'), pairs)  0.91 us
    ppermute x1, waiting for transfers between devices, local(): other = lax.ppermute(part, 'ray', [(0, 1), (1, 0)])  0.9 us
    pallas_call x1, Pallas kernels, local(): pl.pallas_call(forward_kernel, out_shape=(pltpu.VMEM((nrows, nprobe, widt...  0.77 us
    pallas_call x1, Pallas kernels, local(): pl.pallas_call(lambda *refs: combine_kernel(*refs, each=each), out_shape=...  0.75 us
  transfers between devices with their start and end apart: 5, of which 4 were waited for; matrix products, arithmetic and copies ran while one was open for 0% of the time, Pallas kernels for 2%

profile of v9, /device:TPU:27, one launch (start us, length us, event | category | flops | bytes accessed | tf_op | source)
XLA Modules:
  0.0 24.0 jit_solution(2547393869314424664)
XLA Ops:
  0.6 0.0 copy-start
  1.4 1.2 %prepare.1 = (bf16[16,16,128]{2,1,0:T(8,128)(2,1)S(1)}, bf16[9,16,128]{2,1,0:T(8,128)(2,1)S(1)}, f32[256,128]{1,0:T(8,128)S(1)}, f32[16,128]{1,0:T(8,128)S(1)}, ...) custom-call(s32[1,1,96]{2,1,0:T(1,128)} %rows_in.1, s32[1,1,96]{2,1,0:T(1,128)} %cols_in.1, f32[256,128]{1,0:T(8,128)} %bitcast.22, ...), custom_call_target="tpu_custom_call" | custom-call | flops 1200000000 | bytes 1000 | tf_op jit(solution)/shard_map/prepare/pallas_call | solution.py:195
  2.6 0.0 copy-done
  2.6 0.8 %forward.1 = (f32[32,16,128]{2,1,0:T(8,128)S(1)}, bf16[32,16,128]{2,1,0:T(8,128)(2,1)S(1)}) custom-call(s32[1,1]{1,0:T(1,128)S(6)} %copy.13.counts.refs_0_, s32[1,1,96]{2,1,0:T(1,128)S(4)} %get-tuple-element.19.rows, s32[1,1,96]{2,1,0:T(1,128)S(4)} %get-tuple-element.20.cols.refs_1_, bf16[1,1,96,128,128]{4,3,2,1,0:T(8,128)(2,1)S(1)} %copy-done, ...), custom_call_target="tpu_custom_call" | custom-call | flops 50331648 | bytes 3145728 | tf_op jit(solution)/shard_map/forward/pallas_call | solution.py:213
  3.4 0.1 collective-permute-start
  3.5 2.2 %collective-permute-start.2 = (bf16[9,16,128]{2,1,0:T(8,128)(2,1)S(1)}, bf16[9,16,128]{2,1,0:T(8,128)(2,1)S(1)}, u32[]{:S(2)}, u32[]{:S(2)}) collective-permute-start(bf16[9,16,128]{2,1,0:T(8,128)(2,1)S(1)} %get-tuple-element.25), channel_id=1, source_target_pairs={{0,2},{2,0},{4,6},{6,4},{8,10},{10,8},{12,14},{14,12},{1,15},{3,5}... | collective-permute-start | bytes 110600 | tf_op jit(solution)/shard_map/ppermute | solution.py:229
  5.7 3.8 %collective-permute-done = bf16[32,16,128]{2,1,0:T(8,128)(2,1)S(1)} collective-permute-done((bf16[32,16,128]{2,1,0:T(8,128)(2,1)S(1)}, bf16[32,16,128]{2,1,0:T(8,128)(2,1)S(1)}, u32[]{:S(2)}, u32[]{:S(2)}) %collective-permute-start) | collective-permute-done | bytes 131104 | tf_op jit(solution)/shard_map/ppermute | solution.py:249
  9.5 0.7 %collective-permute-start.1 = (bf16[32,16,128]{2,1,0:T(8,128)(2,1)S(1)}, bf16[32,16,128]{2,1,0:T(8,128)(2,1)S(1)}, u32[]{:S(2)}, u32[]{:S(2)}) collective-permute-start(bf16[32,16,128]{2,1,0:T(8,128)(2,1)S(1)} %fusion), channel_id=1, source_target_pairs={{0,4},{1,3},{2,6},{3,1},{4,0},{5,7},{6,2},{7,5},{8,12},{9,11},{10,... | collective-permute-start | bytes 393224 | tf_op jit(solution)/shard_map/ppermute | solution.py:249
  10.2 0.0 collective-permute-done.2.refs_4_
  10.2 0.0 copy-start.1
  10.2 0.5 %smooth.1 = (f32[16,16,128]{2,1,0:T(8,128)S(1)}, f32[16,16,128]{2,1,0:T(8,128)S(1)}, s32[1,1,96]{2,1,0:T(1,128)S(4)}) custom-call(s32[1,1]{1,0:T(1,128)S(6)} %copy.13.counts.refs_0_, s32[1,1,96]{2,1,0:T(1,128)S(4)} %get-tuple-element.20.cols.refs_1_, f32[256,128]{1,0:T(8,128)S(1)} %get-tuple-element.18.refs_2_.refs_0_, ...), custom_call_target="tpu_custom_call" | custom-call | flops 5000000000 | bytes 1000 | tf_op jit(solution)/shard_map/smooth/pallas_call | solution.py:231
  10.7 3.0 %collective-permute-done.1 = bf16[32,16,128]{2,1,0:T(8,128)(2,1)S(1)} collective-permute-done((bf16[32,16,128]{2,1,0:T(8,128)(2,1)S(1)}, bf16[32,16,128]{2,1,0:T(8,128)(2,1)S(1)}, u32[]{:S(2)}, u32[]{:S(2)}) %collective-permute-start.1) | collective-permute-done | bytes 131104 | tf_op jit(solution)/shard_map/ppermute | solution.py:249
  13.7 0.1 collective-permute-start.3
  13.8 3.8 %collective-permute-done.3.got = bf16[32,16,128]{2,1,0:T(8,128)(2,1)S(1)} collective-permute-done((bf16[32,16,128]{2,1,0:T(8,128)(2,1)S(1)}, bf16[32,16,128]{2,1,0:T(8,128)(2,1)S(1)}, u32[]{:S(2)}, u32[]{:S(2)}) %collective-permute-start.3) | collective-permute-done | bytes 131104 | tf_op jit(solution)/shard_map/ppermute | solution.py:249
  17.6 0.0 copy-done.1
  17.6 0.7 %backward.1.refs_2_ = bf16[16,16,128]{2,1,0:T(8,128)(2,1)S(1)} custom-call(s32[1,1,96]{2,1,0:T(1,128)S(4)} %get-tuple-element.19.rows, s32[1,1,96]{2,1,0:T(1,128)S(4)} %get-tuple-element.29.target, bf16[1,1,96,128,128]{4,3,2,1,0:T(8,128)(2,1)S(1)} %copy-done, f32[32,16,128]{2,1,0:T(8,128)S(1)} %get-tuple-element.35.total, ...), custom_call_target="tpu_custom_call" | custom-call | flops 50331648 | bytes 3145728 | tf_op jit(solution)/shard_map/backward/pallas_call | solution.py:256
  18.3 4.0 %collective-permute-start.4 = (bf16[16,16,128]{2,1,0:T(8,128)(2,1)S(1)}, bf16[16,16,128]{2,1,0:T(8,128)(2,1)S(1)}, u32[]{:S(2)}, u32[]{:S(2)}) collective-permute-start(bf16[16,16,128]{2,1,0:T(8,128)(2,1)S(1)} %backward.1.refs_2_), channel_id=1, source_target_pairs={{0,1},{1,0},{2,3},{3,2},{4,5},{5,4},{6,7},{7,6},{8,9},{9,8},{10,11... | collective-permute-start | bytes 196616 | tf_op jit(solution)/shard_map/ppermute | solution.py:270
  22.3 0.9 %collective-permute-done.4.refs_3_ = bf16[16,16,128]{2,1,0:T(8,128)(2,1)S(1)} collective-permute-done((bf16[16,16,128]{2,1,0:T(8,128)(2,1)S(1)}, bf16[16,16,128]{2,1,0:T(8,128)(2,1)S(1)}, u32[]{:S(2)}, u32[]{:S(2)}) %collective-permute-start.4) | collective-permute-done | bytes 65568 | tf_op jit(solution)/shard_map/ppermute | solution.py:270
  23.2 0.7 %combine.1 = (f32[256,128]{1,0:T(8,128)}, f32[16,128]{1,0:T(8,128)}) custom-call(f32[256,128]{1,0:T(8,128)S(1)} %get-tuple-element.18.refs_2_.refs_0_, f32[16,16,128]{2,1,0:T(8,128)S(1)} %get-tuple-element.28.refs_1_, bf16[16,16,128]{2,1,0:T(8,128)(2,1)S(1)} %backward.1.refs_2_, bf16[16,16,128]{2,1,0:T(8,128)(2,1)S(1)} %collective-permute-done.4.refs_3_), custom_call_target="tpu_custom_call" | custom-call | tf_op jit(solution)/shard_map/combine/pallas_call | solution.py:272
  (2 shorter events, 0.1 us)
Async XLA Ops:
  0.6 2.0 %copy-start = (bf16[1,1,96,128,128]{4,3,2,1,0:T(8,128)(2,1)S(1)}, bf16[1,1,96,128,128]{4,3,2,1,0:T(8,128)(2,1)}, u32[]{:S(2)}) copy-start(bf16[1,1,96,128,128]{4,3,2,1,0:T(8,128)(2,1)} %tiles.3) | copy-start | bytes 9437188
  3.4 6.1 %collective-permute-start = (bf16[32,16,128]{2,1,0:T(8,128)(2,1)S(1)}, bf16[32,16,128]{2,1,0:T(8,128)(2,1)S(1)}, u32[]{:S(2)}, u32[]{:S(2)}) collective-permute-start(bf16[32,16,128]{2,1,0:T(8,128)(2,1)S(1)} %get-tuple-element.23), channel_id=1, source_target_pairs={{0,2},{1,9},{2,0},{3,11},{4,6},{5,13},{6,4},{7,15},{8,10},{9,1},{1... | collective-permute-start | bytes 393224 | tf_op jit(solution)/shard_map/ppermute | solution.py:249
  3.5 6.7 %collective-permute-start.2 = (bf16[9,16,128]{2,1,0:T(8,128)(2,1)S(1)}, bf16[9,16,128]{2,1,0:T(8,128)(2,1)S(1)}, u32[]{:S(2)}, u32[]{:S(2)}) collective-permute-start(bf16[9,16,128]{2,1,0:T(8,128)(2,1)S(1)} %get-tuple-element.25), channel_id=1, source_target_pairs={{0,2},{2,0},{4,6},{6,4},{8,10},{10,8},{12,14},{14,12},{1,15},{3,5}... | collective-permute-start | bytes 110600 | tf_op jit(solution)/shard_map/ppermute | solution.py:229
  9.5 4.2 %collective-permute-start.1 = (bf16[32,16,128]{2,1,0:T(8,128)(2,1)S(1)}, bf16[32,16,128]{2,1,0:T(8,128)(2,1)S(1)}, u32[]{:S(2)}, u32[]{:S(2)}) collective-permute-start(bf16[32,16,128]{2,1,0:T(8,128)(2,1)S(1)} %fusion), channel_id=1, source_target_pairs={{0,4},{1,3},{2,6},{3,1},{4,0},{5,7},{6,2},{7,5},{8,12},{9,11},{10,... | collective-permute-start | bytes 393224 | tf_op jit(solution)/shard_map/ppermute | solution.py:249
  10.2 7.4 %copy-start.1 = (f32[4096]{0:T(1024)S(1)}, f32[4096]{0:T(1024)}, u32[]{:S(2)}) copy-start(f32[4096]{0:T(1024)} %param.11) | copy-start | bytes 49156
  13.7 3.9 %collective-permute-start.3 = (bf16[32,16,128]{2,1,0:T(8,128)(2,1)S(1)}, bf16[32,16,128]{2,1,0:T(8,128)(2,1)S(1)}, u32[]{:S(2)}, u32[]{:S(2)}) collective-permute-start(bf16[32,16,128]{2,1,0:T(8,128)(2,1)S(1)} %get-tuple-element.34), channel_id=1, source_target_pairs={{0,8},{1,5},{2,10},{3,7},{4,12},{5,1},{6,14},{7,3},{8,0},{9,13},{1... | collective-permute-start | bytes 393224 | tf_op jit(solution)/shard_map/ppermute | solution.py:249
  18.3 4.9 %collective-permute-start.4 = (bf16[16,16,128]{2,1,0:T(8,128)(2,1)S(1)}, bf16[16,16,128]{2,1,0:T(8,128)(2,1)S(1)}, u32[]{:S(2)}, u32[]{:S(2)}) collective-permute-start(bf16[16,16,128]{2,1,0:T(8,128)(2,1)S(1)} %backward.1.refs_2_), channel_id=1, source_target_pairs={{0,1},{1,0},{2,3},{3,2},{4,5},{5,4},{6,7},{7,6},{8,9},{9,8},{10,11... | collective-permute-start | bytes 196616 | tf_op jit(solution)/shard_map/ppermute | solution.py:270
